TPU v7x, 256 devices: a whole 4x4x8 slice. The times are simulated.
256 devices in a mesh: row: 16 (over y_hi, x, core), col: 16 (over z, y_lo).
Axes of the slice: x: 4, y: 4 (y_hi: 2, y_lo: 2; y = y_hi * 2 + y_lo), z: 8, core: 2. Of those that a mesh axis runs over, the one named last changes fastest.
Arguments:
- bottom_in: bfloat16 [256, 256, 256], P('row', 'col'), may hold values from -6 to 6
- skip_feat: bfloat16 [512, 512, 128], P('row', 'col'), may hold values from -6 to 6
- cotangent: bfloat16 [512, 512, 128], P('row', 'col'), may hold values from -6 to 6
- bot_kernel: bfloat16 [3, 3, 256, 256], replicated, may hold values from -0.125 to 0.125
- up_kernel: bfloat16 [4, 4, 256, 128], replicated, may hold values from -0.1875 to 0.1875
- lvl_kernel: bfloat16 [3, 3, 128, 128], replicated, may hold values from -0.1875 to 0.1875
Outputs:
- level_out: bfloat16 [512, 512, 128], P('row', 'col')
- bottom_grad: bfloat16 [256, 256, 256], P('row', 'col')
- lvl_grad: float32 [3, 3, 128, 128], replicated
- up_grad: float32 [4, 4, 256, 128], replicated
- bot_grad: float32 [3, 3, 256, 256], replicated
All inputs are finite; a program needn't handle non-finite values.
Results may differ from a plain program's by a relative error of at most 0.013.
Values may be sent and summed in bfloat16 or wider, within the bound.
No kernel may reach another device: no remote copies, remote signals or barrier semaphores. Data moves between devices by JAX's collectives and lax.ppermute only.
A program may use at most 64 MiB of HBM per device.

v0:
```python
import math

import jax
import jax.numpy as jnp
from jax import lax
from jax.sharding import PartitionSpec as P

up_taps = (((1, 0), (3, -1)), ((0, 1), (2, 0)))


def extended(x, sides, width):
    for axis, dim in sides:
        count, length = (lax.axis_size(axis), x.shape[dim])
        up = [(i, (i + 1) % count) for i in range(count - 1)]
        down = [(j, i) for i, j in up]
        last = lax.slice_in_dim(x, length - width, length, axis=dim)
        initial = lax.slice_in_dim(x, 0, width, axis=dim)
        before = lax.ppermute(last, axis, up)
        after = lax.ppermute(initial, axis, down)
        x = jnp.concatenate([before, x, after], axis=dim)
    return x


def conv_taps(padded, kernel, height, width):
    total = jnp.zeros((height, width, kernel.shape[3]), jnp.float32)
    for row_tap in range(3):
        for col_tap in range(3):
            window = padded[row_tap : row_tap + height, col_tap : col_tap + width]
            total = total + jnp.einsum(
                "hwc,cd->hwd", window, kernel[row_tap, col_tap], preferred_element_type=jnp.float32
            )
    return total


def conv_back(padded_grad, kernel, height, width):
    total = jnp.zeros((height, width, kernel.shape[2]), jnp.float32)
    for row_tap in range(3):
        for col_tap in range(3):
            window = padded_grad[
                2 - row_tap : 2 - row_tap + height, 2 - col_tap : 2 - col_tap + width
            ]
            total = total + jnp.einsum(
                "hwd,cd->hwc", window, kernel[row_tap, col_tap], preferred_element_type=jnp.float32
            )
    return total


def kernel_grad(padded_in, grad, height, width):
    pieces = []
    for row_tap in range(3):
        for col_tap in range(3):
            window = padded_in[row_tap : row_tap + height, col_tap : col_tap + width]
            pieces.append(
                jnp.einsum("hwc,hwd->cd", window, grad, preferred_element_type=jnp.float32)
            )
    stacked = jnp.stack(pieces, axis=0)
    return stacked.reshape(3, 3, stacked.shape[1], stacked.shape[2])


def up_conv(padded, kernel, height, width):
    rows_out = []
    for row_par in range(2):
        cols_out = []
        for col_par in range(2):
            total = jnp.zeros((height, width, kernel.shape[3]), jnp.float32)
            for row_k, row_s in up_taps[row_par]:
                for col_k, col_s in up_taps[col_par]:
                    window = padded[1 + row_s : 1 + row_s + height, 1 + col_s : 1 + col_s + width]
                    total = total + jnp.einsum(
                        "hwc,cd->hwd",
                        window,
                        kernel[row_k, col_k],
                        preferred_element_type=jnp.float32,
                    )
            cols_out.append(total)
        rows_out.append(jnp.stack(cols_out, axis=2))
    joined = jnp.stack(rows_out, axis=1)
    return joined.reshape(2 * height, 2 * width, kernel.shape[3])


def up_back(padded_grad, kernel, height, width):
    total = jnp.zeros((height, width, kernel.shape[2]), jnp.float32)
    for row_k in range(4):
        for col_k in range(4):
            window = padded_grad[row_k : row_k + 2 * height : 2, col_k : col_k + 2 * width : 2]
            total = total + jnp.einsum(
                "hwd,cd->hwc", window, kernel[row_k, col_k], preferred_element_type=jnp.float32
            )
    return total


def up_kernel_grad(coarse, padded_grad, height, width):
    pieces = []
    for row_k in range(4):
        for col_k in range(4):
            window = padded_grad[row_k : row_k + 2 * height : 2, col_k : col_k + 2 * width : 2]
            pieces.append(
                jnp.einsum("hwc,hwd->cd", coarse, window, preferred_element_type=jnp.float32)
            )
    stacked = jnp.stack(pieces, axis=0)
    return stacked.reshape(4, 4, stacked.shape[1], stacked.shape[2])


def tile_sum(grads):
    return lax.psum((grads[0], grads[1], grads[2]), ("row", "col"))


def on_device(bottom_in, skip_feat, cotangent, bot_kernel, up_kernel, lvl_kernel):
    coarse_h = bottom_in.shape[0]
    coarse_w = bottom_in.shape[1]
    fine_h = 2 * coarse_h
    fine_w = 2 * coarse_w
    pixels = fine_h * lax.axis_size("row") * fine_w * lax.axis_size("col")
    scale = 1.0 / math.sqrt(float(pixels))
    bot_pad = extended(bottom_in, (("row", 0), ("col", 1)), 1)
    pre_act = conv_taps(bot_pad, bot_kernel, coarse_h, coarse_w)
    activ = jax.nn.silu(pre_act).astype(jnp.bfloat16)
    act_pad = extended(activ, (("row", 0), ("col", 1)), 1)
    upsampled = up_conv(act_pad, up_kernel, coarse_h, coarse_w)
    mixed = (upsampled + skip_feat.astype(jnp.float32)).astype(jnp.bfloat16)
    mix_pad = extended(mixed, (("row", 0), ("col", 1)), 1)
    level_out = conv_taps(mix_pad, lvl_kernel, fine_h, fine_w).astype(jnp.bfloat16)
    grad_pad = extended(cotangent, (("row", 0), ("col", 1)), 1)
    mixed_grad = conv_back(grad_pad, lvl_kernel, fine_h, fine_w).astype(jnp.bfloat16)
    lvl_local = kernel_grad(mix_pad, cotangent, fine_h, fine_w) * scale
    mgrad_pad = extended(mixed_grad, (("row", 0), ("col", 1)), 1)
    up_local = up_kernel_grad(activ, mgrad_pad, coarse_h, coarse_w) * scale
    activ_grad = up_back(mgrad_pad, up_kernel, coarse_h, coarse_w)
    sigma = jax.nn.sigmoid(pre_act)
    pre_grad = (activ_grad * sigma * (1.0 + pre_act * (1.0 - sigma))).astype(jnp.bfloat16)
    bot_local = kernel_grad(bot_pad, pre_grad, coarse_h, coarse_w) * scale
    pgrad_pad = extended(pre_grad, (("row", 0), ("col", 1)), 1)
    bottom_grad = conv_back(pgrad_pad, bot_kernel, coarse_h, coarse_w).astype(jnp.bfloat16)
    lvl_grad, up_grad, bot_grad = tile_sum((lvl_local, up_local, bot_local))
    return (level_out, bottom_grad, lvl_grad, up_grad, bot_grad)


def solution(mesh):
    return jax.shard_map(
        on_device,
        mesh=mesh,
        in_specs=(
            P("row", "col", None),
            P("row", "col", None),
            P("row", "col", None),
            P(),
            P(),
            P(),
        ),
        out_specs=(P("row", "col", None), P("row", "col", None), P(), P(), P()),
        check_vma=False,
    )
```

profile of v0, /device:TPU:1, one launch (start us, length us, event | category | flops | bytes accessed | tf_op | source)
XLA Modules:
  0.0 505.2 jit_solution(5548048416659073031)
XLA Ops:
  8.1 5.1 %collective-permute-start.13 = (bf16[1,32,128]{2,1,0:T(8,128)(2,1)S(1)}, bf16[1,32,128]{2,1,0:T(8,128)(2,1)S(1)}, u32[]{:S(2)}, u32[]{:S(2)}) collective-permute-start(bf16[1,32,128]{2,1,0:T(8,128)(2,1)S(1)} %get-tuple-element.18), channel_id=1, source_target_pairs={{16,0},{32,16},{48,32},{64,48},{80,64},{96,80},{112,96},{128,112},... | collective-permute-start | bytes 24584 | tf_op jit(solution)/shard_map/ppermute | solution.py:19
  18.3 3.2 collective-permute-start
  26.9 4.0 collective-permute-start.15
  31.0 3.5 collective-permute-start.2
  53.1 3.6 collective-permute-start.4
  59.4 4.8 slice.539
  64.9 4.8 slice.547
  69.7 4.2 collective-permute-start.18
  80.2 4.7 collective-permute-start.6
  88.7 4.9 slice.553
  93.7 4.9 slice.552
  98.6 4.9 slice.550
  103.4 4.8 slice.549
  108.2 4.8 slice.548
  113.0 4.8 slice.546
  119.0 4.9 slice.541
  123.9 4.8 slice.540
  128.7 4.8 slice.538
  143.5 4.4 collective-permute-start.20
  163.6 3.6 collective-permute-start.8
  170.5 5.0 collective-permute-start.23
  177.5 4.5 collective-permute-start.10
  198.2 293.5 %all-reduce.3.cloned.1.call-done = (f32[3,3,128,128]{3,2,1,0:T(8,128)}, f32[4,4,256,128]{3,2,1,0:T(8,128)}, f32[3,3,256,256]{3,2,1,0:T(8,128)}) async-done(((f32[3,3,128,128]{3,2,1,0:T(8,128)}, f32[4,4,256,128]{3,2,1,0:T(8,128)}, f32[3,3,256,256]{3,2,1,0:T(8,128)}), (f32[3,3,128,128]{3,2,1,0:T(8,128)}, f32[4,4,256,128]{3,2,1,0:T(8,128)}, f32[3,3,256,256]{3,2,1,0:T(8,128)})) %all-reduce.3.cloned.1.call-update) | async-done | bytes 5046288 | tf_op jit(solution)/shard_map/psum | solution.py:105
  493.7 3.3 copy.57
  (280 shorter events, 93.5 us)
Async XLA Ops:
  7.2 484.6 %all-reduce.3.cloned.1.call-start = ((), (), s32[]{:S(2)}) async-start(), calls=%async_computation | async-start | bytes 10092544 | tf_op jit(solution)/shard_map/psum | solution.py:105
  8.1 17.4 %collective-permute-start.13 = (bf16[1,32,128]{2,1,0:T(8,128)(2,1)S(1)}, bf16[1,32,128]{2,1,0:T(8,128)(2,1)S(1)}, u32[]{:S(2)}, u32[]{:S(2)}) collective-permute-start(bf16[1,32,128]{2,1,0:T(8,128)(2,1)S(1)} %get-tuple-element.18), channel_id=1, source_target_pairs={{16,0},{32,16},{48,32},{64,48},{80,64},{96,80},{112,96},{128,112},... | collective-permute-start | bytes 24584 | tf_op jit(solution)/shard_map/ppermute | solution.py:19
  13.2 11.3 %collective-permute-start.12 = (bf16[1,32,128]{2,1,0:T(8,128)(2,1)S(1)}, bf16[1,32,128]{2,1,0:T(8,128)(2,1)S(1)}, u32[]{:S(2)}, u32[]{:S(2)}) collective-permute-start(bf16[1,32,128]{2,1,0:T(8,128)(2,1)S(1)} %get-tuple-element.19), channel_id=1, source_target_pairs={{0,16},{16,32},{32,48},{48,64},{64,80},{80,96},{96,112},{112,128},... | collective-permute-start | bytes 24584 | tf_op jit(solution)/shard_map/ppermute | solution.py:18
  15.9 15.0 %collective-permute-start.1 = (bf16[1,16,256]{2,1,0:T(8,128)(2,1)S(1)}, bf16[1,16,256]{2,1,0:T(8,128)(2,1)S(1)}, u32[]{:S(2)}, u32[]{:S(2)}) collective-permute-start(bf16[1,16,256]{2,1,0:T(8,128)(2,1)S(1)} %get-tuple-element.39), channel_id=1, source_target_pairs={{16,0},{32,16},{48,32},{64,48},{80,64},{96,80},{112,96},{128,112},... | collective-permute-start | bytes 24584 | tf_op jit(solution)/shard_map/ppermute | solution.py:19
  18.3 12.6 %collective-permute-start = (bf16[1,16,256]{2,1,0:T(8,128)(2,1)S(1)}, bf16[1,16,256]{2,1,0:T(8,128)(2,1)S(1)}, u32[]{:S(2)}, u32[]{:S(2)}) collective-permute-start(bf16[1,16,256]{2,1,0:T(8,128)(2,1)S(1)} %get-tuple-element.40), channel_id=1, source_target_pairs={{0,16},{16,32},{32,48},{48,64},{64,80},{80,96},{96,112},{112,128},... | collective-permute-start | bytes 24584 | tf_op jit(solution)/shard_map/ppermute | solution.py:18
  25.6 13.0 %collective-permute-start.14 = (bf16[34,1,128]{2,1,0:T(2,128)(2,1)S(1)}, bf16[34,1,128]{2,1,0:T(2,128)(2,1)S(1)}, u32[]{:S(2)}, u32[]{:S(2)}) collective-permute-start(bf16[34,1,128]{2,1,0:T(2,128)(2,1)S(1)} %get-tuple-element.10), channel_id=1, source_target_pairs={{1,0},{2,1},{3,2},{4,3},{5,4},{6,5},{7,6},{8,7},{9,8},{10,9},{11,1... | collective-permute-start | bytes 26120 | tf_op jit(solution)/shard_map/ppermute | solution.py:19
  26.9 11.2 %collective-permute-start.15 = (bf16[34,1,128]{2,1,0:T(2,128)(2,1)S(1)}, bf16[34,1,128]{2,1,0:T(2,128)(2,1)S(1)}, u32[]{:S(2)}, u32[]{:S(2)}) collective-permute-start(bf16[34,1,128]{2,1,0:T(2,128)(2,1)S(1)} %get-tuple-element.11), channel_id=1, source_target_pairs={{0,1},{1,2},{2,3},{3,4},{4,5},{5,6},{6,7},{7,8},{8,9},{9,10},{10,1... | collective-permute-start | bytes 26120 | tf_op jit(solution)/shard_map/ppermute | solution.py:18
  31.0 15.7 %collective-permute-start.2 = (bf16[18,1,256]{2,1,0:T(2,128)(2,1)S(1)}, bf16[18,1,256]{2,1,0:T(2,128)(2,1)S(1)}, u32[]{:S(2)}, u32[]{:S(2)}) collective-permute-start(bf16[18,1,256]{2,1,0:T(2,128)(2,1)S(1)} %get-tuple-element.30), channel_id=1, source_target_pairs={{0,1},{1,2},{2,3},{3,4},{4,5},{5,6},{6,7},{7,8},{8,9},{9,10},{10,1... | collective-permute-start | bytes 27656 | tf_op jit(solution)/shard_map/ppermute | solution.py:18
  34.5 11.8 %collective-permute-start.3 = (bf16[18,1,256]{2,1,0:T(2,128)(2,1)S(1)}, bf16[18,1,256]{2,1,0:T(2,128)(2,1)S(1)}, u32[]{:S(2)}, u32[]{:S(2)}) collective-permute-start(bf16[18,1,256]{2,1,0:T(2,128)(2,1)S(1)} %get-tuple-element.31), channel_id=1, source_target_pairs={{1,0},{2,1},{3,2},{4,3},{5,4},{6,5},{7,6},{8,7},{9,8},{10,9},{11,1... | collective-permute-start | bytes 27656 | tf_op jit(solution)/shard_map/ppermute | solution.py:19
  40.5 18.1 %collective-permute-start.16 = (bf16[1,32,128]{2,1,0:T(8,128)(2,1)}, bf16[1,32,128]{2,1,0:T(8,128)(2,1)S(1)}, u32[]{:S(2)}, u32[]{:S(2)}) collective-permute-start(bf16[1,32,128]{2,1,0:T(8,128)(2,1)} %get-tuple-element.16), channel_id=1, source_target_pairs={{0,16},{16,32},{32,48},{48,64},{64,80},{80,96},{96,112},{112,128},... | collective-permute-start | bytes 24584 | tf_op jit(solution)/shard_map/ppermute | solution.py:18
  43.3 15.4 %collective-permute-start.17 = (bf16[1,32,128]{2,1,0:T(8,128)(2,1)}, bf16[1,32,128]{2,1,0:T(8,128)(2,1)S(1)}, u32[]{:S(2)}, u32[]{:S(2)}) collective-permute-start(bf16[1,32,128]{2,1,0:T(8,128)(2,1)} %get-tuple-element.17), channel_id=1, source_target_pairs={{16,0},{32,16},{48,32},{64,48},{80,64},{96,80},{112,96},{128,112},... | collective-permute-start | bytes 24584 | tf_op jit(solution)/shard_map/ppermute | solution.py:19
  53.1 26.5 %collective-permute-start.4 = (bf16[1,16,256]{2,1,0:T(8,128)(2,1)}, bf16[1,16,256]{2,1,0:T(8,128)(2,1)S(1)}, u32[]{:S(2)}, u32[]{:S(2)}) collective-permute-start(bf16[1,16,256]{2,1,0:T(8,128)(2,1)} %get-tuple-element.34), channel_id=1, source_target_pairs={{0,16},{16,32},{32,48},{48,64},{64,80},{80,96},{96,112},{112,128},... | collective-permute-start | bytes 24584 | tf_op jit(solution)/shard_map/ppermute | solution.py:18
  56.7 22.9 %collective-permute-start.5 = (bf16[1,16,256]{2,1,0:T(8,128)(2,1)}, bf16[1,16,256]{2,1,0:T(8,128)(2,1)S(1)}, u32[]{:S(2)}, u32[]{:S(2)}) collective-permute-start(bf16[1,16,256]{2,1,0:T(8,128)(2,1)} %get-tuple-element.35), channel_id=1, source_target_pairs={{16,0},{32,16},{48,32},{64,48},{80,64},{96,80},{112,96},{128,112},... | collective-permute-start | bytes 24584 | tf_op jit(solution)/shard_map/ppermute | solution.py:19
  69.7 18.1 %collective-permute-start.18 = (bf16[34,1,128]{2,1,0:T(2,128)(2,1)}, bf16[34,1,128]{2,1,0:T(2,128)(2,1)S(1)}, u32[]{:S(2)}, u32[]{:S(2)}) collective-permute-start(bf16[34,1,128]{2,1,0:T(2,128)(2,1)} %get-tuple-element.8), channel_id=1, source_target_pairs={{0,1},{1,2},{2,3},{3,4},{4,5},{5,6},{6,7},{7,8},{8,9},{9,10},{10,1... | collective-permute-start | bytes 26120 | tf_op jit(solution)/shard_map/ppermute | solution.py:18
  74.0 13.9 %collective-permute-start.19 = (bf16[34,1,128]{2,1,0:T(2,128)(2,1)}, bf16[34,1,128]{2,1,0:T(2,128)(2,1)S(1)}, u32[]{:S(2)}, u32[]{:S(2)}) collective-permute-start(bf16[34,1,128]{2,1,0:T(2,128)(2,1)} %get-tuple-element.9), channel_id=1, source_target_pairs={{1,0},{2,1},{3,2},{4,3},{5,4},{6,5},{7,6},{8,7},{9,8},{10,9},{11,1... | collective-permute-start | bytes 26120 | tf_op jit(solution)/shard_map/ppermute | solution.py:19
  80.2 78.9 %collective-permute-start.6 = (bf16[18,1,256]{2,1,0:T(2,128)(2,1)}, bf16[18,1,256]{2,1,0:T(2,128)(2,1)}, u32[]{:S(2)}, u32[]{:S(2)}) collective-permute-start(bf16[18,1,256]{2,1,0:T(2,128)(2,1)} %get-tuple-element.28), channel_id=1, source_target_pairs={{0,1},{1,2},{2,3},{3,4},{4,5},{5,6},{6,7},{7,8},{8,9},{9,10},{10,1... | collective-permute-start | bytes 27656 | tf_op jit(solution)/shard_map/ppermute | solution.py:18
  84.9 74.3 %collective-permute-start.7 = (bf16[18,1,256]{2,1,0:T(2,128)(2,1)}, bf16[18,1,256]{2,1,0:T(2,128)(2,1)}, u32[]{:S(2)}, u32[]{:S(2)}) collective-permute-start(bf16[18,1,256]{2,1,0:T(2,128)(2,1)} %get-tuple-element.29), channel_id=1, source_target_pairs={{1,0},{2,1},{3,2},{4,3},{5,4},{6,5},{7,6},{8,7},{9,8},{10,9},{11,1... | collective-permute-start | bytes 27656 | tf_op jit(solution)/shard_map/ppermute | solution.py:19
  143.5 25.7 %collective-permute-start.20 = (bf16[1,16,256]{2,1,0:T(8,128)(2,1)S(1)}, bf16[1,16,256]{2,1,0:T(8,128)(2,1)S(1)}, u32[]{:S(2)}, u32[]{:S(2)}) collective-permute-start(bf16[1,16,256]{2,1,0:T(8,128)(2,1)S(1)} %get-tuple-element.32), channel_id=1, source_target_pairs={{0,16},{16,32},{32,48},{48,64},{64,80},{80,96},{96,112},{112,128},... | collective-permute-start | bytes 24584 | tf_op jit(solution)/shard_map/ppermute | solution.py:18
  147.9 21.3 %collective-permute-start.21 = (bf16[1,16,256]{2,1,0:T(8,128)(2,1)S(1)}, bf16[1,16,256]{2,1,0:T(8,128)(2,1)S(1)}, u32[]{:S(2)}, u32[]{:S(2)}) collective-permute-start(bf16[1,16,256]{2,1,0:T(8,128)(2,1)S(1)} %get-tuple-element.33), channel_id=1, source_target_pairs={{16,0},{32,16},{48,32},{64,48},{80,64},{96,80},{112,96},{128,112},... | collective-permute-start | bytes 24584 | tf_op jit(solution)/shard_map/ppermute | solution.py:19
  163.6 13.8 %collective-permute-start.8 = (bf16[1,32,128]{2,1,0:T(8,128)(2,1)S(1)}, bf16[1,32,128]{2,1,0:T(8,128)(2,1)S(1)}, u32[]{:S(2)}, u32[]{:S(2)}) collective-permute-start(bf16[1,32,128]{2,1,0:T(8,128)(2,1)S(1)} %get-tuple-element.20), channel_id=1, source_target_pairs={{0,16},{16,32},{32,48},{48,64},{64,80},{80,96},{96,112},{112,128},... | collective-permute-start | bytes 24584 | tf_op jit(solution)/shard_map/ppermute | solution.py:18
  167.3 10.2 %collective-permute-start.9 = (bf16[1,32,128]{2,1,0:T(8,128)(2,1)S(1)}, bf16[1,32,128]{2,1,0:T(8,128)(2,1)S(1)}, u32[]{:S(2)}, u32[]{:S(2)}) collective-permute-start(bf16[1,32,128]{2,1,0:T(8,128)(2,1)S(1)} %get-tuple-element.21), channel_id=1, source_target_pairs={{16,0},{32,16},{48,32},{64,48},{80,64},{96,80},{112,96},{128,112},... | collective-permute-start | bytes 24584 | tf_op jit(solution)/shard_map/ppermute | solution.py:19
  169.2 17.0 %collective-permute-start.22 = (bf16[18,1,256]{2,1,0:T(2,128)(2,1)S(1)}, bf16[18,1,256]{2,1,0:T(2,128)(2,1)S(1)}, u32[]{:S(2)}, u32[]{:S(2)}) collective-permute-start(bf16[18,1,256]{2,1,0:T(2,128)(2,1)S(1)} %get-tuple-element.24), channel_id=1, source_target_pairs={{1,0},{2,1},{3,2},{4,3},{5,4},{6,5},{7,6},{8,7},{9,8},{10,9},{11,1... | collective-permute-start | bytes 27656 | tf_op jit(solution)/shard_map/ppermute | solution.py:19
  170.5 15.7 %collective-permute-start.23 = (bf16[18,1,256]{2,1,0:T(2,128)(2,1)S(1)}, bf16[18,1,256]{2,1,0:T(2,128)(2,1)S(1)}, u32[]{:S(2)}, u32[]{:S(2)}) collective-permute-start(bf16[18,1,256]{2,1,0:T(2,128)(2,1)S(1)} %get-tuple-element.25), channel_id=1, source_target_pairs={{0,1},{1,2},{2,3},{3,4},{4,5},{5,6},{6,7},{7,8},{8,9},{9,10},{10,1... | collective-permute-start | bytes 27656 | tf_op jit(solution)/shard_map/ppermute | solution.py:18
  177.5 11.4 %collective-permute-start.10 = (bf16[34,1,128]{2,1,0:T(2,128)(2,1)S(1)}, bf16[34,1,128]{2,1,0:T(2,128)(2,1)S(1)}, u32[]{:S(2)}, u32[]{:S(2)}) collective-permute-start(bf16[34,1,128]{2,1,0:T(2,128)(2,1)S(1)} %get-tuple-element.14), channel_id=1, source_target_pairs={{0,1},{1,2},{2,3},{3,4},{4,5},{5,6},{6,7},{7,8},{8,9},{9,10},{10,1... | collective-permute-start | bytes 26120 | tf_op jit(solution)/shard_map/ppermute | solution.py:18
  (52 other events, 359.0 us)
Sparse Core Ops, SparseCore 0:
  192.6 299.1 all-reduce.2
where the time goes:
time: 508 us; the launch traced here: 505 us
  waiting for transfers between devices  294 us (58%)
  starting transfers between devices  68.8 us (14%)
  local copies, waits for them, and re-layouts  68.4 us (13%)
  matrix products  51.1 us (10%)
  between operations  15.7 us (3%)
  other arithmetic  7.62 us (2%)
    psum x1, waiting for transfers between devices, tile_sum(): return lax.psum((grads[0], grads[1], grads[2]), ('row', 'col'))  294 us
    slice x16, local copies, waits for them, and re-layouts, up_back(): window = padded_grad[row_k:row_k + 2 * height:2, col_k:col_k + 2 * width:2]  55.4 us
    ppermute x12, starting transfers between devices, extended(): before = lax.ppermute(last, axis, up)  45.5 us
    ppermute x12, starting transfers between devices, extended(): after = lax.ppermute(initial, axis, down)  23.3 us
    dot_general x16, matrix products, up_back(): jnp.einsum('hwd,cd->hwc', window, kernel[row_k, col_k], preferred_element...  13.8 us
    dot_general x18, matrix products, conv_taps(): jnp.einsum('hwc,cd->hwd', window, kernel[row_tap, col_tap], preferred_ele...  12.3 us
    dot_general x18, matrix products, conv_back(): jnp.einsum('hwd,cd->hwc', window, kernel[row_tap, col_tap], preferred_ele...  10.3 us
  transfers between devices with their start and end apart: 25, of which 1 were waited for; matrix products, arithmetic and copies ran while one was open for 23% of the time, Pallas kernels for 0%

commit v1 on v0

v1 whole, which is shorter than its diff:
```python
import functools

import jax
import jax.numpy as jnp
from jax import lax
from jax.experimental import pallas as pl
from jax.experimental.pallas import tpu as pltpu
from jax.sharding import PartitionSpec as P

AXES = ("row", "col")
F32 = jnp.float32
BF16 = jnp.bfloat16
TILE = 16
EXT = TILE + 4
PITCH = 32
CORE = 8
HALF = 5120


def place(x, y, z, core):
    row = (((y >> 1) & 1) * 4 + x % 4) * 2 + core
    col = (z % 8) * 2 + (y & 1)
    return row * 16 + col


PLANE_GROUPS = [
    [place(x, y, z, core) for x in range(4) for y in range(4)]
    for z in range(8)
    for core in range(2)
]
DEPTH_GROUPS = [
    [place(x, y, z, core) for z in range(8)]
    for x in range(4)
    for y in range(4)
    for core in range(2)
]
CORE_SWAP = [(i, i ^ 1) for i in range(16)]


def split_kernel(bot_ref, skip_ref, cot_ref, out_ref, wide):
    out_ref[0] = bot_ref[...]
    for plane, ref in ((1, cot_ref), (3, skip_ref)):
        wide[...] = ref[...].astype(F32)
        for col_par in range(2):
            part = wide[:, pl.ds(col_par, TILE, stride=2), :].astype(BF16)
            part = part.reshape(TILE, 2, TILE, 128)
            lanes = slice(col_par * 128, col_par * 128 + 128)
            out_ref[plane, :, :, lanes] = part[:, 0]
            out_ref[plane + 1, :, :, lanes] = part[:, 1]


def split(bottom_in, skip_feat, cotangent):
    return pl.pallas_call(
        split_kernel,
        out_shape=jax.ShapeDtypeStruct((5, TILE, TILE, 256), BF16),
        scratch_shapes=[pltpu.VMEM((2 * TILE, 2 * TILE, 128), F32)],
        compiler_params=pltpu.CompilerParams(vmem_limit_bytes=16 << 20),
    )(bottom_in, skip_feat, cotangent)


def nn(a, b):
    return lax.dot_general(a, b, (((1,), (0,)), ((), ())), preferred_element_type=F32)


def nt(a, b):
    return lax.dot_general(a, b, (((1,), (1,)), ((), ())), preferred_element_type=F32)


def tn(a, b):
    return lax.dot_general(a, b, (((0,), (0,)), ((), ())), preferred_element_type=F32)


def flat(x):
    return x.reshape(-1, x.shape[-1])


def left(x):
    return pltpu.roll(x, 1, 0)


def right(x):
    return pltpu.roll(x, x.shape[0] - 1, 0)


def core_of(x):
    rows = x.shape[0] // PITCH
    return x.reshape(rows, PITCH, x.shape[1])[:, CORE : CORE + TILE]


def three(x):
    return (left(x), x, right(x))


def four(x):
    return (left(x[:, 128:]), x, right(x[:, :128]))


def fine_row(offset):
    return offset % 2, offset // 2


def pair_weight(taps, zero):
    first = jnp.concatenate([taps[0], taps[1], taps[2], zero], axis=0)
    second = jnp.concatenate([zero, taps[0], taps[1], taps[2]], axis=0)
    return jnp.concatenate([first, second], axis=1)


def pair_weight_back(taps, zero):
    first = jnp.concatenate([taps[0], taps[1], taps[2], zero], axis=1)
    second = jnp.concatenate([zero, taps[0], taps[1], taps[2]], axis=1)
    return jnp.concatenate([first, second], axis=0)


def main_kernel(
    scale, pos_ref, z_ref, up_ref, down_ref, lo_ref, hi_ref, bk_ref, uk_ref, lk_ref,
    level_ref, bgrad_ref, grad_ref,
    ext, bot3, botc, act3, actc, dsilu, cot4, mg4, mg4c, mix4c, pg3c, pgc, inter,
):
    row0 = pos_ref[0] * TILE
    col0 = pos_ref[1] * TILE
    image_h = pos_ref[2]
    image_w = pos_ref[3]
    mine = pos_ref[4]

    ext[...] = jnp.zeros_like(ext)
    ext[:, 0:2, CORE : CORE + TILE, :] = up_ref[...].astype(F32)
    ext[:, 2 : 2 + TILE, CORE : CORE + TILE, :] = z_ref[...].astype(F32)
    ext[:, 2 + TILE : EXT, CORE : CORE + TILE, :] = down_ref[...].astype(F32)
    ext[:, :, CORE - 2 : CORE, :] = lo_ref[...].astype(F32)
    ext[:, :, CORE + TILE : CORE + TILE + 2, :] = hi_ref[...].astype(F32)

    def masked(x, first):
        rows = x.shape[0] // PITCH
        x = x.reshape(rows, PITCH, x.shape[1])
        i = lax.broadcasted_iota(jnp.int32, x.shape, 0) + (row0 + first - 2)
        w = lax.broadcasted_iota(jnp.int32, x.shape, 1)
        j = w + (col0 - CORE)
        keep = (i >= 0) & (i < image_h) & (j >= 0) & (j < image_w)
        keep = keep & (w >= CORE - 2) & (w < CORE + TILE + 2)
        return flat(jnp.where(keep, x, 0.0))

    zero = jnp.zeros((128, 128), BF16)

    for b, part in enumerate(three(flat(ext[0]))):
        lanes = slice(256 * b, 256 * b + 256)
        bot3[:, :, lanes] = part.reshape(EXT, PITCH, 256).astype(BF16)
        botc[:, :, lanes] = core_of(part)[1 : 19].astype(BF16)
    pre = jnp.zeros((18 * PITCH, 256), F32)
    for a in range(3):
        pre = pre + nn(flat(bot3[a : a + 18]), bk_ref[a].reshape(768, 256))
    sigma = jax.nn.sigmoid(pre)
    dsilu[...] = sigma * (1.0 + pre * (1.0 - sigma))
    activ = masked((pre * sigma).astype(BF16).astype(F32), 1)
    act3[0] = jnp.zeros((PITCH, 768), BF16)
    act3[EXT - 1] = jnp.zeros((PITCH, 768), BF16)
    for b, part in enumerate(three(activ)):
        act3[1:19, :, 256 * b : 256 * b + 256] = part.reshape(18, PITCH, 256).astype(BF16)
    actc[...] = flat(core_of(activ)[1:17]).astype(BF16)

    for par in range(2):
        a, b, c = four(flat(ext[1 + par]))
        cot4[par, :, :, 0:128] = a.reshape(EXT, PITCH, 128).astype(BF16)
        cot4[par, :, :, 128:384] = b.reshape(EXT, PITCH, 256).astype(BF16)
        cot4[par, :, :, 384:512] = c.reshape(EXT, PITCH, 128).astype(BF16)
    for par in range(2):
        first = 1 - par
        total = jnp.zeros((19 * PITCH, 256), F32)
        for a in range(3):
            src, shift = fine_row(par + a - 1)
            weight = pair_weight_back([lk_ref[2 - a, 2 - b] for b in range(3)], zero)
            total = total + nt(flat(cot4[src, first + shift : first + shift + 19]), weight)
        grad = masked(total.astype(BF16).astype(F32), first)
        a, b, c = four(grad)
        mg4[par, first : first + 19, :, 0:128] = a.reshape(19, PITCH, 128).astype(BF16)
        mg4[par, first : first + 19, :, 128:384] = b.reshape(19, PITCH, 256).astype(BF16)
        mg4[par, first : first + 19, :, 384:512] = c.reshape(19, PITCH, 128).astype(BF16)
        mg4c[par, first : first + 19, :, 0:128] = core_of(a).astype(BF16)
        mg4c[par, first : first + 19, :, 128:384] = core_of(b).astype(BF16)
        mg4c[par, first : first + 19, :, 384:512] = core_of(c).astype(BF16)

    def put(half, row, value):
        slot = lax.rem(half + mine, 2)
        grad_ref[slot, pl.ds(row, value.shape[0]), :] = (value * scale).astype(BF16)

    act_t = actc[...].T
    for a in range(4):
        src, shift = fine_row(a - 1)
        prod = nn(act_t, flat(mg4c[src, 2 + shift : 18 + shift]))
        for b in range(4):
            put(0, (4 * a + b) * 256, prod[:, 128 * b : 128 * b + 128])

    agrad = jnp.zeros((18 * PITCH, 256), F32)
    for a in range(4):
        src, shift = fine_row(a - 1)
        weight = jnp.concatenate([uk_ref[a, b] for b in range(4)], axis=1)
        agrad = agrad + nt(flat(mg4[src, 1 + shift : 19 + shift]), weight)
    pgrad = masked((agrad * dsilu[...]).astype(BF16).astype(F32), 1)
    for b, part in enumerate(three(pgrad)):
        pg3c[:, :, 256 * b : 256 * b + 256] = core_of(part).astype(BF16)
    pgc[...] = flat(core_of(pgrad)[1:17]).astype(BF16)

    for a in range(3):
        prod = tn(flat(botc[a : a + 16]), pgc[...])
        put(1, 768 * a, prod[:, :128])
        put(1, 2304 + 768 * a, prod[:, 128:])

    for par in range(2):
        total = flat(ext[3 + par, 1:19])
        for row_k, shift in (((1, 0), (3, -1)), ((0, 1), (2, 0)))[par]:
            k = [uk_ref[row_k, b] for b in range(4)]
            none = jnp.zeros((256, 128), BF16)
            weight = jnp.concatenate(
                [
                    jnp.concatenate([k[3], k[1], none], axis=0),
                    jnp.concatenate([none, k[2], k[0]], axis=0),
                ],
                axis=1,
            )
            total = total + nn(flat(act3[1 + shift : 19 + shift]), weight)
        mixed = masked(total.astype(BF16).astype(F32), 1)
        a, b, c = four(mixed)
        mix4c[par, :, :, 0:128] = core_of(a).astype(BF16)
        mix4c[par, :, :, 128:384] = core_of(b).astype(BF16)
        mix4c[par, :, :, 384:512] = core_of(c).astype(BF16)

    for a in range(3):
        prod = jnp.zeros((512, 256), F32)
        for par in range(2):
            src, shift = fine_row(par + a - 1)
            prod = prod + tn(
                flat(mix4c[src, 1 + shift : 17 + shift]), flat(z_ref[1 + par])
            )
        for b in range(3):
            tap = prod[128 * b : 128 * b + 128, :128] + prod[128 * b + 128 : 128 * b + 256, 128:]
            if a < 2:
                put(0, 4096 + (3 * a + b) * 128, tap)
            else:
                put(1, 4608 + b * 128, tap)
    put(0, 4864, jnp.zeros((HALF - 4864, 128), F32))
    put(1, 4992, jnp.zeros((HALF - 4992, 128), F32))

    for par in range(2):
        total = jnp.zeros((TILE * TILE, 256), F32)
        for a in range(3):
            src, shift = fine_row(par + a - 1)
            weight = pair_weight([lk_ref[a, b] for b in range(3)], zero)
            total = total + nn(flat(mix4c[src, 1 + shift : 17 + shift]), weight)
        total = total.reshape(TILE, TILE, 256)
        for col_par in range(2):
            inter[:, par, pl.ds(col_par, TILE, stride=2), :] = total[
                :, :, 128 * col_par : 128 * col_par + 128
            ]
    level_ref[...] = inter[...].reshape(2 * TILE, 2 * TILE, 128).astype(BF16)

    total = jnp.zeros((TILE * TILE, 256), F32)
    for a in range(3):
        weight = jnp.concatenate([bk_ref[2 - a, 2 - b] for b in range(3)], axis=1)
        total = total + nt(flat(pg3c[a : a + 16]), weight)
    bgrad_ref[...] = total.reshape(TILE, TILE, 256).astype(BF16)


def local_work(scale, pos, z, up, down, lo, hi, bot_kernel, up_kernel, lvl_kernel):
    vmem = pl.BlockSpec(memory_space=pltpu.VMEM)
    return pl.pallas_call(
        functools.partial(main_kernel, scale),
        out_shape=(
            jax.ShapeDtypeStruct((2 * TILE, 2 * TILE, 128), BF16),
            jax.ShapeDtypeStruct((TILE, TILE, 256), BF16),
            jax.ShapeDtypeStruct((2, HALF, 128), BF16),
        ),
        in_specs=[pl.BlockSpec(memory_space=pltpu.SMEM)] + [vmem] * 8,
        out_specs=(vmem, vmem, vmem),
        scratch_shapes=[
            pltpu.VMEM((5, EXT, PITCH, 256), F32),
            pltpu.VMEM((EXT, PITCH, 768), BF16),
            pltpu.VMEM((18, TILE, 768), BF16),
            pltpu.VMEM((EXT, PITCH, 768), BF16),
            pltpu.VMEM((TILE * TILE, 256), BF16),
            pltpu.VMEM((18 * PITCH, 256), F32),
            pltpu.VMEM((2, EXT, PITCH, 512), BF16),
            pltpu.VMEM((2, EXT, PITCH, 512), BF16),
            pltpu.VMEM((2, EXT, TILE, 512), BF16),
            pltpu.VMEM((2, 18, TILE, 512), BF16),
            pltpu.VMEM((18, TILE, 768), BF16),
            pltpu.VMEM((TILE * TILE, 256), BF16),
            pltpu.VMEM((TILE, 2, 2 * TILE, 128), F32),
        ],
        compiler_params=pltpu.CompilerParams(vmem_limit_bytes=56 << 20),
    )(pos, z, up, down, lo, hi, bot_kernel, up_kernel, lvl_kernel)


def shifted(last, first, axis):
    count = lax.axis_size(axis)
    up = [(i, i + 1) for i in range(count - 1)]
    down = [(i + 1, i) for i in range(count - 1)]
    return lax.ppermute(last, axis, up), lax.ppermute(first, axis, down)


def spread(x, count, groups):
    return lax.all_to_all(
        jnp.broadcast_to(x[None], (count,) + x.shape), AXES, 0, 0, axis_index_groups=groups
    )


def sum_parts(x):
    return jnp.sum(x.astype(F32), axis=0).astype(BF16)


def total_over_devices(grads):
    got = lax.ppermute(grads[1], "row", CORE_SWAP)
    half = (grads[0].astype(F32) + got.astype(F32)).astype(BF16).reshape(16, HALF // 16, 128)
    part = sum_parts(lax.all_to_all(half, AXES, 0, 0, axis_index_groups=PLANE_GROUPS))
    part = jnp.pad(part.reshape(8, HALF // 128, 128), ((0, 0), (0, 8), (0, 0)))
    piece = sum_parts(lax.all_to_all(part, AXES, 0, 0, axis_index_groups=DEPTH_GROUPS))
    part = spread(piece, 8, DEPTH_GROUPS)[:, : HALF // 128].reshape(HALF // 16, 128)
    half = spread(part, 16, PLANE_GROUPS).reshape(HALF, 128)
    other = lax.ppermute(half, "row", CORE_SWAP)
    core = lax.rem(lax.axis_index("row"), 2)
    return jnp.where(core == 0, half, other), jnp.where(core == 0, other, half)


def on_device(bottom_in, skip_feat, cotangent, bot_kernel, up_kernel, lvl_kernel):
    rows, cols = lax.axis_size("row"), lax.axis_size("col")
    scale = 1.0 / float(2 * TILE * rows * 2 * TILE * cols) ** 0.5
    z = split(bottom_in, skip_feat, cotangent)
    up, down = shifted(z[:, TILE - 2 :], z[:, :2], "row")
    last = jnp.concatenate([up[:, :, -2:], z[:, :, -2:], down[:, :, -2:]], axis=1)
    first = jnp.concatenate([up[:, :, :2], z[:, :, :2], down[:, :, :2]], axis=1)
    lo, hi = shifted(last, first, "col")
    row = lax.axis_index("row")
    pos = jnp.stack(
        [row, lax.axis_index("col"), jnp.int32(TILE * rows), jnp.int32(TILE * cols), row % 2]
    ).astype(jnp.int32)
    level_out, bottom_grad, grads = local_work(
        scale, pos, z, up, down, lo, hi, bot_kernel, up_kernel, lvl_kernel
    )
    even, odd = total_over_devices(grads)
    up_grad = even[:4096].astype(F32).reshape(4, 4, 256, 128)
    lvl_grad = jnp.concatenate([even[4096:4864], odd[4608:4992]], axis=0).astype(F32)
    bot_grad = jnp.concatenate([odd[:2304], odd[2304:4608]], axis=1).astype(F32)
    return (
        level_out,
        bottom_grad,
        lvl_grad.reshape(3, 3, 128, 128),
        up_grad,
        bot_grad.reshape(3, 3, 256, 256),
    )


def solution(mesh):
    return jax.shard_map(
        on_device,
        mesh=mesh,
        in_specs=(
            P("row", "col", None),
            P("row", "col", None),
            P("row", "col", None),
            P(),
            P(),
            P(),
        ),
        out_specs=(P("row", "col", None), P("row", "col", None), P(), P(), P()),
        check_vma=False,
    )
```

time: 508 us -> 127 us (0.25)
  waiting for transfers between devices: 294 us -> 10.8 us
  blocking collectives: 0 us -> 75.9 us
  local copies, waits for them, and re-layouts: 68.4 us -> 5.65 us
  starting transfers between devices: 68.8 us -> 16.9 us
  matrix products: 51.1 us -> 0 us
  between operations: 15.7 us -> 0.88 us
  Pallas kernels: 0 us -> 10.9 us
    psum x1 -> x0, waiting for transfers between devices: 294 us -> none  [tile_sum(): return lax.psum((grads[0], grads[1], grads[2]), ('row', 'col'))]
    all_to_all x0 -> x4, blocking collectives: none -> 75.9 us  [the longest x1 31.6 us: total_over_devices(): lax.all_to_all(half, AXES, 0, 0, axis_index_groups=PLANE_GROUPS)]
    slice x25 -> x9, local copies, waits for them, and re-layouts: 58.9 us -> 0.36 us  [the longest x3 0.17 us: on_device(): first = jnp.concatenate([up[:, :, :2], z[:, :, :2], down[:, :, :2]], axis=1)]
    ppermute x24 -> x6, starting transfers between devices: 68.7 us -> 16.9 us  [the longest x4 10.9 us: shifted(): return (lax.ppermute(last, axis, up), lax.ppermute(first, axis, down))]
    dot_general x102 -> x0, matrix products: 51.1 us -> none  [the longest x16 13.8 us: up_back(): jnp.einsum('hwd,cd->hwc', window, kernel[row_k, col_k], preferred_element...]
    pallas_call x0 -> x2, Pallas kernels: none -> 10.9 us  [the longest x1 10.8 us: local_work(): pl.pallas_call(functools.partial(main_kernel, scale), out_shape=(jax.Shap...]
    ppermute x24 -> x6, waiting for transfers between devices: 0.06 us -> 10.8 us  [the longest x4 5.36 us: shifted(): return (lax.ppermute(last, axis, up), lax.ppermute(first, axis, down))]
    unnamed x108 -> x18, local copies, waits for them, and re-layouts: 9.13 us -> 3.45 us
  transfers between devices with their start and end apart: 25 -> 6, of which waited for: 1 -> 5; matrix products, arithmetic and copies ran while one was open for 23% -> 1% of each run, Pallas kernels for 0% -> 0%
where the time goes in v1:
time: 127 us
  blocking collectives  75.9 us (60%)
  starting transfers between devices  16.9 us (13%)
  Pallas kernels  10.9 us (9%)
  waiting for transfers between devices  10.8 us (9%)
  other arithmetic  5.75 us (5%)
  local copies, waits for them, and re-layouts  5.65 us (4%)
    all_to_all x1, blocking collectives, total_over_devices(): lax.all_to_all(half, AXES, 0, 0, axis_index_groups=PLANE_GROUPS)  31.6 us
    all_to_all x2, blocking collectives, spread(): lax.all_to_all(jnp.broadcast_to(x[None], (count,) + x.shape), AXES, 0, 0,...  28.5 us
    all_to_all x1, blocking collectives, total_over_devices(): lax.all_to_all(part, AXES, 0, 0, axis_index_groups=DEPTH_GROUPS)  15.9 us
    ppermute x4, starting transfers between devices, shifted(): return (lax.ppermute(last, axis, up), lax.ppermute(first, axis, down))  10.9 us
    pallas_call x1, Pallas kernels, local_work(): pl.pallas_call(functools.partial(main_kernel, scale), out_shape=(jax.Shap...  10.8 us
    ppermute x1, starting transfers between devices, total_over_devices(): other = lax.ppermute(half, 'row', CORE_SWAP)  5.66 us
    ppermute x4, waiting for transfers between devices, shifted(): return (lax.ppermute(last, axis, up), lax.ppermute(first, axis, down))  5.36 us
    unnamed x18, local copies, waits for them, and re-layouts  3.45 us
  transfers between devices with their start and end apart: 6, of which 5 were waited for; matrix products, arithmetic and copies ran while one was open for 1% of the time, Pallas kernels for 0%

profile of v1, /device:TPU:1, one launch (start us, length us, event | category | flops | bytes accessed | tf_op | source)
XLA Modules:
  0.0 126.9 jit_solution(7475447139595949752)
XLA Ops:
  0.6 0.9 copy-done.1
  1.6 0.9 copy-done.2
  2.5 0.9 copy-done.3
  3.6 5.1 %collective-permute-start.1 = (bf16[5,2,16,256]{3,2,1,0:T(8,128)(2,1)S(1)}, bf16[5,2,16,256]{3,2,1,0:T(8,128)(2,1)S(1)}, u32[]{:S(2)}, u32[]{:S(2)}) collective-permute-start(bf16[5,2,16,256]{3,2,1,0:T(8,128)(2,1)S(1)} %get-tuple-element.17), channel_id=1, source_target_pairs={{16,0},{32,16},{48,32},{64,48},{80,64},{96,80},{112,96},{128,112},... | collective-permute-start | bytes 245768 | tf_op jit(solution)/shard_map/ppermute | solution.py:296
  8.8 1.9 %collective-permute-start = (bf16[5,2,16,256]{3,2,1,0:T(8,128)(2,1)S(1)}, bf16[5,2,16,256]{3,2,1,0:T(8,128)(2,1)S(1)}, u32[]{:S(2)}, u32[]{:S(2)}) collective-permute-start(bf16[5,2,16,256]{3,2,1,0:T(8,128)(2,1)S(1)} %get-tuple-element.18), channel_id=1, source_target_pairs={{0,16},{16,32},{32,48},{48,64},{64,80},{80,96},{96,112},{112,128},... | collective-permute-start | bytes 245768 | tf_op jit(solution)/shard_map/ppermute | solution.py:296
  10.9 1.3 collective-permute-done.up_ref
  12.4 2.6 %collective-permute-start.2 = (bf16[5,20,2,256]{3,2,1,0:T(2,128)(2,1)S(1)}, bf16[5,20,2,256]{3,2,1,0:T(2,128)(2,1)S(1)}, u32[]{:S(2)}, u32[]{:S(2)}) collective-permute-start(bf16[5,20,2,256]{3,2,1,0:T(2,128)(2,1)S(1)} %pad_maximum_fusion.1), channel_id=1, source_target_pairs={{0,1},{1,2},{2,3},{3,4},{4,5},{5,6},{6,7},{7,8},{8,9},{9,10},{10,1... | collective-permute-start | bytes 307208 | tf_op jit(solution)/shard_map/ppermute | solution.py:296
  15.1 1.3 %collective-permute-start.3 = (bf16[5,20,2,256]{3,2,1,0:T(2,128)(2,1)S(1)}, bf16[5,20,2,256]{3,2,1,0:T(2,128)(2,1)S(1)}, u32[]{:S(2)}, u32[]{:S(2)}) collective-permute-start(bf16[5,20,2,256]{3,2,1,0:T(2,128)(2,1)S(1)} %pad_maximum_fusion.2), channel_id=1, source_target_pairs={{1,0},{2,1},{3,2},{4,3},{5,4},{6,5},{7,6},{8,7},{9,8},{10,9},{11,1... | collective-permute-start | bytes 307208 | tf_op jit(solution)/shard_map/ppermute | solution.py:296
  16.4 0.7 pad_add_fusion.pos_ref
  17.1 0.7 collective-permute-done.2.lo_ref
  17.8 3.4 %collective-permute-done.3.hi_ref = bf16[5,20,2,256]{3,2,1,0:T(2,128)(2,1)S(1)} collective-permute-done((bf16[5,20,2,256]{3,2,1,0:T(2,128)(2,1)S(1)}, bf16[5,20,2,256]{3,2,1,0:T(2,128)(2,1)S(1)}, u32[]{:S(2)}, u32[]{:S(2)}) %collective-permute-start.3) | collective-permute-done | bytes 102432 | tf_op jit(solution)/shard_map/ppermute | solution.py:296
  21.2 0.6 copy-done.8
  21.8 10.8 %shard_map.102 = (bf16[32,32,128]{2,1,0:T(8,128)(2,1)}, bf16[16,16,256]{2,1,0:T(8,128)(2,1)}, bf16[2,5120,128]{2,1,0:T(8,128)(2,1)}) custom-call(s32[5]{0:T(128)} %pad_add_fusion.pos_ref, bf16[5,16,16,256]{3,2,1,0:T(8,128)(2,1)} %copy-done, bf16[5,2,16,256]{3,2,1,0:T(8,128)(2,1)} %copy-done.6, bf16[5,2,16,256]{3,2,1,0:T(8,128)(2,1)} %copy-done.5, ...), custom_call_target="tpu_custom_call" | custom-call | tf_op jit(solution)/shard_map/pallas_call | solution.py:264
  32.6 1.6 %slice_bitcast_fusion = bf16[5120,128]{1,0:T(8,128)(2,1)S(1)} fusion(bf16[2,5120,128]{2,1,0:T(8,128)(2,1)} %get-tuple-element.10), kind=kLoop, calls=%fused_computation.2 | loop fusion | bytes 2621440 | tf_op jit(solution)/shard_map/squeeze | solution.py:310
  34.5 2.8 %collective-permute-done.4 = bf16[5120,128]{1,0:T(8,128)(2,1)S(1)} collective-permute-done((bf16[5120,128]{1,0:T(8,128)(2,1)S(1)}, bf16[5120,128]{1,0:T(8,128)(2,1)S(1)}, u32[]{:S(2)}, u32[]{:S(2)}) %collective-permute-start.4) | collective-permute-done | bytes 1310752 | tf_op jit(solution)/shard_map/ppermute | solution.py:310
  37.7 31.6 %all_to_all.20 = bf16[16,320,128]{2,1,0:T(8,128)(2,1)S(1)} all-to-all(bf16[16,320,128]{2,1,0:T(8,128)(2,1)S(1)} %bitcast.21), channel_id=1, replica_groups={{0,1,128,129,32,33,160,161,64,65,192,193,96,97,224,225},{16,17,144,145,..., dimensions={0} | all-to-all | bytes 2621440 | tf_op jit(solution)/shard_map/all_to_all | solution.py:312
  69.4 15.9 %all_to_all.21 = bf16[8,48,128]{2,1,0:T(8,128)(2,1)S(1)} all-to-all(bf16[8,48,128]{2,1,0:T(8,128)(2,1)S(1)} %pad.4), channel_id=1, replica_groups={{0,2,4,6,8,10,12,14},{16,18,20,22,24,26,28,30},{1,3,5,7,9,11,13,15},{17..., dimensions={0} | all-to-all | bytes 196608 | tf_op jit(solution)/shard_map/all_to_all | solution.py:314
  85.4 10.1 %all_to_all.22 = bf16[8,48,128]{2,1,0:T(8,128)(2,1)S(1)} all-to-all(bf16[8,48,128]{2,1,0:T(8,128)(2,1)S(1)} %broadcast_in_dim.6), channel_id=1, replica_groups={{0,2,4,6,8,10,12,14},{16,18,20,22,24,26,28,30},{1,3,5,7,9,11,13,15},{17..., dimensions={0} | all-to-all | bytes 196608 | tf_op jit(solution)/shard_map/all_to_all | solution.py:300
  95.7 18.4 %all_to_all.23 = bf16[16,320,128]{2,1,0:T(8,128)(2,1)S(1)} all-to-all(bf16[16,320,128]{2,1,0:T(8,128)(2,1)S(1)} %broadcast_in_dim.15), channel_id=1, replica_groups={{0,1,128,129,32,33,160,161,64,65,192,193,96,97,224,225},{16,17,144,145,..., dimensions={0} | all-to-all | bytes 2621440 | tf_op jit(solution)/shard_map/all_to_all | solution.py:300
  114.1 5.7 %collective-permute-start.5 = (bf16[5120,128]{1,0:T(8,128)(2,1)S(1)}, bf16[5120,128]{1,0:T(8,128)(2,1)S(1)}, u32[]{:S(2)}, u32[]{:S(2)}) collective-permute-start(bf16[5120,128]{1,0:T(8,128)(2,1)S(1)} %bitcast.20), channel_id=1, source_target_pairs={{0,16},{16,0},{32,48},{48,32},{64,80},{80,64},{96,112},{112,96},{1... | collective-permute-start | bytes 3932168 | tf_op jit(solution)/shard_map/ppermute | solution.py:317
  119.8 2.7 %collective-permute-done.5 = bf16[5120,128]{1,0:T(8,128)(2,1)S(1)} collective-permute-done((bf16[5120,128]{1,0:T(8,128)(2,1)S(1)}, bf16[5120,128]{1,0:T(8,128)(2,1)S(1)}, u32[]{:S(2)}, u32[]{:S(2)}) %collective-permute-start.5) | collective-permute-done | bytes 1310752 | tf_op jit(solution)/shard_map/ppermute | solution.py:317
  122.9 0.9 convert.6
  123.8 1.5 %convert.7 = f32[4,4,256,128]{3,2,1,0:T(8,128)} convert(bf16[4,4,256,128]{3,2,1,0:T(8,128)(2,1)S(1)} %bitcast.22) | non-fusion elementwise | flops 524288 | bytes 3145728 | tf_op jit(solution)/shard_map/reshape | solution.py:338
  125.3 1.6 %maximum_convert_fusion = f32[3,3,256,256]{3,2,1,0:T(8,128)} fusion(bf16[3,3,256,128]{3,2,1,0:T(8,128)(2,1)S(1)} %bitcast.24, bf16[3,3,256,128]{3,2,1,0:T(8,128)(2,1)S(1)} %bitcast.23), kind=kLoop, calls=%fused_computation.5 | loop fusion | flops 2359296 | bytes 3538944 | tf_op jit(solution)/shard_map/convert_element_type | solution.py:340
  (37 shorter events, 2.3 us)
Async XLA Ops:
  0.6 1.0 copy-start.1
  1.6 0.9 copy-start.2
  2.5 0.9 copy-start.3
  3.6 17.6 %copy-start = (bf16[5,16,16,256]{3,2,1,0:T(8,128)(2,1)}, bf16[5,16,16,256]{3,2,1,0:T(8,128)(2,1)S(1)}, u32[]{:S(2)}) copy-start(bf16[5,16,16,256]{3,2,1,0:T(8,128)(2,1)S(1)} %shard_map.101.z_ref) | copy-start | bytes 1966084
  3.6 7.2 %collective-permute-start.1 = (bf16[5,2,16,256]{3,2,1,0:T(8,128)(2,1)S(1)}, bf16[5,2,16,256]{3,2,1,0:T(8,128)(2,1)S(1)}, u32[]{:S(2)}, u32[]{:S(2)}) collective-permute-start(bf16[5,2,16,256]{3,2,1,0:T(8,128)(2,1)S(1)} %get-tuple-element.17), channel_id=1, source_target_pairs={{16,0},{32,16},{48,32},{64,48},{80,64},{96,80},{112,96},{128,112},... | collective-permute-start | bytes 245768 | tf_op jit(solution)/shard_map/ppermute | solution.py:296
  8.8 3.4 %collective-permute-start = (bf16[5,2,16,256]{3,2,1,0:T(8,128)(2,1)S(1)}, bf16[5,2,16,256]{3,2,1,0:T(8,128)(2,1)S(1)}, u32[]{:S(2)}, u32[]{:S(2)}) collective-permute-start(bf16[5,2,16,256]{3,2,1,0:T(8,128)(2,1)S(1)} %get-tuple-element.18), channel_id=1, source_target_pairs={{0,16},{16,32},{32,48},{48,64},{64,80},{80,96},{96,112},{112,128},... | collective-permute-start | bytes 245768 | tf_op jit(solution)/shard_map/ppermute | solution.py:296
  10.9 10.3 %copy-start.5 = (bf16[5,2,16,256]{3,2,1,0:T(8,128)(2,1)}, bf16[5,2,16,256]{3,2,1,0:T(8,128)(2,1)S(1)}, u32[]{:S(2)}) copy-start(bf16[5,2,16,256]{3,2,1,0:T(8,128)(2,1)S(1)} %collective-permute-done.1.down_ref) | copy-start | bytes 245764
  12.2 9.0 %copy-start.6 = (bf16[5,2,16,256]{3,2,1,0:T(8,128)(2,1)}, bf16[5,2,16,256]{3,2,1,0:T(8,128)(2,1)S(1)}, u32[]{:S(2)}) copy-start(bf16[5,2,16,256]{3,2,1,0:T(8,128)(2,1)S(1)} %collective-permute-done.up_ref) | copy-start | bytes 245764
  12.4 5.4 %collective-permute-start.2 = (bf16[5,20,2,256]{3,2,1,0:T(2,128)(2,1)S(1)}, bf16[5,20,2,256]{3,2,1,0:T(2,128)(2,1)S(1)}, u32[]{:S(2)}, u32[]{:S(2)}) collective-permute-start(bf16[5,20,2,256]{3,2,1,0:T(2,128)(2,1)S(1)} %pad_maximum_fusion.1), channel_id=1, source_target_pairs={{0,1},{1,2},{2,3},{3,4},{4,5},{5,6},{6,7},{7,8},{8,9},{9,10},{10,1... | collective-permute-start | bytes 307208 | tf_op jit(solution)/shard_map/ppermute | solution.py:296
  15.1 6.1 %collective-permute-start.3 = (bf16[5,20,2,256]{3,2,1,0:T(2,128)(2,1)S(1)}, bf16[5,20,2,256]{3,2,1,0:T(2,128)(2,1)S(1)}, u32[]{:S(2)}, u32[]{:S(2)}) collective-permute-start(bf16[5,20,2,256]{3,2,1,0:T(2,128)(2,1)S(1)} %pad_maximum_fusion.2), channel_id=1, source_target_pairs={{1,0},{2,1},{3,2},{4,3},{5,4},{6,5},{7,6},{8,7},{9,8},{10,9},{11,1... | collective-permute-start | bytes 307208 | tf_op jit(solution)/shard_map/ppermute | solution.py:296
  17.8 3.4 %copy-start.7 = (bf16[5,20,2,256]{3,2,1,0:T(2,128)(2,1)}, bf16[5,20,2,256]{3,2,1,0:T(2,128)(2,1)S(1)}, u32[]{:S(2)}) copy-start(bf16[5,20,2,256]{3,2,1,0:T(2,128)(2,1)S(1)} %collective-permute-done.2.lo_ref) | copy-start | bytes 307204
  21.2 0.6 copy-start.8
  32.6 4.7 %copy-start.4 = (bf16[2,5120,128]{2,1,0:T(8,128)(2,1)S(1)}, bf16[2,5120,128]{2,1,0:T(8,128)(2,1)}, u32[]{:S(2)}) copy-start(bf16[2,5120,128]{2,1,0:T(8,128)(2,1)} %get-tuple-element.10) | copy-start | bytes 7864324
  34.2 3.1 %collective-permute-start.4 = (bf16[5120,128]{1,0:T(8,128)(2,1)S(1)}, bf16[5120,128]{1,0:T(8,128)(2,1)S(1)}, u32[]{:S(2)}, u32[]{:S(2)}) collective-permute-start(bf16[5120,128]{1,0:T(8,128)(2,1)S(1)} %slice_bitcast_fusion), channel_id=1, source_target_pairs={{0,16},{16,0},{32,48},{48,32},{64,80},{80,64},{96,112},{112,96},{1... | collective-permute-start | bytes 3932168 | tf_op jit(solution)/shard_map/ppermute | solution.py:310
  114.1 8.3 %collective-permute-start.5 = (bf16[5120,128]{1,0:T(8,128)(2,1)S(1)}, bf16[5120,128]{1,0:T(8,128)(2,1)S(1)}, u32[]{:S(2)}, u32[]{:S(2)}) collective-permute-start(bf16[5120,128]{1,0:T(8,128)(2,1)S(1)} %bitcast.20), channel_id=1, source_target_pairs={{0,16},{16,0},{32,48},{48,32},{64,80},{80,64},{96,112},{112,96},{1... | collective-permute-start | bytes 3932168 | tf_op jit(solution)/shard_map/ppermute | solution.py:317

commit v2 on v1

--- a/solution.py
+++ b/solution.py
@@ -23,23 +23,41 @@
     return row * 16 + col
 
 
-PLANE_GROUPS = [
-    [place(x, y, z, core) for x in range(4) for y in range(4)]
-    for z in range(8)
+def device_xyz(device):
+    row, col = divmod(device, 16)
+    return (row >> 1) & 3, ((row >> 3) << 1) | (col & 1), col >> 1, row & 1
+
+
+BLOCK = 32
+BLOCK_GROUPS = [
+    [place(x, y, z + dz, core) for dz in range(2) for x in range(4) for y in range(4)]
+    for z in range(0, 8, 2)
     for core in range(2)
 ]
-DEPTH_GROUPS = [
-    [place(x, y, z, core) for z in range(8)]
-    for x in range(4)
-    for y in range(4)
-    for core in range(2)
-]
+
+
+def depth_shift(step):
+    moves = []
+    for device in range(256):
+        x, y, z, core = device_xyz(device)
+        moves.append((device, place(x, y, z + step, core)))
+    return moves
+
+
 CORE_SWAP = [(i, i ^ 1) for i in range(16)]
 
 
-def split_kernel(bot_ref, skip_ref, cot_ref, out_ref, wide):
-    out_ref[0] = bot_ref[...]
-    for plane, ref in ((1, cot_ref), (3, skip_ref)):
+def split_kernel(
+    bot_hbm, skip_hbm, cot_hbm, out_ref, last_ref, first_ref, bot, skip, cot, wide, sems
+):
+    copies = [
+        pltpu.make_async_copy(src, dst, sems.at[i])
+        for i, (src, dst) in enumerate(((cot_hbm, cot), (skip_hbm, skip), (bot_hbm, bot)))
+    ]
+    for copy in copies:
+        copy.start()
+    for plane, ref, copy in ((1, cot, copies[0]), (3, skip, copies[1])):
+        copy.wait()
         wide[...] = ref[...].astype(F32)
         for col_par in range(2):
             part = wide[:, pl.ds(col_par, TILE, stride=2), :].astype(BF16)
@@ -47,13 +65,30 @@
             lanes = slice(col_par * 128, col_par * 128 + 128)
             out_ref[plane, :, :, lanes] = part[:, 0]
             out_ref[plane + 1, :, :, lanes] = part[:, 1]
+    copies[2].wait()
+    out_ref[0] = bot[...]
+    for plane in range(3):
+        last_ref[2 * plane : 2 * plane + 2] = out_ref[plane, TILE - 2 : TILE]
+        first_ref[2 * plane : 2 * plane + 2] = out_ref[plane, 0:2]
+    last_ref[6] = out_ref[4, TILE - 1]
+    first_ref[6] = out_ref[3, 0]
 
 
 def split(bottom_in, skip_feat, cotangent):
+    vmem = pl.BlockSpec(memory_space=pltpu.VMEM)
+    strip = jax.ShapeDtypeStruct((7, TILE, 256), BF16)
     return pl.pallas_call(
         split_kernel,
-        out_shape=jax.ShapeDtypeStruct((5, TILE, TILE, 256), BF16),
-        scratch_shapes=[pltpu.VMEM((2 * TILE, 2 * TILE, 128), F32)],
+        out_shape=(jax.ShapeDtypeStruct((5, TILE, TILE, 256), BF16), strip, strip),
+        in_specs=[pl.BlockSpec(memory_space=pl.ANY)] * 3,
+        out_specs=(vmem, vmem, vmem),
+        scratch_shapes=[
+            pltpu.VMEM((TILE, TILE, 256), BF16),
+            pltpu.VMEM((2 * TILE, 2 * TILE, 128), BF16),
+            pltpu.VMEM((2 * TILE, 2 * TILE, 128), BF16),
+            pltpu.VMEM((2 * TILE, 2 * TILE, 128), F32),
+            pltpu.SemaphoreType.DMA((3,)),
+        ],
         compiler_params=pltpu.CompilerParams(vmem_limit_bytes=16 << 20),
     )(bottom_in, skip_feat, cotangent)
 
@@ -113,8 +148,8 @@
 
 def main_kernel(
     scale, pos_ref, z_ref, up_ref, down_ref, lo_ref, hi_ref, bk_ref, uk_ref, lk_ref,
-    level_ref, bgrad_ref, grad_ref,
-    ext, bot3, botc, act3, actc, dsilu, cot4, mg4, mg4c, mix4c, pg3c, pgc, inter,
+    mix4c, pg3c, keep_ref, send_ref,
+    ext, bot3, botc, act3, actc, dsilu, cot4, mg4, mg4c, pgc, packed, sems,
 ):
     row0 = pos_ref[0] * TILE
     col0 = pos_ref[1] * TILE
@@ -122,12 +157,24 @@
     image_w = pos_ref[3]
     mine = pos_ref[4]
 
+    core = slice(CORE, CORE + TILE)
     ext[...] = jnp.zeros_like(ext)
-    ext[:, 0:2, CORE : CORE + TILE, :] = up_ref[...].astype(F32)
-    ext[:, 2 : 2 + TILE, CORE : CORE + TILE, :] = z_ref[...].astype(F32)
-    ext[:, 2 + TILE : EXT, CORE : CORE + TILE, :] = down_ref[...].astype(F32)
-    ext[:, :, CORE - 2 : CORE, :] = lo_ref[...].astype(F32)
-    ext[:, :, CORE + TILE : CORE + TILE + 2, :] = hi_ref[...].astype(F32)
+    ext[:, 2 : 2 + TILE, core, :] = z_ref[...].astype(F32)
+    for plane in range(3):
+        two = slice(2 * plane, 2 * plane + 2)
+        ext[plane, 0:2, core, :] = up_ref[two].astype(F32)
+        ext[plane, 2 + TILE : EXT, core, :] = down_ref[two].astype(F32)
+        side = slice(EXT * plane, EXT * plane + EXT)
+        ext[plane, :, CORE - 2 : CORE, :] = lo_ref[side].astype(F32)
+        ext[plane, :, CORE + TILE : CORE + TILE + 2, :] = hi_ref[side].astype(F32)
+    ext[4, 1, core, :] = up_ref[6].astype(F32)
+    ext[3, 2 + TILE, core, :] = down_ref[6].astype(F32)
+    for par in range(2):
+        side = slice(3 * EXT, 3 * EXT + 18)
+        ext[3 + par, 1:19, CORE - 1 : CORE, :] = lo_ref[side, par : par + 1].astype(F32)
+        ext[3 + par, 1:19, CORE + TILE : CORE + TILE + 1, :] = hi_ref[
+            side, par : par + 1
+        ].astype(F32)
 
     def masked(x, first):
         rows = x.shape[0] // PITCH
@@ -179,8 +226,18 @@
         mg4c[par, first : first + 19, :, 384:512] = core_of(c).astype(BF16)
 
     def put(half, row, value):
-        slot = lax.rem(half + mine, 2)
-        grad_ref[slot, pl.ds(row, value.shape[0]), :] = (value * scale).astype(BF16)
+        packed[half, row : row + value.shape[0], :] = (value * scale).astype(BF16)
+
+    def hand_out(number, half, first, count, act):
+        rows = pl.ds(first, count)
+        for which in range(2):
+
+            @pl.when(mine == which)
+            def _():
+                out = keep_ref if half == which else send_ref
+                act(pltpu.make_async_copy(packed.at[half, rows], out.at[rows], sems.at[number]))
+
+    parts = ((0, 0, 0, 4096), (1, 1, 0, 4608), (2, 0, 4096, HALF - 4096), (3, 1, 4608, HALF - 4608))
 
     act_t = actc[...].T
     for a in range(4):
@@ -188,6 +245,7 @@
         prod = nn(act_t, flat(mg4c[src, 2 + shift : 18 + shift]))
         for b in range(4):
             put(0, (4 * a + b) * 256, prod[:, 128 * b : 128 * b + 128])
+    hand_out(*parts[0], lambda copy: copy.start())
 
     agrad = jnp.zeros((18 * PITCH, 256), F32)
     for a in range(4):
@@ -203,6 +261,7 @@
         prod = tn(flat(botc[a : a + 16]), pgc[...])
         put(1, 768 * a, prod[:, :128])
         put(1, 2304 + 768 * a, prod[:, 128:])
+    hand_out(*parts[1], lambda copy: copy.start())
 
     for par in range(2):
         total = flat(ext[3 + par, 1:19])
@@ -239,6 +298,15 @@
     put(0, 4864, jnp.zeros((HALF - 4864, 128), F32))
     put(1, 4992, jnp.zeros((HALF - 4992, 128), F32))
 
+    for part in parts[2:]:
+        hand_out(*part, lambda copy: copy.start())
+    for part in parts:
+        hand_out(*part, lambda copy: copy.wait())
+
+
+def rest_kernel(mix4c, pg3c, bk_ref, lk_ref, level_ref, bgrad_ref, inter):
+    zero = jnp.zeros((128, 128), BF16)
+
     for par in range(2):
         total = jnp.zeros((TILE * TILE, 256), F32)
         for a in range(3):
@@ -259,17 +327,34 @@
     bgrad_ref[...] = total.reshape(TILE, TILE, 256).astype(BF16)
 
 
+def rest_work(mix4c, pg3c, bot_kernel, lvl_kernel):
+    return pl.pallas_call(
+        rest_kernel,
+        out_shape=(
+            jax.ShapeDtypeStruct((2 * TILE, 2 * TILE, 128), BF16),
+            jax.ShapeDtypeStruct((TILE, TILE, 256), BF16),
+        ),
+        scratch_shapes=[pltpu.VMEM((TILE, 2, 2 * TILE, 128), F32)],
+        compiler_params=pltpu.CompilerParams(vmem_limit_bytes=16 << 20),
+        cost_estimate=pl.CostEstimate(
+            flops=1000000000, bytes_accessed=3000000, transcendentals=0
+        ),
+    )(mix4c, pg3c, bot_kernel, lvl_kernel)
+
+
 def local_work(scale, pos, z, up, down, lo, hi, bot_kernel, up_kernel, lvl_kernel):
     vmem = pl.BlockSpec(memory_space=pltpu.VMEM)
+    anywhere = pl.BlockSpec(memory_space=pl.ANY)
     return pl.pallas_call(
         functools.partial(main_kernel, scale),
         out_shape=(
-            jax.ShapeDtypeStruct((2 * TILE, 2 * TILE, 128), BF16),
-            jax.ShapeDtypeStruct((TILE, TILE, 256), BF16),
-            jax.ShapeDtypeStruct((2, HALF, 128), BF16),
+            jax.ShapeDtypeStruct((2, 18, TILE, 512), BF16),
+            jax.ShapeDtypeStruct((18, TILE, 768), BF16),
+            jax.ShapeDtypeStruct((HALF, 128), BF16),
+            jax.ShapeDtypeStruct((HALF, 128), BF16),
         ),
         in_specs=[pl.BlockSpec(memory_space=pltpu.SMEM)] + [vmem] * 8,
-        out_specs=(vmem, vmem, vmem),
+        out_specs=(vmem, vmem, anywhere, anywhere),
         scratch_shapes=[
             pltpu.VMEM((5, EXT, PITCH, 256), F32),
             pltpu.VMEM((EXT, PITCH, 768), BF16),
@@ -280,13 +365,60 @@
             pltpu.VMEM((2, EXT, PITCH, 512), BF16),
             pltpu.VMEM((2, EXT, PITCH, 512), BF16),
             pltpu.VMEM((2, EXT, TILE, 512), BF16),
-            pltpu.VMEM((2, 18, TILE, 512), BF16),
-            pltpu.VMEM((18, TILE, 768), BF16),
             pltpu.VMEM((TILE * TILE, 256), BF16),
-            pltpu.VMEM((TILE, 2, 2 * TILE, 128), F32),
+            pltpu.VMEM((2, HALF, 128), BF16),
+            pltpu.SemaphoreType.DMA((4,)),
         ],
-        compiler_params=pltpu.CompilerParams(vmem_limit_bytes=56 << 20),
+        compiler_params=pltpu.CompilerParams(vmem_limit_bytes=48 << 20),
     )(pos, z, up, down, lo, hi, bot_kernel, up_kernel, lvl_kernel)
+
+
+def unpack_kernel(
+    pos_ref, half_hbm, other_hbm, up_hbm, bot_hbm, lvl_hbm,
+    half, other, up, bot, lvl, in_sems, out_sems,
+):
+    ins = [
+        pltpu.make_async_copy(src, dst, in_sems.at[i])
+        for i, (src, dst) in enumerate(((half_hbm, half), (other_hbm, other)))
+    ]
+    for copy in ins:
+        copy.start()
+    for copy in ins:
+        copy.wait()
+    for which in range(2):
+
+        @pl.when(pos_ref[4] == which)
+        def _():
+            even, odd = (half, other) if which == 0 else (other, half)
+            up[...] = even[0:4096].astype(F32)
+            lvl[0:768] = even[4096:4864].astype(F32)
+            lvl[768:1152] = odd[4608:4992].astype(F32)
+            bot[:, 0:128] = odd[0:2304].astype(F32)
+            bot[:, 128:256] = odd[2304:4608].astype(F32)
+
+    outs = [
+        pltpu.make_async_copy(src, dst, out_sems.at[i])
+        for i, (src, dst) in enumerate(((up, up_hbm), (bot, bot_hbm), (lvl, lvl_hbm)))
+    ]
+    for copy in outs:
+        copy.start()
+    for copy in outs:
+        copy.wait()
+
+
+def unpack(pos, half, other):
+    anywhere = pl.BlockSpec(memory_space=pl.ANY)
+    shapes = ((4096, 128), (2304, 256), (1152, 128))
+    return pl.pallas_call(
+        unpack_kernel,
+        out_shape=tuple(jax.ShapeDtypeStruct(shape, F32) for shape in shapes),
+        in_specs=[pl.BlockSpec(memory_space=pltpu.SMEM), anywhere, anywhere],
+        out_specs=(anywhere,) * 3,
+        scratch_shapes=[pltpu.VMEM((HALF, 128), BF16)] * 2
+        + [pltpu.VMEM(shape, F32) for shape in shapes]
+        + [pltpu.SemaphoreType.DMA((2,)), pltpu.SemaphoreType.DMA((3,))],
+        compiler_params=pltpu.CompilerParams(vmem_limit_bytes=16 << 20),
+    )(pos, half, other)
 
 
 def shifted(last, first, axis):
@@ -296,53 +428,63 @@
     return lax.ppermute(last, axis, up), lax.ppermute(first, axis, down)
 
 
-def spread(x, count, groups):
-    return lax.all_to_all(
-        jnp.broadcast_to(x[None], (count,) + x.shape), AXES, 0, 0, axis_index_groups=groups
-    )
-
-
-def sum_parts(x):
-    return jnp.sum(x.astype(F32), axis=0).astype(BF16)
-
-
-def total_over_devices(grads):
-    got = lax.ppermute(grads[1], "row", CORE_SWAP)
-    half = (grads[0].astype(F32) + got.astype(F32)).astype(BF16).reshape(16, HALF // 16, 128)
-    part = sum_parts(lax.all_to_all(half, AXES, 0, 0, axis_index_groups=PLANE_GROUPS))
-    part = jnp.pad(part.reshape(8, HALF // 128, 128), ((0, 0), (0, 8), (0, 0)))
-    piece = sum_parts(lax.all_to_all(part, AXES, 0, 0, axis_index_groups=DEPTH_GROUPS))
-    part = spread(piece, 8, DEPTH_GROUPS)[:, : HALF // 128].reshape(HALF // 16, 128)
-    half = spread(part, 16, PLANE_GROUPS).reshape(HALF, 128)
-    other = lax.ppermute(half, "row", CORE_SWAP)
-    core = lax.rem(lax.axis_index("row"), 2)
-    return jnp.where(core == 0, half, other), jnp.where(core == 0, other, half)
+def exchange(x):
+    return lax.all_to_all(x, AXES, 0, 0, axis_index_groups=BLOCK_GROUPS)
+
+
+def total_over_devices(keep, send):
+    got = lax.ppermute(send, "row", CORE_SWAP)
+    half = (keep.astype(F32) + got.astype(F32)).astype(BF16)
+    parts = exchange(half.reshape(BLOCK, HALF // BLOCK, 128))
+    part = jnp.sum(parts.astype(F32), axis=0).astype(BF16)
+    planes = [lax.ppermute(part, AXES, depth_shift(step)) for step in (2, 6, 4)]
+    pair = lax.axis_index("col") // 4
+    terms = [part] + planes
+    places = [pair, (pair + 3) % 4, (pair + 1) % 4, (pair + 2) % 4]
+    total = jnp.zeros(part.shape, F32)
+    for slot in range(4):
+        for term, where in zip(terms, places):
+            total = total + jnp.where(where == slot, term.astype(F32), 0.0)
+    total = total.astype(BF16)
+    half = exchange(jnp.broadcast_to(total[None], parts.shape)).reshape(HALF, 128)
+    return half, lax.ppermute(half, "row", CORE_SWAP)
 
 
 def on_device(bottom_in, skip_feat, cotangent, bot_kernel, up_kernel, lvl_kernel):
     rows, cols = lax.axis_size("row"), lax.axis_size("col")
     scale = 1.0 / float(2 * TILE * rows * 2 * TILE * cols) ** 0.5
-    z = split(bottom_in, skip_feat, cotangent)
-    up, down = shifted(z[:, TILE - 2 :], z[:, :2], "row")
-    last = jnp.concatenate([up[:, :, -2:], z[:, :, -2:], down[:, :, -2:]], axis=1)
-    first = jnp.concatenate([up[:, :, :2], z[:, :, :2], down[:, :, :2]], axis=1)
-    lo, hi = shifted(last, first, "col")
+    z, last, first = split(bottom_in, skip_feat, cotangent)
+    up, down = shifted(last, first, "row")
+
+    def side(cols, skip_col):
+        parts = [
+            jnp.concatenate(
+                [up[2 * p : 2 * p + 2, cols], z[p, :, cols], down[2 * p : 2 * p + 2, cols]], axis=0
+            )
+            for p in range(3)
+        ]
+        blank = jnp.zeros((1, 1, 256), BF16)
+        even = jnp.concatenate([blank, z[3, :, skip_col], down[6:7, skip_col]], axis=0)
+        odd = jnp.concatenate([up[6:7, skip_col], z[4, :, skip_col], blank], axis=0)
+        return jnp.concatenate(parts + [jnp.concatenate([even, odd], axis=1)], axis=0)
+
+    lo, hi = shifted(
+        side(slice(TILE - 2, TILE), slice(TILE - 1, TILE)), side(slice(0, 2), slice(0, 1)), "col"
+    )
     row = lax.axis_index("row")
     pos = jnp.stack(
         [row, lax.axis_index("col"), jnp.int32(TILE * rows), jnp.int32(TILE * cols), row % 2]
     ).astype(jnp.int32)
-    level_out, bottom_grad, grads = local_work(
+    mix4c, pg3c, keep, send = local_work(
         scale, pos, z, up, down, lo, hi, bot_kernel, up_kernel, lvl_kernel
     )
-    even, odd = total_over_devices(grads)
-    up_grad = even[:4096].astype(F32).reshape(4, 4, 256, 128)
-    lvl_grad = jnp.concatenate([even[4096:4864], odd[4608:4992]], axis=0).astype(F32)
-    bot_grad = jnp.concatenate([odd[:2304], odd[2304:4608]], axis=1).astype(F32)
+    level_out, bottom_grad = rest_work(mix4c, pg3c, bot_kernel, lvl_kernel)
+    up_grad, bot_grad, lvl_grad = unpack(pos, *total_over_devices(keep, send))
     return (
         level_out,
         bottom_grad,
         lvl_grad.reshape(3, 3, 128, 128),
-        up_grad,
+        up_grad.reshape(4, 4, 256, 128),
         bot_grad.reshape(3, 3, 256, 256),
     )
 

time: 127 us -> 118 us (0.929)
  blocking collectives: 75.9 us -> 53.6 us
  starting transfers between devices: 16.9 us -> 23.6 us
  waiting for transfers between devices: 10.8 us -> 17.1 us
  Pallas kernels: 10.9 us -> 14.4 us
  other arithmetic: 5.75 us -> 2.35 us
    all_to_all x4 -> x2, blocking collectives: 75.9 us -> 53.6 us  [exchange(): return lax.all_to_all(x, AXES, 0, 0, axis_index_groups=BLOCK_GROUPS)]
    ppermute x2 -> x5, starting transfers between devices: 6.02 us -> 12.7 us  [the longest x3 8.71 us: total_over_devices(): planes = [lax.ppermute(part, AXES, depth_shift(step)) for step in (2, 6, 4)]]
    pallas_call x1 -> x3, Pallas kernels: 0.16 us -> 5.5 us  [the longest x1 3.39 us: unpack(): pl.pallas_call(unpack_kernel, out_shape=tuple((jax.ShapeDtypeStruct(shape...]
    ppermute x2 -> x5, waiting for transfers between devices: 5.43 us -> 9.8 us  [the longest x3 5.61 us: total_over_devices(): planes = [lax.ppermute(part, AXES, depth_shift(step)) for step in (2, 6, 4)]]
    pallas_call x1, Pallas kernels: 10.8 us -> 8.85 us  [local_work(): pl.pallas_call(functools.partial(main_kernel, scale), out_shape=(jax.Shap...]
    ppermute x4, waiting for transfers between devices: 5.36 us -> 7.26 us  [shifted(): return (lax.ppermute(last, axis, up), lax.ppermute(first, axis, down))]
    unnamed x18 -> x23, local copies, waits for them, and re-layouts: 3.45 us -> 5.28 us
    convert_element_type x3 -> x2, other arithmetic: 2.78 us -> 1.23 us  [the longest x1 0.89 us: total_over_devices(): total = total.astype(BF16)]
  transfers between devices with their start and end apart: 6 -> 9, of which waited for: 5 -> 6; matrix products, arithmetic and copies ran while one was open for 1% -> 0% of each run, Pallas kernels for 0% -> 1%
where the time goes in v2:
time: 118 us; the launch traced here: 117 us
  blocking collectives  53.6 us (45%)
  starting transfers between devices  23.6 us (20%)
  waiting for transfers between devices  17.1 us (14%)
  Pallas kernels  14.4 us (12%)
  local copies, waits for them, and re-layouts  5.53 us (5%)
  other arithmetic  2.35 us (2%)
    all_to_all x2, blocking collectives, exchange(): return lax.all_to_all(x, AXES, 0, 0, axis_index_groups=BLOCK_GROUPS)  53.6 us
    ppermute x4, starting transfers between devices, shifted(): return (lax.ppermute(last, axis, up), lax.ppermute(first, axis, down))  10.9 us
    pallas_call x1, Pallas kernels, local_work(): pl.pallas_call(functools.partial(main_kernel, scale), out_shape=(jax.Shap...  8.85 us
    ppermute x3, starting transfers between devices, total_over_devices(): planes = [lax.ppermute(part, AXES, depth_shift(step)) for step in (2, 6, 4)]  8.71 us
    ppermute x4, waiting for transfers between devices, shifted(): return (lax.ppermute(last, axis, up), lax.ppermute(first, axis, down))  7.26 us
    ppermute x3, waiting for transfers between devices, total_over_devices(): planes = [lax.ppermute(part, AXES, depth_shift(step)) for step in (2, 6, 4)]  5.61 us
    unnamed x23, local copies, waits for them, and re-layouts  5.28 us
    ppermute x1, starting transfers between devices, total_over_devices(): return (half, lax.ppermute(half, 'row', CORE_SWAP))  3.85 us
  transfers between devices with their start and end apart: 9, of which 6 were waited for; matrix products, arithmetic and copies ran while one was open for 0% of the time, Pallas kernels for 1%

profile of v2, /device:TPU:1, one launch (start us, length us, event | category | flops | bytes accessed | tf_op | source)
XLA Modules:
  0.0 117.3 jit_solution(10163389572895291797)
XLA Ops:
  0.7 1.0 copy-done.4
  1.7 0.9 copy-done.5
  2.6 0.9 copy-done.6
  4.0 4.5 %collective-permute-start = (bf16[7,16,256]{2,1,0:T(8,128)(2,1)S(1)}, bf16[7,16,256]{2,1,0:T(8,128)(2,1)S(1)}, u32[]{:S(2)}, u32[]{:S(2)}) collective-permute-start(bf16[7,16,256]{2,1,0:T(8,128)(2,1)S(1)} %get-tuple-element.18), channel_id=1, source_target_pairs={{0,16},{16,32},{32,48},{48,64},{64,80},{80,96},{96,112},{112,128},... | collective-permute-start | bytes 172040 | tf_op jit(solution)/shard_map/ppermute | solution.py:428
  8.5 1.9 %collective-permute-start.1 = (bf16[7,16,256]{2,1,0:T(8,128)(2,1)S(1)}, bf16[7,16,256]{2,1,0:T(8,128)(2,1)S(1)}, u32[]{:S(2)}, u32[]{:S(2)}) collective-permute-start(bf16[7,16,256]{2,1,0:T(8,128)(2,1)S(1)} %get-tuple-element.19), channel_id=1, source_target_pairs={{16,0},{32,16},{48,32},{64,48},{80,64},{96,80},{112,96},{128,112},... | collective-permute-start | bytes 172040 | tf_op jit(solution)/shard_map/ppermute | solution.py:428
  10.6 3.4 %collective-permute-done.1.down_ref = bf16[7,16,256]{2,1,0:T(8,128)(2,1)S(1)} collective-permute-done((bf16[7,16,256]{2,1,0:T(8,128)(2,1)S(1)}, bf16[7,16,256]{2,1,0:T(8,128)(2,1)S(1)}, u32[]{:S(2)}, u32[]{:S(2)}) %collective-permute-start.1) | collective-permute-done | bytes 57376 | tf_op jit(solution)/shard_map/ppermute | solution.py:428
  14.4 3.2 %collective-permute-start.2 = (bf16[78,2,256]{2,1,0:T(2,128)(2,1)S(1)}, bf16[78,2,256]{2,1,0:T(2,128)(2,1)S(1)}, u32[]{:S(2)}, u32[]{:S(2)}) collective-permute-start(bf16[78,2,256]{2,1,0:T(2,128)(2,1)S(1)} %constant_dynamic-update-slice_fusion), channel_id=1, source_target_pairs={{0,1},{1,2},{2,3},{3,4},{4,5},{5,6},{6,7},{7,8},{8,9},{9,10},{10,1... | collective-permute-start | bytes 239624 | tf_op jit(solution)/shard_map/ppermute | solution.py:428
  17.6 1.3 %collective-permute-start.3 = (bf16[78,2,256]{2,1,0:T(2,128)(2,1)S(1)}, bf16[78,2,256]{2,1,0:T(2,128)(2,1)S(1)}, u32[]{:S(2)}, u32[]{:S(2)}) collective-permute-start(bf16[78,2,256]{2,1,0:T(2,128)(2,1)S(1)} %constant_dynamic-update-slice_fusion.10), channel_id=1, source_target_pairs={{1,0},{2,1},{3,2},{4,3},{5,4},{6,5},{7,6},{8,7},{9,8},{10,9},{11,1... | collective-permute-start | bytes 239624 | tf_op jit(solution)/shard_map/ppermute | solution.py:428
  19.0 3.8 %collective-permute-done.3.hi_ref = bf16[78,2,256]{2,1,0:T(2,128)(2,1)S(1)} collective-permute-done((bf16[78,2,256]{2,1,0:T(2,128)(2,1)S(1)}, bf16[78,2,256]{2,1,0:T(2,128)(2,1)S(1)}, u32[]{:S(2)}, u32[]{:S(2)}) %collective-permute-start.3) | collective-permute-done | bytes 79904 | tf_op jit(solution)/shard_map/ppermute | solution.py:428
  22.9 1.2 %copy-done.1 = bf16[4,4,256,128]{3,2,1,0:T(8,128)(2,1)S(1)} copy-done((bf16[4,4,256,128]{3,2,1,0:T(8,128)(2,1)S(1)}, bf16[4,4,256,128]{3,2,1,0:T(8,128)(2,1)}, u32[]{:S(2)}) %copy-start.1) | copy-done | bytes 1048600
  24.1 1.0 copy-done.2
  25.1 8.9 %shard_map.102 = (bf16[2,18,16,512]{3,2,1,0:T(8,128)(2,1)S(1)}, bf16[18,16,768]{2,1,0:T(8,128)(2,1)S(1)}, bf16[5120,128]{1,0:T(8,128)(2,1)S(1)}, bf16[5120,128]{1,0:T(8,128)(2,1)}) custom-call(s32[5]{0:T(128)S(1)} %pad_add_fusion.pos_ref, bf16[5,16,16,256]{3,2,1,0:T(8,128)(2,1)S(1)} %get-tuple-element.17.z_ref, ...), custom_call_target="tpu_custom_call" | custom-call | tf_op jit(solution)/shard_map/pallas_call | solution.py:348
  34.0 3.2 %collective-permute-done.4 = bf16[5120,128]{1,0:T(8,128)(2,1)S(1)} collective-permute-done((bf16[5120,128]{1,0:T(8,128)(2,1)}, bf16[5120,128]{1,0:T(8,128)(2,1)S(1)}, u32[]{:S(2)}, u32[]{:S(2)}) %collective-permute-start.4) | collective-permute-done | bytes 1310752 | tf_op jit(solution)/shard_map/ppermute | solution.py:436
  37.6 32.2 %all_to_all.10 = bf16[32,160,128]{2,1,0:T(8,128)(2,1)S(1)} all-to-all(bf16[32,160,128]{2,1,0:T(8,128)(2,1)S(1)} %bitcast.30), channel_id=1, replica_groups={{0,1,128,129,32,33,160,161,64,65,192,193,96,97,224,225,2,3,130,131,34,3..., dimensions={0} | all-to-all | bytes 2621440 | tf_op jit(solution)/shard_map/all_to_all | solution.py:432
  70.6 5.1 %collective-permute-start.7 = (bf16[160,128]{1,0:T(8,128)(2,1)}, bf16[160,128]{1,0:T(8,128)(2,1)S(1)}, u32[]{:S(2)}, u32[]{:S(2)}) collective-permute-start(bf16[160,128]{1,0:T(8,128)(2,1)} %reduce_sum.12), channel_id=1, source_target_pairs={{0,8},{1,9},{2,10},{3,11},{4,12},{5,13},{6,14},{7,15},{8,0},{9,1},... | collective-permute-start | bytes 122888 | tf_op jit(solution)/shard_map/ppermute | solution.py:440
  75.7 3.6 %collective-permute-start.6 = (bf16[160,128]{1,0:T(8,128)(2,1)}, bf16[160,128]{1,0:T(8,128)(2,1)S(1)}, u32[]{:S(2)}, u32[]{:S(2)}) collective-permute-start(bf16[160,128]{1,0:T(8,128)(2,1)} %reduce_sum.12), channel_id=1, source_target_pairs={{0,12},{1,13},{2,14},{3,15},{4,0},{5,1},{6,2},{7,3},{8,4},{9,5},{1... | collective-permute-start | bytes 122888 | tf_op jit(solution)/shard_map/ppermute | solution.py:440
  79.3 1.7 %collective-permute-done.6 = bf16[160,128]{1,0:T(8,128)(2,1)S(1)} collective-permute-done((bf16[160,128]{1,0:T(8,128)(2,1)}, bf16[160,128]{1,0:T(8,128)(2,1)S(1)}, u32[]{:S(2)}, u32[]{:S(2)}) %collective-permute-start.6) | collective-permute-done | bytes 40992 | tf_op jit(solution)/shard_map/ppermute | solution.py:440
  81.0 3.9 %collective-permute-done.5 = bf16[160,128]{1,0:T(8,128)(2,1)S(1)} collective-permute-done((bf16[160,128]{1,0:T(8,128)(2,1)}, bf16[160,128]{1,0:T(8,128)(2,1)S(1)}, u32[]{:S(2)}, u32[]{:S(2)}) %collective-permute-start.5) | collective-permute-done | bytes 40992 | tf_op jit(solution)/shard_map/ppermute | solution.py:440
  84.9 0.9 fusion.15
  86.0 21.4 %all_to_all.11 = bf16[32,160,128]{2,1,0:T(8,128)(2,1)S(1)} all-to-all(bf16[32,160,128]{2,1,0:T(8,128)(2,1)S(1)} %broadcast_in_dim.26), channel_id=1, replica_groups={{0,1,128,129,32,33,160,161,64,65,192,193,96,97,224,225,2,3,130,131,34,3..., dimensions={0} | all-to-all | bytes 2621440 | tf_op jit(solution)/shard_map/all_to_all | solution.py:432
  107.4 3.9 %collective-permute-start.8 = (bf16[5120,128]{1,0:T(8,128)(2,1)S(1)}, bf16[5120,128]{1,0:T(8,128)(2,1)S(1)}, u32[]{:S(2)}, u32[]{:S(2)}) collective-permute-start(bf16[5120,128]{1,0:T(8,128)(2,1)S(1)} %bitcast.28), channel_id=1, source_target_pairs={{0,16},{16,0},{32,48},{48,32},{64,80},{80,64},{96,112},{112,96},{1... | collective-permute-start | bytes 3932168 | tf_op jit(solution)/shard_map/ppermute | solution.py:450
  111.2 1.7 %shard_map.103 = (bf16[32,32,128]{2,1,0:T(8,128)(2,1)}, bf16[16,16,256]{2,1,0:T(8,128)(2,1)}) custom-call(bf16[2,18,16,512]{3,2,1,0:T(8,128)(2,1)S(1)} %get-tuple-element.20.mix4c, bf16[18,16,768]{2,1,0:T(8,128)(2,1)S(1)} %get-tuple-element.21.pg3c, bf16[3,3,256,256]{3,2,1,0:T(8,128)(2,1)S(1)} %copy-done, bf16[3,3,128,128]{3,2,1,0:T(8,128)(2,1)S(1)} %copy-done.3), custom_call_target="tpu_custom_call" | custom-call | flops 1000000000 | bytes 3000000 | tf_op jit(solution)/shard_map/pallas_call | solution.py:331
  112.9 1.0 collective-permute-done.8.other_hbm
  113.9 3.4 %shard_map.104 = (f32[4096,128]{1,0:T(8,128)}, f32[2304,256]{1,0:T(8,128)}, f32[1152,128]{1,0:T(8,128)}) custom-call(s32[5]{0:T(128)S(1)} %pad_add_fusion.pos_ref, bf16[5120,128]{1,0:T(8,128)(2,1)S(1)} %bitcast.29, bf16[5120,128]{1,0:T(8,128)(2,1)S(1)} %collective-permute-done.8.other_hbm), custom_call_target="tpu_custom_call" | custom-call | tf_op jit(solution)/shard_map/pallas_call | solution.py:412
  (36 shorter events, 2.4 us)
Async XLA Ops:
  0.6 22.2 %copy-start = (bf16[3,3,256,256]{3,2,1,0:T(8,128)(2,1)S(1)}, bf16[3,3,256,256]{3,2,1,0:T(8,128)(2,1)}, u32[]{:S(2)}) copy-start(bf16[3,3,256,256]{3,2,1,0:T(8,128)(2,1)} %bk_ref.3) | copy-start | bytes 3538948
  0.6 1.0 copy-start.4
  1.7 0.9 copy-start.5
  2.6 0.9 copy-start.6
  4.0 6.5 %collective-permute-start = (bf16[7,16,256]{2,1,0:T(8,128)(2,1)S(1)}, bf16[7,16,256]{2,1,0:T(8,128)(2,1)S(1)}, u32[]{:S(2)}, u32[]{:S(2)}) collective-permute-start(bf16[7,16,256]{2,1,0:T(8,128)(2,1)S(1)} %get-tuple-element.18), channel_id=1, source_target_pairs={{0,16},{16,32},{32,48},{48,64},{64,80},{80,96},{96,112},{112,128},... | collective-permute-start | bytes 172040 | tf_op jit(solution)/shard_map/ppermute | solution.py:428
  8.5 5.5 %collective-permute-start.1 = (bf16[7,16,256]{2,1,0:T(8,128)(2,1)S(1)}, bf16[7,16,256]{2,1,0:T(8,128)(2,1)S(1)}, u32[]{:S(2)}, u32[]{:S(2)}) collective-permute-start(bf16[7,16,256]{2,1,0:T(8,128)(2,1)S(1)} %get-tuple-element.19), channel_id=1, source_target_pairs={{16,0},{32,16},{48,32},{64,48},{80,64},{96,80},{112,96},{128,112},... | collective-permute-start | bytes 172040 | tf_op jit(solution)/shard_map/ppermute | solution.py:428
  14.4 4.7 %collective-permute-start.2 = (bf16[78,2,256]{2,1,0:T(2,128)(2,1)S(1)}, bf16[78,2,256]{2,1,0:T(2,128)(2,1)S(1)}, u32[]{:S(2)}, u32[]{:S(2)}) collective-permute-start(bf16[78,2,256]{2,1,0:T(2,128)(2,1)S(1)} %constant_dynamic-update-slice_fusion), channel_id=1, source_target_pairs={{0,1},{1,2},{2,3},{3,4},{4,5},{5,6},{6,7},{7,8},{8,9},{9,10},{10,1... | collective-permute-start | bytes 239624 | tf_op jit(solution)/shard_map/ppermute | solution.py:428
  17.6 5.2 %collective-permute-start.3 = (bf16[78,2,256]{2,1,0:T(2,128)(2,1)S(1)}, bf16[78,2,256]{2,1,0:T(2,128)(2,1)S(1)}, u32[]{:S(2)}, u32[]{:S(2)}) collective-permute-start(bf16[78,2,256]{2,1,0:T(2,128)(2,1)S(1)} %constant_dynamic-update-slice_fusion.10), channel_id=1, source_target_pairs={{1,0},{2,1},{3,2},{4,3},{5,4},{6,5},{7,6},{8,7},{9,8},{10,9},{11,1... | collective-permute-start | bytes 239624 | tf_op jit(solution)/shard_map/ppermute | solution.py:428
  22.9 1.2 %copy-start.1 = (bf16[4,4,256,128]{3,2,1,0:T(8,128)(2,1)S(1)}, bf16[4,4,256,128]{3,2,1,0:T(8,128)(2,1)}, u32[]{:S(2)}) copy-start(bf16[4,4,256,128]{3,2,1,0:T(8,128)(2,1)} %uk_ref.1) | copy-start | bytes 3145732
  24.1 1.0 copy-start.2
  33.9 3.3 %collective-permute-start.4 = (bf16[5120,128]{1,0:T(8,128)(2,1)}, bf16[5120,128]{1,0:T(8,128)(2,1)S(1)}, u32[]{:S(2)}, u32[]{:S(2)}) collective-permute-start(bf16[5120,128]{1,0:T(8,128)(2,1)} %get-tuple-element.25), channel_id=1, source_target_pairs={{0,16},{16,0},{32,48},{48,32},{64,80},{80,64},{96,112},{112,96},{1... | collective-permute-start | bytes 3932168 | tf_op jit(solution)/shard_map/ppermute | solution.py:436
  70.6 8.7 %collective-permute-start.7 = (bf16[160,128]{1,0:T(8,128)(2,1)}, bf16[160,128]{1,0:T(8,128)(2,1)S(1)}, u32[]{:S(2)}, u32[]{:S(2)}) collective-permute-start(bf16[160,128]{1,0:T(8,128)(2,1)} %reduce_sum.12), channel_id=1, source_target_pairs={{0,8},{1,9},{2,10},{3,11},{4,12},{5,13},{6,14},{7,15},{8,0},{9,1},... | collective-permute-start | bytes 122888 | tf_op jit(solution)/shard_map/ppermute | solution.py:440
  75.7 5.3 %collective-permute-start.6 = (bf16[160,128]{1,0:T(8,128)(2,1)}, bf16[160,128]{1,0:T(8,128)(2,1)S(1)}, u32[]{:S(2)}, u32[]{:S(2)}) collective-permute-start(bf16[160,128]{1,0:T(8,128)(2,1)} %reduce_sum.12), channel_id=1, source_target_pairs={{0,12},{1,13},{2,14},{3,15},{4,0},{5,1},{6,2},{7,3},{8,4},{9,5},{1... | collective-permute-start | bytes 122888 | tf_op jit(solution)/shard_map/ppermute | solution.py:440
  79.3 5.6 %collective-permute-start.5 = (bf16[160,128]{1,0:T(8,128)(2,1)}, bf16[160,128]{1,0:T(8,128)(2,1)S(1)}, u32[]{:S(2)}, u32[]{:S(2)}) collective-permute-start(bf16[160,128]{1,0:T(8,128)(2,1)} %reduce_sum.12), channel_id=1, source_target_pairs={{0,4},{1,5},{2,6},{3,7},{4,8},{5,9},{6,10},{7,11},{8,12},{9,13},{1... | collective-permute-start | bytes 122888 | tf_op jit(solution)/shard_map/ppermute | solution.py:440
  86.0 25.2 %copy-start.3 = (bf16[3,3,128,128]{3,2,1,0:T(8,128)(2,1)S(1)}, bf16[3,3,128,128]{3,2,1,0:T(8,128)(2,1)}, u32[]{:S(2)}) copy-start(bf16[3,3,128,128]{3,2,1,0:T(8,128)(2,1)} %lk_ref.3) | copy-start | bytes 884740
  107.4 6.5 %collective-permute-start.8 = (bf16[5120,128]{1,0:T(8,128)(2,1)S(1)}, bf16[5120,128]{1,0:T(8,128)(2,1)S(1)}, u32[]{:S(2)}, u32[]{:S(2)}) collective-permute-start(bf16[5120,128]{1,0:T(8,128)(2,1)S(1)} %bitcast.28), channel_id=1, source_target_pairs={{0,16},{16,0},{32,48},{48,32},{64,80},{80,64},{96,112},{112,96},{1... | collective-permute-start | bytes 3932168 | tf_op jit(solution)/shard_map/ppermute | solution.py:450

commit v3 on v2

--- a/solution.py
+++ b/solution.py
@@ -14,6 +14,7 @@
 EXT = TILE + 4
 PITCH = 32
 CORE = 8
+WHOLE = 62 << 20
 HALF = 5120
 
 
@@ -45,11 +46,15 @@
 
 
 CORE_SWAP = [(i, i ^ 1) for i in range(16)]
+INNER_PAIRS = CORE_SWAP
+OUTER_PAIRS = [pair for i in range(1, 15, 2) for pair in ((i, i + 1), (i + 1, i))]
 
 
 def split_kernel(
-    bot_hbm, skip_hbm, cot_hbm, out_ref, last_ref, first_ref, bot, skip, cot, wide, sems
+    bot_hbm, skip_hbm, cot_hbm, out_hbm, inner_hbm, outer_hbm,
+    bot, skip, cot, wide, out_ref, inner_ref, outer_ref, sems, out_sems,
 ):
+    even = lax.rem(lax.axis_index("row"), 2) == 0
     copies = [
         pltpu.make_async_copy(src, dst, sems.at[i])
         for i, (src, dst) in enumerate(((cot_hbm, cot), (skip_hbm, skip), (bot_hbm, bot)))
@@ -68,28 +73,43 @@
     copies[2].wait()
     out_ref[0] = bot[...]
     for plane in range(3):
-        last_ref[2 * plane : 2 * plane + 2] = out_ref[plane, TILE - 2 : TILE]
-        first_ref[2 * plane : 2 * plane + 2] = out_ref[plane, 0:2]
-    last_ref[6] = out_ref[4, TILE - 1]
-    first_ref[6] = out_ref[3, 0]
+        two = slice(2 * plane, 2 * plane + 2)
+        last, first = out_ref[plane, TILE - 2 : TILE], out_ref[plane, 0:2]
+        inner_ref[two] = jnp.where(even, last, first)
+        outer_ref[two] = jnp.where(even, first, last)
+    last, first = out_ref[4, TILE - 1], out_ref[3, 0]
+    inner_ref[6] = jnp.where(even, last, first)
+    outer_ref[6] = jnp.where(even, first, last)
+    copies = [
+        pltpu.make_async_copy(src, dst, out_sems.at[i])
+        for i, (src, dst) in enumerate(
+            ((inner_ref, inner_hbm), (outer_ref, outer_hbm), (out_ref, out_hbm))
+        )
+    ]
+    for copy in copies:
+        copy.start()
+    for copy in copies:
+        copy.wait()
 
 
 def split(bottom_in, skip_feat, cotangent):
-    vmem = pl.BlockSpec(memory_space=pltpu.VMEM)
-    strip = jax.ShapeDtypeStruct((7, TILE, 256), BF16)
+    anywhere = pl.BlockSpec(memory_space=pl.ANY)
+    fine = (2 * TILE, 2 * TILE, 128)
+    shapes = ((5, TILE, TILE, 256), (7, TILE, 256), (7, TILE, 256))
     return pl.pallas_call(
         split_kernel,
-        out_shape=(jax.ShapeDtypeStruct((5, TILE, TILE, 256), BF16), strip, strip),
-        in_specs=[pl.BlockSpec(memory_space=pl.ANY)] * 3,
-        out_specs=(vmem, vmem, vmem),
+        out_shape=tuple(jax.ShapeDtypeStruct(shape, BF16) for shape in shapes),
+        in_specs=[anywhere] * 3,
+        out_specs=(anywhere,) * 3,
         scratch_shapes=[
             pltpu.VMEM((TILE, TILE, 256), BF16),
-            pltpu.VMEM((2 * TILE, 2 * TILE, 128), BF16),
-            pltpu.VMEM((2 * TILE, 2 * TILE, 128), BF16),
-            pltpu.VMEM((2 * TILE, 2 * TILE, 128), F32),
-            pltpu.SemaphoreType.DMA((3,)),
-        ],
-        compiler_params=pltpu.CompilerParams(vmem_limit_bytes=16 << 20),
+            pltpu.VMEM(fine, BF16),
+            pltpu.VMEM(fine, BF16),
+            pltpu.VMEM(fine, F32),
+        ]
+        + [pltpu.VMEM(shape, BF16) for shape in shapes]
+        + [pltpu.SemaphoreType.DMA((3,)), pltpu.SemaphoreType.DMA((3,))],
+        compiler_params=pltpu.CompilerParams(vmem_limit_bytes=WHOLE),
     )(bottom_in, skip_feat, cotangent)
 
 
@@ -147,10 +167,28 @@
 
 
 def main_kernel(
-    scale, pos_ref, z_ref, up_ref, down_ref, lo_ref, hi_ref, bk_ref, uk_ref, lk_ref,
-    mix4c, pg3c, keep_ref, send_ref,
+    scale, pos_ref, z_hbm, up_hbm, down_hbm, lo_hbm, hi_hbm, bk_hbm, uk_hbm, lk_hbm,
+    mix4c_hbm, pg3c_hbm, keep_ref, send_ref,
     ext, bot3, botc, act3, actc, dsilu, cot4, mg4, mg4c, pgc, packed, sems,
+    mix4c, pg3c, z_ref, up_ref, down_ref, lo_ref, hi_ref, bk_ref, uk_ref, lk_ref, in_sems, out_sems,
 ):
+    loads = [
+        pltpu.make_async_copy(src, dst, in_sems.at[i])
+        for i, (src, dst) in enumerate(
+            (
+                (z_hbm, z_ref),
+                (up_hbm, up_ref),
+                (down_hbm, down_ref),
+                (lo_hbm, lo_ref),
+                (hi_hbm, hi_ref),
+                (bk_hbm, bk_ref),
+                (lk_hbm, lk_ref),
+                (uk_hbm, uk_ref),
+            )
+        )
+    ]
+    for copy in loads:
+        copy.start()
     row0 = pos_ref[0] * TILE
     col0 = pos_ref[1] * TILE
     image_h = pos_ref[2]
@@ -159,6 +197,8 @@
 
     core = slice(CORE, CORE + TILE)
     ext[...] = jnp.zeros_like(ext)
+    for copy in loads[:5]:
+        copy.wait()
     ext[:, 2 : 2 + TILE, core, :] = z_ref[...].astype(F32)
     for plane in range(3):
         two = slice(2 * plane, 2 * plane + 2)
@@ -192,6 +232,7 @@
         lanes = slice(256 * b, 256 * b + 256)
         bot3[:, :, lanes] = part.reshape(EXT, PITCH, 256).astype(BF16)
         botc[:, :, lanes] = core_of(part)[1 : 19].astype(BF16)
+    loads[5].wait()
     pre = jnp.zeros((18 * PITCH, 256), F32)
     for a in range(3):
         pre = pre + nn(flat(bot3[a : a + 18]), bk_ref[a].reshape(768, 256))
@@ -209,6 +250,7 @@
         cot4[par, :, :, 0:128] = a.reshape(EXT, PITCH, 128).astype(BF16)
         cot4[par, :, :, 128:384] = b.reshape(EXT, PITCH, 256).astype(BF16)
         cot4[par, :, :, 384:512] = c.reshape(EXT, PITCH, 128).astype(BF16)
+    loads[6].wait()
     for par in range(2):
         first = 1 - par
         total = jnp.zeros((19 * PITCH, 256), F32)
@@ -247,6 +289,7 @@
             put(0, (4 * a + b) * 256, prod[:, 128 * b : 128 * b + 128])
     hand_out(*parts[0], lambda copy: copy.start())
 
+    loads[7].wait()
     agrad = jnp.zeros((18 * PITCH, 256), F32)
     for a in range(4):
         src, shift = fine_row(a - 1)
@@ -256,6 +299,12 @@
     for b, part in enumerate(three(pgrad)):
         pg3c[:, :, 256 * b : 256 * b + 256] = core_of(part).astype(BF16)
     pgc[...] = flat(core_of(pgrad)[1:17]).astype(BF16)
+
+    rest = [
+        pltpu.make_async_copy(pg3c, pg3c_hbm, out_sems.at[0]),
+        pltpu.make_async_copy(mix4c, mix4c_hbm, out_sems.at[1]),
+    ]
+    rest[0].start()
 
     for a in range(3):
         prod = tn(flat(botc[a : a + 16]), pgc[...])
@@ -282,6 +331,8 @@
         mix4c[par, :, :, 128:384] = core_of(b).astype(BF16)
         mix4c[par, :, :, 384:512] = core_of(c).astype(BF16)
 
+    rest[1].start()
+
     for a in range(3):
         prod = jnp.zeros((512, 256), F32)
         for par in range(2):
@@ -302,6 +353,8 @@
         hand_out(*part, lambda copy: copy.start())
     for part in parts:
         hand_out(*part, lambda copy: copy.wait())
+    for copy in rest:
+        copy.wait()
 
 
 def rest_kernel(mix4c, pg3c, bk_ref, lk_ref, level_ref, bgrad_ref, inter):
@@ -343,18 +396,14 @@
 
 
 def local_work(scale, pos, z, up, down, lo, hi, bot_kernel, up_kernel, lvl_kernel):
-    vmem = pl.BlockSpec(memory_space=pltpu.VMEM)
     anywhere = pl.BlockSpec(memory_space=pl.ANY)
+    operands = (z, up, down, lo, hi, bot_kernel, up_kernel, lvl_kernel)
+    shapes = ((2, 18, TILE, 512), (18, TILE, 768), (HALF, 128), (HALF, 128))
     return pl.pallas_call(
         functools.partial(main_kernel, scale),
-        out_shape=(
-            jax.ShapeDtypeStruct((2, 18, TILE, 512), BF16),
-            jax.ShapeDtypeStruct((18, TILE, 768), BF16),
-            jax.ShapeDtypeStruct((HALF, 128), BF16),
-            jax.ShapeDtypeStruct((HALF, 128), BF16),
-        ),
-        in_specs=[pl.BlockSpec(memory_space=pltpu.SMEM)] + [vmem] * 8,
-        out_specs=(vmem, vmem, anywhere, anywhere),
+        out_shape=tuple(jax.ShapeDtypeStruct(shape, BF16) for shape in shapes),
+        in_specs=[pl.BlockSpec(memory_space=pltpu.SMEM)] + [anywhere] * len(operands),
+        out_specs=(anywhere,) * len(shapes),
         scratch_shapes=[
             pltpu.VMEM((5, EXT, PITCH, 256), F32),
             pltpu.VMEM((EXT, PITCH, 768), BF16),
@@ -368,64 +417,67 @@
             pltpu.VMEM((TILE * TILE, 256), BF16),
             pltpu.VMEM((2, HALF, 128), BF16),
             pltpu.SemaphoreType.DMA((4,)),
-        ],
-        compiler_params=pltpu.CompilerParams(vmem_limit_bytes=48 << 20),
-    )(pos, z, up, down, lo, hi, bot_kernel, up_kernel, lvl_kernel)
+        ]
+        + [pltpu.VMEM(shape, BF16) for shape in shapes[:2]]
+        + [pltpu.VMEM(x.shape, BF16) for x in operands]
+        + [pltpu.SemaphoreType.DMA((len(operands),)), pltpu.SemaphoreType.DMA((2,))],
+        compiler_params=pltpu.CompilerParams(vmem_limit_bytes=WHOLE),
+    )(pos, *operands)
 
 
 def unpack_kernel(
-    pos_ref, half_hbm, other_hbm, up_hbm, bot_hbm, lvl_hbm,
-    half, other, up, bot, lvl, in_sems, out_sems,
+    pos_ref, half, other, up_hbm, bot_hbm, lvl_hbm, up, bot, lvl, sems
 ):
-    ins = [
-        pltpu.make_async_copy(src, dst, in_sems.at[i])
-        for i, (src, dst) in enumerate(((half_hbm, half), (other_hbm, other)))
-    ]
-    for copy in ins:
+    copies = []
+
+    def send(src, dst):
+        copy = pltpu.make_async_copy(src, dst, sems.at[len(copies)])
         copy.start()
-    for copy in ins:
+        copies.append(copy)
+
+    own_even = pos_ref[4] == 0
+
+    def rows(parity, first, count):
+        at = slice(first, first + count)
+        mine, theirs = (half, other) if parity == 0 else (other, half)
+        return jnp.where(own_even, mine[at], theirs[at]).astype(F32)
+
+    step = 1024
+    for first in range(0, 4096, step):
+        up[first : first + step] = rows(0, first, step)
+        send(up.at[pl.ds(first, step)], up_hbm.at[pl.ds(first, step)])
+    step = 768
+    for first in range(0, 2304, step):
+        bot[first : first + step, 0:128] = rows(1, first, step)
+        bot[first : first + step, 128:256] = rows(1, 2304 + first, step)
+        send(bot.at[pl.ds(first, step)], bot_hbm.at[pl.ds(first, step)])
+    lvl[0:768] = rows(0, 4096, 768)
+    lvl[768:1152] = rows(1, 4608, 384)
+    send(lvl, lvl_hbm)
+    for copy in copies:
         copy.wait()
-    for which in range(2):
-
-        @pl.when(pos_ref[4] == which)
-        def _():
-            even, odd = (half, other) if which == 0 else (other, half)
-            up[...] = even[0:4096].astype(F32)
-            lvl[0:768] = even[4096:4864].astype(F32)
-            lvl[768:1152] = odd[4608:4992].astype(F32)
-            bot[:, 0:128] = odd[0:2304].astype(F32)
-            bot[:, 128:256] = odd[2304:4608].astype(F32)
-
-    outs = [
-        pltpu.make_async_copy(src, dst, out_sems.at[i])
-        for i, (src, dst) in enumerate(((up, up_hbm), (bot, bot_hbm), (lvl, lvl_hbm)))
-    ]
-    for copy in outs:
-        copy.start()
-    for copy in outs:
-        copy.wait()
 
 
 def unpack(pos, half, other):
+    vmem = pl.BlockSpec(memory_space=pltpu.VMEM)
     anywhere = pl.BlockSpec(memory_space=pl.ANY)
     shapes = ((4096, 128), (2304, 256), (1152, 128))
     return pl.pallas_call(
         unpack_kernel,
         out_shape=tuple(jax.ShapeDtypeStruct(shape, F32) for shape in shapes),
-        in_specs=[pl.BlockSpec(memory_space=pltpu.SMEM), anywhere, anywhere],
+        in_specs=[pl.BlockSpec(memory_space=pltpu.SMEM), vmem, vmem],
         out_specs=(anywhere,) * 3,
-        scratch_shapes=[pltpu.VMEM((HALF, 128), BF16)] * 2
-        + [pltpu.VMEM(shape, F32) for shape in shapes]
-        + [pltpu.SemaphoreType.DMA((2,)), pltpu.SemaphoreType.DMA((3,))],
+        scratch_shapes=[pltpu.VMEM(shape, F32) for shape in shapes]
+        + [pltpu.SemaphoreType.DMA((8,))],
         compiler_params=pltpu.CompilerParams(vmem_limit_bytes=16 << 20),
     )(pos, half, other)
 
 
-def shifted(last, first, axis):
-    count = lax.axis_size(axis)
-    up = [(i, i + 1) for i in range(count - 1)]
-    down = [(i + 1, i) for i in range(count - 1)]
-    return lax.ppermute(last, axis, up), lax.ppermute(first, axis, down)
+def swapped(inner, outer, axis):
+    got_inner = lax.ppermute(inner, axis, INNER_PAIRS)
+    got_outer = lax.ppermute(outer, axis, OUTER_PAIRS)
+    even = lax.rem(lax.axis_index(axis), 2) == 0
+    return jnp.where(even, got_outer, got_inner), jnp.where(even, got_inner, got_outer)
 
 
 def exchange(x):
@@ -453,8 +505,8 @@
 def on_device(bottom_in, skip_feat, cotangent, bot_kernel, up_kernel, lvl_kernel):
     rows, cols = lax.axis_size("row"), lax.axis_size("col")
     scale = 1.0 / float(2 * TILE * rows * 2 * TILE * cols) ** 0.5
-    z, last, first = split(bottom_in, skip_feat, cotangent)
-    up, down = shifted(last, first, "row")
+    z, inner, outer = split(bottom_in, skip_feat, cotangent)
+    up, down = swapped(inner, outer, "row")
 
     def side(cols, skip_col):
         parts = [
@@ -468,9 +520,10 @@
         odd = jnp.concatenate([up[6:7, skip_col], z[4, :, skip_col], blank], axis=0)
         return jnp.concatenate(parts + [jnp.concatenate([even, odd], axis=1)], axis=0)
 
-    lo, hi = shifted(
-        side(slice(TILE - 2, TILE), slice(TILE - 1, TILE)), side(slice(0, 2), slice(0, 1)), "col"
-    )
+    last = side(slice(TILE - 2, TILE), slice(TILE - 1, TILE))
+    first = side(slice(0, 2), slice(0, 1))
+    even = lax.rem(lax.axis_index("col"), 2) == 0
+    lo, hi = swapped(jnp.where(even, last, first), jnp.where(even, first, last), "col")
     row = lax.axis_index("row")
     pos = jnp.stack(
         [row, lax.axis_index("col"), jnp.int32(TILE * rows), jnp.int32(TILE * cols), row % 2]

time: 118 us -> 112 us (0.949)
  waiting for transfers between devices: 17.1 us -> 9.13 us
  Pallas kernels: 14.4 us -> 18.4 us
  starting transfers between devices: 23.6 us -> 21 us
  local copies, waits for them, and re-layouts: 5.53 us -> 4.03 us
  other arithmetic: 2.35 us -> 3.76 us
    ppermute x4, waiting for transfers between devices: 7.26 us -> 2.67 us  [the longest x2 1.73 us: swapped(): got_inner = lax.ppermute(inner, axis, INNER_PAIRS)]
    pallas_call x2, Pallas kernels: 9.26 us -> 13.8 us  [the longest x1 11.7 us: local_work(): pl.pallas_call(functools.partial(main_kernel, scale), out_shape=tuple((ja...]
    ppermute x4, starting transfers between devices: 10.9 us -> 6.64 us  [the longest x2 5.16 us: swapped(): got_outer = lax.ppermute(outer, axis, OUTER_PAIRS)]
    ppermute x3, waiting for transfers between devices: 5.61 us -> 2.64 us  [total_over_devices(): planes = [lax.ppermute(part, AXES, depth_shift(step)) for step in (2, 6, 4)]]
    unnamed x23, local copies, waits for them, and re-layouts: 5.28 us -> 2.86 us
    convert_element_type x1, other arithmetic: 0.34 us -> 1.66 us  [total_over_devices(): half = (keep.astype(F32) + got.astype(F32)).astype(BF16)]
  transfers between devices with their start and end apart: 9 -> 9, of which waited for: 6 -> 6; matrix products, arithmetic and copies ran while one was open for 0% -> 1% of each run, Pallas kernels for 1% -> 2%
where the time goes in v3:
time: 112 us; the launch traced here: 111 us
  blocking collectives  53.9 us (48%)
  starting transfers between devices  21 us (19%)
  Pallas kernels  18.4 us (16%)
  waiting for transfers between devices  9.13 us (8%)
  local copies, waits for them, and re-layouts  4.03 us (4%)
  other arithmetic  3.76 us (3%)
    all_to_all x2, blocking collectives, exchange(): return lax.all_to_all(x, AXES, 0, 0, axis_index_groups=BLOCK_GROUPS)  53.9 us
    pallas_call x1, Pallas kernels, local_work(): pl.pallas_call(functools.partial(main_kernel, scale), out_shape=tuple((ja...  11.7 us
    ppermute x3, starting transfers between devices, total_over_devices(): planes = [lax.ppermute(part, AXES, depth_shift(step)) for step in (2, 6, 4)]  9.21 us
    ppermute x2, starting transfers between devices, swapped(): got_outer = lax.ppermute(outer, axis, OUTER_PAIRS)  5.16 us
    ppermute x1, starting transfers between devices, total_over_devices(): return (half, lax.ppermute(half, 'row', CORE_SWAP))  4.56 us
    pallas_call x1, Pallas kernels, unpack(): pl.pallas_call(unpack_kernel, out_shape=tuple((jax.ShapeDtypeStruct(shape...  2.95 us
    ppermute x1, waiting for transfers between devices, total_over_devices(): got = lax.ppermute(send, 'row', CORE_SWAP)  2.87 us
    unnamed x23, local copies, waits for them, and re-layouts  2.86 us
  transfers between devices with their start and end apart: 9, of which 6 were waited for; matrix products, arithmetic and copies ran while one was open for 1% of the time, Pallas kernels for 2%

profile of v3, /device:TPU:1, one launch (start us, length us, event | category | flops | bytes accessed | tf_op | source)
XLA Modules:
  0.0 111.2 jit_solution(9232785886347896924)
XLA Ops:
  0.6 2.1 %shard_map.101 = (bf16[5,16,16,256]{3,2,1,0:T(8,128)(2,1)}, bf16[7,16,256]{2,1,0:T(8,128)(2,1)}, bf16[7,16,256]{2,1,0:T(8,128)(2,1)}) custom-call(bf16[16,16,256]{2,1,0:T(8,128)(2,1)} %bot_hbm.1, bf16[32,32,128]{2,1,0:T(8,128)(2,1)} %skip_hbm.1, bf16[32,32,128]{2,1,0:T(8,128)(2,1)} %cot_hbm.1), custom_call_target="tpu_custom_call" | custom-call | tf_op jit(solution)/shard_map/pallas_call | solution.py:99
  2.7 4.5 %collective-permute-start = (bf16[7,16,256]{2,1,0:T(8,128)(2,1)}, bf16[7,16,256]{2,1,0:T(8,128)(2,1)S(1)}, u32[]{:S(2)}, u32[]{:S(2)}) collective-permute-start(bf16[7,16,256]{2,1,0:T(8,128)(2,1)} %get-tuple-element.18), channel_id=1, source_target_pairs={{16,32},{32,16},{48,64},{64,48},{80,96},{96,80},{112,128},{128,112... | collective-permute-start | bytes 172040 | tf_op jit(solution)/shard_map/ppermute | solution.py:478
  7.3 1.0 slice_bitcast_fusion.1
  8.3 0.9 collective-permute-done
  9.3 0.9 constant_dynamic-update-slice_fusion.18
  10.3 0.9 constant_dynamic-update-slice_fusion.15
  11.2 0.9 constant_dynamic-update-slice_fusion.12
  12.6 1.4 %collective-permute-start.3 = (bf16[78,2,256]{2,1,0:T(2,128)(2,1)S(1)}, bf16[78,2,256]{2,1,0:T(2,128)(2,1)S(1)}, u32[]{:S(2)}, u32[]{:S(2)}) collective-permute-start(bf16[78,2,256]{2,1,0:T(2,128)(2,1)S(1)} %get-tuple-element.41), channel_id=1, source_target_pairs={{0,1},{1,0},{2,3},{3,2},{4,5},{5,4},{6,7},{7,6},{8,9},{9,8},{10,11... | collective-permute-start | bytes 239624 | tf_op jit(solution)/shard_map/ppermute | solution.py:477
  13.9 0.7 collective-permute-start.2
  15.2 1.7 %collective-permute-done.3 = bf16[78,2,256]{2,1,0:T(2,128)(2,1)S(1)} collective-permute-done((bf16[78,2,256]{2,1,0:T(2,128)(2,1)S(1)}, bf16[78,2,256]{2,1,0:T(2,128)(2,1)S(1)}, u32[]{:S(2)}, u32[]{:S(2)}) %collective-permute-start.3) | collective-permute-done | bytes 79904 | tf_op jit(solution)/shard_map/ppermute | solution.py:477
  17.0 0.8 broadcast_select_fusion
  17.8 11.7 %shard_map.102 = (bf16[2,18,16,512]{3,2,1,0:T(8,128)(2,1)}, bf16[18,16,768]{2,1,0:T(8,128)(2,1)}, bf16[5120,128]{1,0:T(8,128)(2,1)}, bf16[5120,128]{1,0:T(8,128)(2,1)}) custom-call(s32[5]{0:T(128)} %pad_add_fusion.pos_ref, bf16[5,16,16,256]{3,2,1,0:T(8,128)(2,1)} %get-tuple-element.17.z_hbm, bf16[7,16,256]{2,1,0:T(8,128)(2,1)} %copy-done.6, ...), custom_call_target="tpu_custom_call" | custom-call | tf_op jit(solution)/shard_map/pallas_call | solution.py:402
  30.1 2.9 %collective-permute-done.4 = bf16[5120,128]{1,0:T(8,128)(2,1)S(1)} collective-permute-done((bf16[5120,128]{1,0:T(8,128)(2,1)}, bf16[5120,128]{1,0:T(8,128)(2,1)S(1)}, u32[]{:S(2)}, u32[]{:S(2)}) %collective-permute-start.4) | collective-permute-done | bytes 1310752 | tf_op jit(solution)/shard_map/ppermute | solution.py:488
  33.0 1.7 %add_convert_fusion = bf16[5120,128]{1,0:T(8,128)(2,1)S(1)} fusion(bf16[5120,128]{1,0:T(8,128)(2,1)S(1)} %collective-permute-done.4, bf16[5120,128]{1,0:T(8,128)(2,1)} %get-tuple-element.24), kind=kLoop, calls=%fused_computation | loop fusion | flops 2621440 | bytes 3932160 | tf_op jit(solution)/shard_map/convert_element_type | solution.py:489
  34.6 32.7 %all_to_all.10 = bf16[32,160,128]{2,1,0:T(8,128)(2,1)S(1)} all-to-all(bf16[32,160,128]{2,1,0:T(8,128)(2,1)S(1)} %bitcast.30), channel_id=1, replica_groups={{0,1,128,129,32,33,160,161,64,65,192,193,96,97,224,225,2,3,130,131,34,3..., dimensions={0} | all-to-all | bytes 2621440 | tf_op jit(solution)/shard_map/all_to_all | solution.py:484
  67.5 6.8 %collective-permute-start.7 = (bf16[160,128]{1,0:T(8,128)(2,1)S(1)}, bf16[160,128]{1,0:T(8,128)(2,1)S(1)}, u32[]{:S(2)}, u32[]{:S(2)}) collective-permute-start(bf16[160,128]{1,0:T(8,128)(2,1)S(1)} %reduce_sum.12), channel_id=1, source_target_pairs={{0,8},{1,9},{2,10},{3,11},{4,12},{5,13},{6,14},{7,15},{8,0},{9,1},... | collective-permute-start | bytes 122888 | tf_op jit(solution)/shard_map/ppermute | solution.py:492
  74.4 2.4 %collective-permute-start.5 = (bf16[160,128]{1,0:T(8,128)(2,1)S(1)}, bf16[160,128]{1,0:T(8,128)(2,1)S(1)}, u32[]{:S(2)}, u32[]{:S(2)}) collective-permute-start(bf16[160,128]{1,0:T(8,128)(2,1)S(1)} %reduce_sum.12), channel_id=1, source_target_pairs={{0,4},{1,5},{2,6},{3,7},{4,8},{5,9},{6,10},{7,11},{8,12},{9,13},{1... | collective-permute-start | bytes 122888 | tf_op jit(solution)/shard_map/ppermute | solution.py:492
  76.8 1.8 %collective-permute-done.6 = bf16[160,128]{1,0:T(8,128)(2,1)S(1)} collective-permute-done((bf16[160,128]{1,0:T(8,128)(2,1)S(1)}, bf16[160,128]{1,0:T(8,128)(2,1)S(1)}, u32[]{:S(2)}, u32[]{:S(2)}) %collective-permute-start.6) | collective-permute-done | bytes 40992 | tf_op jit(solution)/shard_map/ppermute | solution.py:492
  78.5 0.9 collective-permute-done.5
  79.7 21.2 %all_to_all.11 = bf16[32,160,128]{2,1,0:T(8,128)(2,1)S(1)} all-to-all(bf16[32,160,128]{2,1,0:T(8,128)(2,1)S(1)} %broadcast_in_dim.26), channel_id=1, replica_groups={{0,1,128,129,32,33,160,161,64,65,192,193,96,97,224,225,2,3,130,131,34,3..., dimensions={0} | all-to-all | bytes 2621440 | tf_op jit(solution)/shard_map/all_to_all | solution.py:484
  100.9 4.6 %collective-permute-start.8 = (bf16[5120,128]{1,0:T(8,128)(2,1)S(1)}, bf16[5120,128]{1,0:T(8,128)(2,1)S(1)}, u32[]{:S(2)}, u32[]{:S(2)}) collective-permute-start(bf16[5120,128]{1,0:T(8,128)(2,1)S(1)} %bitcast.28), channel_id=1, source_target_pairs={{0,16},{16,0},{32,48},{48,32},{64,80},{80,64},{96,112},{112,96},{1... | collective-permute-start | bytes 3932168 | tf_op jit(solution)/shard_map/ppermute | solution.py:502
  105.5 1.7 %shard_map.103 = (bf16[32,32,128]{2,1,0:T(8,128)(2,1)}, bf16[16,16,256]{2,1,0:T(8,128)(2,1)}) custom-call(bf16[2,18,16,512]{3,2,1,0:T(8,128)(2,1)S(1)} %copy-done.3, bf16[18,16,768]{2,1,0:T(8,128)(2,1)S(1)} %copy-done.4, bf16[3,3,256,256]{3,2,1,0:T(8,128)(2,1)S(1)} %copy-done, bf16[3,3,128,128]{3,2,1,0:T(8,128)(2,1)S(1)} %copy-done.1), custom_call_target="tpu_custom_call" | custom-call | flops 1000000000 | bytes 3000000 | tf_op jit(solution)/shard_map/pallas_call | solution.py:384
  107.2 0.9 collective-permute-done.8.other
  108.1 2.9 %shard_map.104 = (f32[4096,128]{1,0:T(8,128)}, f32[2304,256]{1,0:T(8,128)}, f32[1152,128]{1,0:T(8,128)}) custom-call(s32[5]{0:T(128)S(1)} %copy-done.2, bf16[5120,128]{1,0:T(8,128)(2,1)S(1)} %bitcast.29, bf16[5120,128]{1,0:T(8,128)(2,1)S(1)} %collective-permute-done.8.other), custom_call_target="tpu_custom_call" | custom-call | tf_op jit(solution)/shard_map/pallas_call | solution.py:465
  (38 shorter events, 2.3 us)
Async XLA Ops:
  2.7 6.6 %collective-permute-start = (bf16[7,16,256]{2,1,0:T(8,128)(2,1)}, bf16[7,16,256]{2,1,0:T(8,128)(2,1)S(1)}, u32[]{:S(2)}, u32[]{:S(2)}) collective-permute-start(bf16[7,16,256]{2,1,0:T(8,128)(2,1)} %get-tuple-element.18), channel_id=1, source_target_pairs={{16,32},{32,16},{48,64},{64,48},{80,96},{96,80},{112,128},{128,112... | collective-permute-start | bytes 172040 | tf_op jit(solution)/shard_map/ppermute | solution.py:478
  7.2 2.1 %collective-permute-start.1 = (bf16[7,16,256]{2,1,0:T(8,128)(2,1)}, bf16[7,16,256]{2,1,0:T(8,128)(2,1)S(1)}, u32[]{:S(2)}, u32[]{:S(2)}) collective-permute-start(bf16[7,16,256]{2,1,0:T(8,128)(2,1)} %get-tuple-element.19), channel_id=1, source_target_pairs={{0,16},{16,0},{32,48},{48,32},{64,80},{80,64},{96,112},{112,96},{1... | collective-permute-start | bytes 172040 | tf_op jit(solution)/shard_map/ppermute | solution.py:477
  9.3 8.5 %copy-start.5 = (bf16[7,16,256]{2,1,0:T(8,128)(2,1)}, bf16[7,16,256]{2,1,0:T(8,128)(2,1)S(1)}, u32[]{:S(2)}) copy-start(bf16[7,16,256]{2,1,0:T(8,128)(2,1)S(1)} %get-tuple-element.43.down_hbm) | copy-start | bytes 172036
  9.3 8.5 %copy-start.6 = (bf16[7,16,256]{2,1,0:T(8,128)(2,1)}, bf16[7,16,256]{2,1,0:T(8,128)(2,1)S(1)}, u32[]{:S(2)}) copy-start(bf16[7,16,256]{2,1,0:T(8,128)(2,1)S(1)} %get-tuple-element.44.up_hbm) | copy-start | bytes 172036
  12.6 4.4 %collective-permute-start.3 = (bf16[78,2,256]{2,1,0:T(2,128)(2,1)S(1)}, bf16[78,2,256]{2,1,0:T(2,128)(2,1)S(1)}, u32[]{:S(2)}, u32[]{:S(2)}) collective-permute-start(bf16[78,2,256]{2,1,0:T(2,128)(2,1)S(1)} %get-tuple-element.41), channel_id=1, source_target_pairs={{0,1},{1,0},{2,3},{3,2},{4,5},{5,4},{6,7},{7,6},{8,9},{9,8},{10,11... | collective-permute-start | bytes 239624 | tf_op jit(solution)/shard_map/ppermute | solution.py:477
  13.9 3.0 %collective-permute-start.2 = (bf16[78,2,256]{2,1,0:T(2,128)(2,1)S(1)}, bf16[78,2,256]{2,1,0:T(2,128)(2,1)S(1)}, u32[]{:S(2)}, u32[]{:S(2)}) collective-permute-start(bf16[78,2,256]{2,1,0:T(2,128)(2,1)S(1)} %get-tuple-element.42), channel_id=1, source_target_pairs={{1,2},{2,1},{3,4},{4,3},{5,6},{6,5},{7,8},{8,7},{9,10},{10,9},{11,... | collective-permute-start | bytes 239624 | tf_op jit(solution)/shard_map/ppermute | solution.py:478
  29.5 3.5 %collective-permute-start.4 = (bf16[5120,128]{1,0:T(8,128)(2,1)}, bf16[5120,128]{1,0:T(8,128)(2,1)S(1)}, u32[]{:S(2)}, u32[]{:S(2)}) collective-permute-start(bf16[5120,128]{1,0:T(8,128)(2,1)} %get-tuple-element.25), channel_id=1, source_target_pairs={{0,16},{16,0},{32,48},{48,32},{64,80},{80,64},{96,112},{112,96},{1... | collective-permute-start | bytes 3932168 | tf_op jit(solution)/shard_map/ppermute | solution.py:488
  67.5 9.2 %collective-permute-start.7 = (bf16[160,128]{1,0:T(8,128)(2,1)S(1)}, bf16[160,128]{1,0:T(8,128)(2,1)S(1)}, u32[]{:S(2)}, u32[]{:S(2)}) collective-permute-start(bf16[160,128]{1,0:T(8,128)(2,1)S(1)} %reduce_sum.12), channel_id=1, source_target_pairs={{0,8},{1,9},{2,10},{3,11},{4,12},{5,13},{6,14},{7,15},{8,0},{9,1},... | collective-permute-start | bytes 122888 | tf_op jit(solution)/shard_map/ppermute | solution.py:492
  74.4 4.1 %collective-permute-start.6 = (bf16[160,128]{1,0:T(8,128)(2,1)S(1)}, bf16[160,128]{1,0:T(8,128)(2,1)S(1)}, u32[]{:S(2)}, u32[]{:S(2)}) collective-permute-start(bf16[160,128]{1,0:T(8,128)(2,1)S(1)} %reduce_sum.12), channel_id=1, source_target_pairs={{0,12},{1,13},{2,14},{3,15},{4,0},{5,1},{6,2},{7,3},{8,4},{9,5},{1... | collective-permute-start | bytes 122888 | tf_op jit(solution)/shard_map/ppermute | solution.py:492
  74.4 5.0 %collective-permute-start.5 = (bf16[160,128]{1,0:T(8,128)(2,1)S(1)}, bf16[160,128]{1,0:T(8,128)(2,1)S(1)}, u32[]{:S(2)}, u32[]{:S(2)}) collective-permute-start(bf16[160,128]{1,0:T(8,128)(2,1)S(1)} %reduce_sum.12), channel_id=1, source_target_pairs={{0,4},{1,5},{2,6},{3,7},{4,8},{5,9},{6,10},{7,11},{8,12},{9,13},{1... | collective-permute-start | bytes 122888 | tf_op jit(solution)/shard_map/ppermute | solution.py:492
  79.7 25.8 %copy-start = (bf16[3,3,256,256]{3,2,1,0:T(8,128)(2,1)S(1)}, bf16[3,3,256,256]{3,2,1,0:T(8,128)(2,1)}, u32[]{:S(2)}) copy-start(bf16[3,3,256,256]{3,2,1,0:T(8,128)(2,1)} %bk_ref.1) | copy-start | bytes 3538948
  79.7 25.8 %copy-start.1 = (bf16[3,3,128,128]{3,2,1,0:T(8,128)(2,1)S(1)}, bf16[3,3,128,128]{3,2,1,0:T(8,128)(2,1)}, u32[]{:S(2)}) copy-start(bf16[3,3,128,128]{3,2,1,0:T(8,128)(2,1)} %lk_ref.1) | copy-start | bytes 884740
  79.7 25.8 %copy-start.3 = (bf16[2,18,16,512]{3,2,1,0:T(8,128)(2,1)S(1)}, bf16[2,18,16,512]{3,2,1,0:T(8,128)(2,1)}, u32[]{:S(2)}) copy-start(bf16[2,18,16,512]{3,2,1,0:T(8,128)(2,1)} %get-tuple-element.20.mix4c) | copy-start | bytes 1769476
  79.7 25.8 %copy-start.4 = (bf16[18,16,768]{2,1,0:T(8,128)(2,1)S(1)}, bf16[18,16,768]{2,1,0:T(8,128)(2,1)}, u32[]{:S(2)}) copy-start(bf16[18,16,768]{2,1,0:T(8,128)(2,1)} %get-tuple-element.21.pg3c) | copy-start | bytes 1327108
  100.9 7.2 %collective-permute-start.8 = (bf16[5120,128]{1,0:T(8,128)(2,1)S(1)}, bf16[5120,128]{1,0:T(8,128)(2,1)S(1)}, u32[]{:S(2)}, u32[]{:S(2)}) collective-permute-start(bf16[5120,128]{1,0:T(8,128)(2,1)S(1)} %bitcast.28), channel_id=1, source_target_pairs={{0,16},{16,0},{32,48},{48,32},{64,80},{80,64},{96,112},{112,96},{1... | collective-permute-start | bytes 3932168 | tf_op jit(solution)/shard_map/ppermute | solution.py:502
  105.5 2.7 %copy-start.2 = (s32[5]{0:T(128)S(1)}, s32[5]{0:T(128)}, u32[]{:S(2)}) copy-start(s32[5]{0:T(128)} %pad_add_fusion.pos_ref) | copy-start | bytes 64

commit v4 on v2

--- a/solution.py
+++ b/solution.py
@@ -14,6 +14,7 @@
 EXT = TILE + 4
 PITCH = 32
 CORE = 8
+MAIN_LIMIT = 40 << 20
 HALF = 5120
 
 
@@ -45,19 +46,13 @@
 
 
 CORE_SWAP = [(i, i ^ 1) for i in range(16)]
-
-
-def split_kernel(
-    bot_hbm, skip_hbm, cot_hbm, out_ref, last_ref, first_ref, bot, skip, cot, wide, sems
-):
-    copies = [
-        pltpu.make_async_copy(src, dst, sems.at[i])
-        for i, (src, dst) in enumerate(((cot_hbm, cot), (skip_hbm, skip), (bot_hbm, bot)))
-    ]
-    for copy in copies:
-        copy.start()
-    for plane, ref, copy in ((1, cot, copies[0]), (3, skip, copies[1])):
-        copy.wait()
+INNER_PAIRS = CORE_SWAP
+OUTER_PAIRS = [pair for i in range(1, 15, 2) for pair in ((i, i + 1), (i + 1, i))]
+
+
+def split_kernel(bot, skip, cot, out_ref, inner_ref, outer_ref, wide):
+    even = lax.rem(lax.axis_index("row"), 2) == 0
+    for plane, ref in ((1, cot), (3, skip)):
         wide[...] = ref[...].astype(F32)
         for col_par in range(2):
             part = wide[:, pl.ds(col_par, TILE, stride=2), :].astype(BF16)
@@ -65,30 +60,26 @@
             lanes = slice(col_par * 128, col_par * 128 + 128)
             out_ref[plane, :, :, lanes] = part[:, 0]
             out_ref[plane + 1, :, :, lanes] = part[:, 1]
-    copies[2].wait()
     out_ref[0] = bot[...]
     for plane in range(3):
-        last_ref[2 * plane : 2 * plane + 2] = out_ref[plane, TILE - 2 : TILE]
-        first_ref[2 * plane : 2 * plane + 2] = out_ref[plane, 0:2]
-    last_ref[6] = out_ref[4, TILE - 1]
-    first_ref[6] = out_ref[3, 0]
+        two = slice(2 * plane, 2 * plane + 2)
+        last, first = out_ref[plane, TILE - 2 : TILE], out_ref[plane, 0:2]
+        inner_ref[two] = jnp.where(even, last, first)
+        outer_ref[two] = jnp.where(even, first, last)
+    last, first = out_ref[4, TILE - 1], out_ref[3, 0]
+    inner_ref[6] = jnp.where(even, last, first)
+    outer_ref[6] = jnp.where(even, first, last)
 
 
 def split(bottom_in, skip_feat, cotangent):
     vmem = pl.BlockSpec(memory_space=pltpu.VMEM)
-    strip = jax.ShapeDtypeStruct((7, TILE, 256), BF16)
+    shapes = ((5, TILE, TILE, 256), (7, TILE, 256), (7, TILE, 256))
     return pl.pallas_call(
         split_kernel,
-        out_shape=(jax.ShapeDtypeStruct((5, TILE, TILE, 256), BF16), strip, strip),
-        in_specs=[pl.BlockSpec(memory_space=pl.ANY)] * 3,
-        out_specs=(vmem, vmem, vmem),
-        scratch_shapes=[
-            pltpu.VMEM((TILE, TILE, 256), BF16),
-            pltpu.VMEM((2 * TILE, 2 * TILE, 128), BF16),
-            pltpu.VMEM((2 * TILE, 2 * TILE, 128), BF16),
-            pltpu.VMEM((2 * TILE, 2 * TILE, 128), F32),
-            pltpu.SemaphoreType.DMA((3,)),
-        ],
+        out_shape=tuple(jax.ShapeDtypeStruct(shape, BF16) for shape in shapes),
+        in_specs=[vmem] * 3,
+        out_specs=(vmem,) * 3,
+        scratch_shapes=[pltpu.VMEM((2 * TILE, 2 * TILE, 128), F32)],
         compiler_params=pltpu.CompilerParams(vmem_limit_bytes=16 << 20),
     )(bottom_in, skip_feat, cotangent)
 
@@ -147,7 +138,7 @@
 
 
 def main_kernel(
-    scale, pos_ref, z_ref, up_ref, down_ref, lo_ref, hi_ref, bk_ref, uk_ref, lk_ref,
+    scale, pos_ref, z_ref, up_ref, down_ref, lo_ref, hi_ref, bk_ref, uk_ref, flip_ref,
     mix4c, pg3c, keep_ref, send_ref,
     ext, bot3, botc, act3, actc, dsilu, cot4, mg4, mg4c, pgc, packed, sems,
 ):
@@ -214,7 +205,7 @@
         total = jnp.zeros((19 * PITCH, 256), F32)
         for a in range(3):
             src, shift = fine_row(par + a - 1)
-            weight = pair_weight_back([lk_ref[2 - a, 2 - b] for b in range(3)], zero)
+            weight = pair_weight_back([flip_ref[a, b] for b in range(3)], zero)
             total = total + nt(flat(cot4[src, first + shift : first + shift + 19]), weight)
         grad = masked(total.astype(BF16).astype(F32), first)
         a, b, c = four(grad)
@@ -342,18 +333,14 @@
     )(mix4c, pg3c, bot_kernel, lvl_kernel)
 
 
-def local_work(scale, pos, z, up, down, lo, hi, bot_kernel, up_kernel, lvl_kernel):
+def local_work(scale, pos, *operands):
     vmem = pl.BlockSpec(memory_space=pltpu.VMEM)
     anywhere = pl.BlockSpec(memory_space=pl.ANY)
+    shapes = ((2, 18, TILE, 512), (18, TILE, 768), (HALF, 128), (HALF, 128))
     return pl.pallas_call(
         functools.partial(main_kernel, scale),
-        out_shape=(
-            jax.ShapeDtypeStruct((2, 18, TILE, 512), BF16),
-            jax.ShapeDtypeStruct((18, TILE, 768), BF16),
-            jax.ShapeDtypeStruct((HALF, 128), BF16),
-            jax.ShapeDtypeStruct((HALF, 128), BF16),
-        ),
-        in_specs=[pl.BlockSpec(memory_space=pltpu.SMEM)] + [vmem] * 8,
+        out_shape=tuple(jax.ShapeDtypeStruct(shape, BF16) for shape in shapes),
+        in_specs=[pl.BlockSpec(memory_space=pltpu.SMEM)] + [vmem] * len(operands),
         out_specs=(vmem, vmem, anywhere, anywhere),
         scratch_shapes=[
             pltpu.VMEM((5, EXT, PITCH, 256), F32),
@@ -369,74 +356,79 @@
             pltpu.VMEM((2, HALF, 128), BF16),
             pltpu.SemaphoreType.DMA((4,)),
         ],
-        compiler_params=pltpu.CompilerParams(vmem_limit_bytes=48 << 20),
-    )(pos, z, up, down, lo, hi, bot_kernel, up_kernel, lvl_kernel)
-
-
-def unpack_kernel(
-    pos_ref, half_hbm, other_hbm, up_hbm, bot_hbm, lvl_hbm,
-    half, other, up, bot, lvl, in_sems, out_sems,
-):
-    ins = [
-        pltpu.make_async_copy(src, dst, in_sems.at[i])
-        for i, (src, dst) in enumerate(((half_hbm, half), (other_hbm, other)))
-    ]
-    for copy in ins:
-        copy.start()
-    for copy in ins:
-        copy.wait()
-    for which in range(2):
-
-        @pl.when(pos_ref[4] == which)
-        def _():
-            even, odd = (half, other) if which == 0 else (other, half)
-            up[...] = even[0:4096].astype(F32)
-            lvl[0:768] = even[4096:4864].astype(F32)
-            lvl[768:1152] = odd[4608:4992].astype(F32)
-            bot[:, 0:128] = odd[0:2304].astype(F32)
-            bot[:, 128:256] = odd[2304:4608].astype(F32)
-
-    outs = [
-        pltpu.make_async_copy(src, dst, out_sems.at[i])
-        for i, (src, dst) in enumerate(((up, up_hbm), (bot, bot_hbm), (lvl, lvl_hbm)))
-    ]
-    for copy in outs:
-        copy.start()
-    for copy in outs:
-        copy.wait()
-
-
-def unpack(pos, half, other):
+        compiler_params=pltpu.CompilerParams(vmem_limit_bytes=MAIN_LIMIT),
+    )(pos, *operands)
+
+
+def unpack_kernel(half_of, pos_ref, half, *refs):
+    up_hbm, bot_hbm, lvl_hbm, up, bot, lvl, sems = refs[-7:]
+
+    @pl.when(pos_ref[4] == half_of)
+    def _():
+        copies = []
+        for i in range(4):
+            rows = pl.ds(1024 * i, 1024)
+            up[rows] = half[rows].astype(F32)
+            copies.append(pltpu.make_async_copy(up.at[rows], up_hbm.at[rows], sems.at[i]))
+            copies[-1].start()
+        rows = pl.ds(0, 768)
+        lvl[rows] = half[4096:4864].astype(F32)
+        copies.append(pltpu.make_async_copy(lvl.at[rows], lvl_hbm.at[rows], sems.at[4]))
+        copies[-1].start()
+        for copy in copies:
+            copy.wait()
+
+    @pl.when(pos_ref[4] != half_of)
+    def _():
+        copies = []
+        for i in range(3):
+            rows = pl.ds(768 * i, 768)
+            bot[rows, 0:128] = half[768 * i : 768 * i + 768].astype(F32)
+            bot[rows, 128:256] = half[2304 + 768 * i : 3072 + 768 * i].astype(F32)
+            copies.append(pltpu.make_async_copy(bot.at[rows], bot_hbm.at[rows], sems.at[i]))
+            copies[-1].start()
+        rows = pl.ds(768, 384)
+        lvl[rows] = half[4608:4992].astype(F32)
+        copies.append(pltpu.make_async_copy(lvl.at[rows], lvl_hbm.at[rows], sems.at[3]))
+        copies[-1].start()
+        for copy in copies:
+            copy.wait()
+
+
+def unpack(pos, half, begun=()):
+    vmem = pl.BlockSpec(memory_space=pltpu.VMEM)
     anywhere = pl.BlockSpec(memory_space=pl.ANY)
     shapes = ((4096, 128), (2304, 256), (1152, 128))
     return pl.pallas_call(
-        unpack_kernel,
+        functools.partial(unpack_kernel, 1 if begun else 0),
         out_shape=tuple(jax.ShapeDtypeStruct(shape, F32) for shape in shapes),
-        in_specs=[pl.BlockSpec(memory_space=pltpu.SMEM), anywhere, anywhere],
+        in_specs=[pl.BlockSpec(memory_space=pltpu.SMEM), vmem] + [anywhere] * len(begun),
         out_specs=(anywhere,) * 3,
-        scratch_shapes=[pltpu.VMEM((HALF, 128), BF16)] * 2
-        + [pltpu.VMEM(shape, F32) for shape in shapes]
-        + [pltpu.SemaphoreType.DMA((2,)), pltpu.SemaphoreType.DMA((3,))],
+        scratch_shapes=[pltpu.VMEM(shape, F32) for shape in shapes]
+        + [pltpu.SemaphoreType.DMA((5,))],
+        input_output_aliases={2 + i: i for i in range(len(begun))},
         compiler_params=pltpu.CompilerParams(vmem_limit_bytes=16 << 20),
-    )(pos, half, other)
-
-
-def shifted(last, first, axis):
-    count = lax.axis_size(axis)
-    up = [(i, i + 1) for i in range(count - 1)]
-    down = [(i + 1, i) for i in range(count - 1)]
-    return lax.ppermute(last, axis, up), lax.ppermute(first, axis, down)
+        cost_estimate=pl.CostEstimate(flops=0, bytes_accessed=4000000, transcendentals=0),
+    )(pos, half, *begun)
+
+
+def swapped(inner, outer, axis):
+    got_inner = lax.ppermute(inner, axis, INNER_PAIRS)
+    got_outer = lax.ppermute(outer, axis, OUTER_PAIRS)
+    even = lax.rem(lax.axis_index(axis), 2) == 0
+    return jnp.where(even, got_outer, got_inner), jnp.where(even, got_inner, got_outer)
 
 
 def exchange(x):
     return lax.all_to_all(x, AXES, 0, 0, axis_index_groups=BLOCK_GROUPS)
 
 
-def total_over_devices(keep, send):
+def total_over_devices(keep, send, rest):
     got = lax.ppermute(send, "row", CORE_SWAP)
     half = (keep.astype(F32) + got.astype(F32)).astype(BF16)
     parts = exchange(half.reshape(BLOCK, HALF // BLOCK, 128))
     part = jnp.sum(parts.astype(F32), axis=0).astype(BF16)
+    part, rest = lax.optimization_barrier((part, rest))
     planes = [lax.ppermute(part, AXES, depth_shift(step)) for step in (2, 6, 4)]
     pair = lax.axis_index("col") // 4
     terms = [part] + planes
@@ -447,14 +439,14 @@
             total = total + jnp.where(where == slot, term.astype(F32), 0.0)
     total = total.astype(BF16)
     half = exchange(jnp.broadcast_to(total[None], parts.shape)).reshape(HALF, 128)
-    return half, lax.ppermute(half, "row", CORE_SWAP)
+    return half, lax.ppermute(half, "row", CORE_SWAP), rest
 
 
 def on_device(bottom_in, skip_feat, cotangent, bot_kernel, up_kernel, lvl_kernel):
     rows, cols = lax.axis_size("row"), lax.axis_size("col")
     scale = 1.0 / float(2 * TILE * rows * 2 * TILE * cols) ** 0.5
-    z, last, first = split(bottom_in, skip_feat, cotangent)
-    up, down = shifted(last, first, "row")
+    z, inner, outer = split(bottom_in, skip_feat, cotangent)
+    up, down = swapped(inner, outer, "row")
 
     def side(cols, skip_col):
         parts = [
@@ -468,18 +460,21 @@
         odd = jnp.concatenate([up[6:7, skip_col], z[4, :, skip_col], blank], axis=0)
         return jnp.concatenate(parts + [jnp.concatenate([even, odd], axis=1)], axis=0)
 
-    lo, hi = shifted(
-        side(slice(TILE - 2, TILE), slice(TILE - 1, TILE)), side(slice(0, 2), slice(0, 1)), "col"
-    )
+    last = side(slice(TILE - 2, TILE), slice(TILE - 1, TILE))
+    first = side(slice(0, 2), slice(0, 1))
+    even = lax.rem(lax.axis_index("col"), 2) == 0
+    lo, hi = swapped(jnp.where(even, last, first), jnp.where(even, first, last), "col")
     row = lax.axis_index("row")
     pos = jnp.stack(
         [row, lax.axis_index("col"), jnp.int32(TILE * rows), jnp.int32(TILE * cols), row % 2]
     ).astype(jnp.int32)
+    flip = lvl_kernel[::-1, ::-1]
     mix4c, pg3c, keep, send = local_work(
-        scale, pos, z, up, down, lo, hi, bot_kernel, up_kernel, lvl_kernel
+        scale, pos, z, up, down, lo, hi, bot_kernel, up_kernel, flip
     )
-    level_out, bottom_grad = rest_work(mix4c, pg3c, bot_kernel, lvl_kernel)
-    up_grad, bot_grad, lvl_grad = unpack(pos, *total_over_devices(keep, send))
+    rest = rest_work(mix4c, pg3c, bot_kernel, lvl_kernel)
+    half, other, (level_out, bottom_grad) = total_over_devices(keep, send, rest)
+    up_grad, bot_grad, lvl_grad = unpack(pos, other, unpack(pos, half))
     return (
         level_out,
         bottom_grad,

time: 118 us -> 106 us (0.90)
  blocking collectives: 53.6 us -> 23 us
  starting transfers between devices: 23.6 us -> 34.5 us
  waiting for transfers between devices: 17.1 us -> 25.2 us
  other arithmetic: 2.35 us -> 3.6 us
  local copies, waits for them, and re-layouts: 5.53 us -> 4.35 us
    all_to_all x2 -> x1, blocking collectives: 53.6 us -> 23 us  [exchange(): return lax.all_to_all(x, AXES, 0, 0, axis_index_groups=BLOCK_GROUPS)]
    all_to_all x0 -> x1, waiting for transfers between devices: none -> 15.9 us  [exchange(): return lax.all_to_all(x, AXES, 0, 0, axis_index_groups=BLOCK_GROUPS)]
    all_to_all x0 -> x1, starting transfers between devices: none -> 13.6 us  [exchange(): return lax.all_to_all(x, AXES, 0, 0, axis_index_groups=BLOCK_GROUPS)]
    ppermute x5, waiting for transfers between devices: 8.21 us -> 3.98 us  [the longest x2 2.76 us: swapped(): got_inner = lax.ppermute(inner, axis, INNER_PAIRS)]
    ppermute x5, starting transfers between devices: 14.8 us -> 10.9 us  [the longest x2 5.29 us: swapped(): got_outer = lax.ppermute(outer, axis, OUTER_PAIRS)]
    ppermute x3, waiting for transfers between devices: 5.61 us -> 2.63 us  [total_over_devices(): planes = [lax.ppermute(part, AXES, depth_shift(step)) for step in (2, 6, 4)]]
    unnamed x23 -> x29, local copies, waits for them, and re-layouts: 5.28 us -> 3.13 us
    pallas_call x3 -> x4, Pallas kernels: 12.7 us -> 12.7 us  [the longest x1 8.42 us: local_work(): pl.pallas_call(functools.partial(main_kernel, scale), out_shape=tuple((ja...]
  transfers between devices with their start and end apart: 9 -> 10, of which waited for: 6 -> 7; matrix products, arithmetic and copies ran while one was open for 0% -> 1% of each run, Pallas kernels for 1% -> 4%
where the time goes in v4:
time: 106 us
  starting transfers between devices  34.5 us (33%)
  waiting for transfers between devices  25.2 us (24%)
  blocking collectives  23 us (22%)
  Pallas kernels  14.5 us (14%)
  local copies, waits for them, and re-layouts  4.35 us (4%)
  other arithmetic  3.6 us (3%)
    all_to_all x1, blocking collectives, exchange(): return lax.all_to_all(x, AXES, 0, 0, axis_index_groups=BLOCK_GROUPS)  23 us
    all_to_all x1, waiting for transfers between devices, exchange(): return lax.all_to_all(x, AXES, 0, 0, axis_index_groups=BLOCK_GROUPS)  15.9 us
    all_to_all x1, starting transfers between devices, exchange(): return lax.all_to_all(x, AXES, 0, 0, axis_index_groups=BLOCK_GROUPS)  13.6 us
    ppermute x3, starting transfers between devices, total_over_devices(): planes = [lax.ppermute(part, AXES, depth_shift(step)) for step in (2, 6, 4)]  9.22 us
    pallas_call x1, Pallas kernels, local_work(): pl.pallas_call(functools.partial(main_kernel, scale), out_shape=tuple((ja...  8.42 us
    ppermute x2, starting transfers between devices, swapped(): got_outer = lax.ppermute(outer, axis, OUTER_PAIRS)  5.29 us
    pallas_call x2, Pallas kernels, unpack(): pl.pallas_call(functools.partial(unpack_kernel, 1 if begun else 0), out_s...  4.16 us
    ppermute x1, starting transfers between devices, total_over_devices(): return (half, lax.ppermute(half, 'row', CORE_SWAP), rest)  4.12 us
  transfers between devices with their start and end apart: 10, of which 7 were waited for; matrix products, arithmetic and copies ran while one was open for 1% of the time, Pallas kernels for 4%

profile of v4, /device:TPU:1, one launch (start us, length us, event | category | flops | bytes accessed | tf_op | source)
XLA Modules:
  0.0 106.0 jit_solution(17338513314329349674)
XLA Ops:
  0.7 1.0 copy-done.3
  1.7 0.9 copy-done.4
  2.6 0.9 copy-done.5
  3.7 4.6 %collective-permute-start = (bf16[7,16,256]{2,1,0:T(8,128)(2,1)S(1)}, bf16[7,16,256]{2,1,0:T(8,128)(2,1)S(1)}, u32[]{:S(2)}, u32[]{:S(2)}) collective-permute-start(bf16[7,16,256]{2,1,0:T(8,128)(2,1)S(1)} %get-tuple-element.24), channel_id=1, source_target_pairs={{16,32},{32,16},{48,64},{64,48},{80,96},{96,80},{112,128},{128,112... | collective-permute-start | bytes 172040 | tf_op jit(solution)/shard_map/ppermute | solution.py:417
  8.6 1.0 rev.3.flip_ref
  9.5 0.7 collective-permute-done
  10.9 1.4 %collective-permute-start.3 = (bf16[78,2,256]{2,1,0:T(2,128)(2,1)S(1)}, bf16[78,2,256]{2,1,0:T(2,128)(2,1)S(1)}, u32[]{:S(2)}, u32[]{:S(2)}) collective-permute-start(bf16[78,2,256]{2,1,0:T(2,128)(2,1)S(1)} %get-tuple-element.53), channel_id=1, source_target_pairs={{0,1},{1,0},{2,3},{3,2},{4,5},{5,4},{6,7},{7,6},{8,9},{9,8},{10,11... | collective-permute-start | bytes 239624 | tf_op jit(solution)/shard_map/ppermute | solution.py:416
  13.0 2.8 %collective-permute-done.3 = bf16[78,2,256]{2,1,0:T(2,128)(2,1)S(1)} collective-permute-done((bf16[78,2,256]{2,1,0:T(2,128)(2,1)S(1)}, bf16[78,2,256]{2,1,0:T(2,128)(2,1)S(1)}, u32[]{:S(2)}, u32[]{:S(2)}) %collective-permute-start.3) | collective-permute-done | bytes 79904 | tf_op jit(solution)/shard_map/ppermute | solution.py:416
  15.9 8.4 %shard_map.102 = (bf16[2,18,16,512]{3,2,1,0:T(8,128)(2,1)S(1)}, bf16[18,16,768]{2,1,0:T(8,128)(2,1)S(1)}, bf16[5120,128]{1,0:T(8,128)(2,1)S(1)}, bf16[5120,128]{1,0:T(8,128)(2,1)S(1)}) custom-call(s32[5]{0:T(128)S(1)} %pad_add_fusion.pos_ref, bf16[5,16,16,256]{3,2,1,0:T(8,128)(2,1)S(1)} %get-tuple-element.23.z_ref, ...), custom_call_target="tpu_custom_call" | custom-call | tf_op jit(solution)/shard_map/pallas_call | solution.py:340
  24.4 0.7 collective-permute-start.4
  25.1 2.7 %collective-permute-done.4 = bf16[5120,128]{1,0:T(8,128)(2,1)S(1)} collective-permute-done((bf16[5120,128]{1,0:T(8,128)(2,1)S(1)}, bf16[5120,128]{1,0:T(8,128)(2,1)S(1)}, u32[]{:S(2)}, u32[]{:S(2)}) %collective-permute-start.4) | collective-permute-done | bytes 1310752 | tf_op jit(solution)/shard_map/ppermute | solution.py:427
  27.8 1.4 %add_convert_fusion = bf16[5120,128]{1,0:T(8,128)(2,1)} fusion(bf16[5120,128]{1,0:T(8,128)(2,1)S(1)} %collective-permute-done.4, bf16[5120,128]{1,0:T(8,128)(2,1)S(1)} %get-tuple-element.26), kind=kLoop, calls=%fused_computation | loop fusion | flops 2621440 | bytes 3932160 | tf_op jit(solution)/shard_map/convert_element_type | solution.py:428
  29.2 13.6 %all-to-all-start = ((bf16[32,160,128]{2,1,0:T(8,128)(2,1)}), bf16[32,160,128]{2,1,0:T(8,128)(2,1)}, u32[]{:S(2)}, u32[]{:S(2)}) async-start(bf16[32,160,128]{2,1,0:T(8,128)(2,1)} %bitcast.30), calls=%async_computation | async-start | bytes 2621440 | tf_op jit(solution)/shard_map/all_to_all | solution.py:423
  42.8 1.7 %shard_map.103 = (bf16[32,32,128]{2,1,0:T(8,128)(2,1)}, bf16[16,16,256]{2,1,0:T(8,128)(2,1)}) custom-call(bf16[2,18,16,512]{3,2,1,0:T(8,128)(2,1)S(1)} %copy-done.7, bf16[18,16,768]{2,1,0:T(8,128)(2,1)S(1)} %copy-done.9, bf16[3,3,256,256]{3,2,1,0:T(8,128)(2,1)S(1)} %copy-done, bf16[3,3,128,128]{3,2,1,0:T(8,128)(2,1)S(1)} %copy-done.2), custom_call_target="tpu_custom_call" | custom-call | flops 1000000000 | bytes 3000000 | tf_op jit(solution)/shard_map/pallas_call | solution.py:322
  44.5 15.9 %all-to-all-done = bf16[32,160,128]{2,1,0:T(8,128)(2,1)} async-done(((bf16[32,160,128]{2,1,0:T(8,128)(2,1)}), bf16[32,160,128]{2,1,0:T(8,128)(2,1)}, u32[]{:S(2)}, u32[]{:S(2)}) %all-to-all-start) | async-done | bytes 1310752 | tf_op jit(solution)/shard_map/all_to_all | solution.py:423
  60.5 1.5 %reduce_sum.12 = bf16[160,128]{1,0:T(8,128)(2,1)S(1)} reduce(bf16[32,160,128]{2,1,0:T(8,128)(2,1)} %all-to-all-done, bf16[]{:T(256)} %constant.58.clone.1), dimensions={0}, to_apply=%region_0.1 | reduce | flops 634880 | bytes 1351682 | tf_op jit(solution)/shard_map/reduce_sum | solution.py:430
  62.0 6.9 %collective-permute-start.7 = (bf16[160,128]{1,0:T(8,128)(2,1)S(1)}, bf16[160,128]{1,0:T(8,128)(2,1)S(1)}, u32[]{:S(2)}, u32[]{:S(2)}) collective-permute-start(bf16[160,128]{1,0:T(8,128)(2,1)S(1)} %reduce_sum.12), channel_id=1, source_target_pairs={{0,8},{1,9},{2,10},{3,11},{4,12},{5,13},{6,14},{7,15},{8,0},{9,1},... | collective-permute-start | bytes 122888 | tf_op jit(solution)/shard_map/ppermute | solution.py:432
  68.9 2.4 %collective-permute-start.5 = (bf16[160,128]{1,0:T(8,128)(2,1)S(1)}, bf16[160,128]{1,0:T(8,128)(2,1)S(1)}, u32[]{:S(2)}, u32[]{:S(2)}) collective-permute-start(bf16[160,128]{1,0:T(8,128)(2,1)S(1)} %reduce_sum.12), channel_id=1, source_target_pairs={{0,4},{1,5},{2,6},{3,7},{4,8},{5,9},{6,10},{7,11},{8,12},{9,13},{1... | collective-permute-start | bytes 122888 | tf_op jit(solution)/shard_map/ppermute | solution.py:432
  71.2 1.7 %collective-permute-done.6 = bf16[160,128]{1,0:T(8,128)(2,1)S(1)} collective-permute-done((bf16[160,128]{1,0:T(8,128)(2,1)S(1)}, bf16[160,128]{1,0:T(8,128)(2,1)S(1)}, u32[]{:S(2)}, u32[]{:S(2)}) %collective-permute-start.6) | collective-permute-done | bytes 40992 | tf_op jit(solution)/shard_map/ppermute | solution.py:432
  72.9 0.9 collective-permute-done.5
  74.1 23.0 %all_to_all.10 = bf16[32,160,128]{2,1,0:T(8,128)(2,1)S(1)} all-to-all(bf16[32,160,128]{2,1,0:T(8,128)(2,1)S(1)} %broadcast_in_dim.26), channel_id=1, replica_groups={{0,1,128,129,32,33,160,161,64,65,192,193,96,97,224,225,2,3,130,131,34,3..., dimensions={0} | all-to-all | bytes 2621440 | tf_op jit(solution)/shard_map/all_to_all | solution.py:423
  97.2 4.1 %collective-permute-start.8 = (bf16[5120,128]{1,0:T(8,128)(2,1)S(1)}, bf16[5120,128]{1,0:T(8,128)(2,1)S(1)}, u32[]{:S(2)}, u32[]{:S(2)}) collective-permute-start(bf16[5120,128]{1,0:T(8,128)(2,1)S(1)} %bitcast.28), channel_id=1, source_target_pairs={{0,16},{16,0},{32,48},{48,32},{64,80},{80,64},{96,112},{112,96},{1... | collective-permute-start | bytes 3932168 | tf_op jit(solution)/shard_map/ppermute | solution.py:442
  101.3 2.1 %shard_map.104 = (f32[4096,128]{1,0:T(8,128)}, f32[2304,256]{1,0:T(8,128)}, f32[1152,128]{1,0:T(8,128)}) custom-call(s32[5]{0:T(128)S(1)} %pad_add_fusion.pos_ref, bf16[5120,128]{1,0:T(8,128)(2,1)S(1)} %bitcast.29), custom_call_target="tpu_custom_call" | custom-call | bytes 4000000 | tf_op jit(solution)/shard_map/pallas_call | solution.py:402
  104.0 2.1 %shard_map.105 = (f32[4096,128]{1,0:T(8,128)}, f32[2304,256]{1,0:T(8,128)}, f32[1152,128]{1,0:T(8,128)}) custom-call(s32[5]{0:T(128)S(1)} %pad_add_fusion.pos_ref, bf16[5120,128]{1,0:T(8,128)(2,1)S(1)} %collective-permute-done.8.half, f32[4096,128]{1,0:T(8,128)} %get-tuple-element.35.refs_0_, ...), custom_call_target="tpu_custom_call", output_to_operand_aliasing={{0}: (2, {}), {1}: (3, {}), {2}: (4, {})} | custom-call | bytes 4000000 | tf_op jit(solution)/shard_map/pallas_call | solution.py:402
  (47 shorter events, 2.7 us)
Async XLA Ops:
  0.6 15.3 %copy-start = (bf16[3,3,256,256]{3,2,1,0:T(8,128)(2,1)S(1)}, bf16[3,3,256,256]{3,2,1,0:T(8,128)(2,1)}, u32[]{:S(2)}) copy-start(bf16[3,3,256,256]{3,2,1,0:T(8,128)(2,1)} %bk_ref.3) | copy-start | bytes 3538948
  0.6 1.0 copy-start.3
  1.7 0.9 copy-start.4
  2.6 0.9 copy-start.5
  3.5 12.4 %copy-start.1 = (bf16[4,4,256,128]{3,2,1,0:T(8,128)(2,1)S(1)}, bf16[4,4,256,128]{3,2,1,0:T(8,128)(2,1)}, u32[]{:S(2)}) copy-start(bf16[4,4,256,128]{3,2,1,0:T(8,128)(2,1)} %uk_ref.1) | copy-start | bytes 3145732
  3.7 6.5 %collective-permute-start = (bf16[7,16,256]{2,1,0:T(8,128)(2,1)S(1)}, bf16[7,16,256]{2,1,0:T(8,128)(2,1)S(1)}, u32[]{:S(2)}, u32[]{:S(2)}) collective-permute-start(bf16[7,16,256]{2,1,0:T(8,128)(2,1)S(1)} %get-tuple-element.24), channel_id=1, source_target_pairs={{16,32},{32,16},{48,64},{64,48},{80,96},{96,80},{112,128},{128,112... | collective-permute-start | bytes 172040 | tf_op jit(solution)/shard_map/ppermute | solution.py:417
  8.4 1.9 %collective-permute-start.1 = (bf16[7,16,256]{2,1,0:T(8,128)(2,1)S(1)}, bf16[7,16,256]{2,1,0:T(8,128)(2,1)S(1)}, u32[]{:S(2)}, u32[]{:S(2)}) collective-permute-start(bf16[7,16,256]{2,1,0:T(8,128)(2,1)S(1)} %get-tuple-element.25), channel_id=1, source_target_pairs={{0,16},{16,0},{32,48},{48,32},{64,80},{80,64},{96,112},{112,96},{1... | collective-permute-start | bytes 172040 | tf_op jit(solution)/shard_map/ppermute | solution.py:416
  10.9 4.9 %collective-permute-start.3 = (bf16[78,2,256]{2,1,0:T(2,128)(2,1)S(1)}, bf16[78,2,256]{2,1,0:T(2,128)(2,1)S(1)}, u32[]{:S(2)}, u32[]{:S(2)}) collective-permute-start(bf16[78,2,256]{2,1,0:T(2,128)(2,1)S(1)} %get-tuple-element.53), channel_id=1, source_target_pairs={{0,1},{1,0},{2,3},{3,2},{4,5},{5,4},{6,7},{7,6},{8,9},{9,8},{10,11... | collective-permute-start | bytes 239624 | tf_op jit(solution)/shard_map/ppermute | solution.py:416
  12.3 3.5 %collective-permute-start.2 = (bf16[78,2,256]{2,1,0:T(2,128)(2,1)S(1)}, bf16[78,2,256]{2,1,0:T(2,128)(2,1)S(1)}, u32[]{:S(2)}, u32[]{:S(2)}) collective-permute-start(bf16[78,2,256]{2,1,0:T(2,128)(2,1)S(1)} %get-tuple-element.54), channel_id=1, source_target_pairs={{1,2},{2,1},{3,4},{4,3},{5,6},{6,5},{7,8},{8,7},{9,10},{10,9},{11,... | collective-permute-start | bytes 239624 | tf_op jit(solution)/shard_map/ppermute | solution.py:417
  24.4 4.8 %copy-start.6 = (bf16[2,18,16,512]{3,2,1,0:T(8,128)(2,1)}, bf16[2,18,16,512]{3,2,1,0:T(8,128)(2,1)S(1)}, u32[]{:S(2)}) copy-start(bf16[2,18,16,512]{3,2,1,0:T(8,128)(2,1)S(1)} %get-tuple-element.28.mix4c) | copy-start | bytes 1769476
  24.4 4.8 %copy-start.8 = (bf16[18,16,768]{2,1,0:T(8,128)(2,1)}, bf16[18,16,768]{2,1,0:T(8,128)(2,1)S(1)}, u32[]{:S(2)}) copy-start(bf16[18,16,768]{2,1,0:T(8,128)(2,1)S(1)} %get-tuple-element.29.pg3c) | copy-start | bytes 1327108
  24.4 3.4 %collective-permute-start.4 = (bf16[5120,128]{1,0:T(8,128)(2,1)S(1)}, bf16[5120,128]{1,0:T(8,128)(2,1)S(1)}, u32[]{:S(2)}, u32[]{:S(2)}) collective-permute-start(bf16[5120,128]{1,0:T(8,128)(2,1)S(1)} %get-tuple-element.27), channel_id=1, source_target_pairs={{0,16},{16,0},{32,48},{48,32},{64,80},{80,64},{96,112},{112,96},{1... | collective-permute-start | bytes 3932168 | tf_op jit(solution)/shard_map/ppermute | solution.py:427
  29.2 13.6 %copy-start.2 = (bf16[3,3,128,128]{3,2,1,0:T(8,128)(2,1)S(1)}, bf16[3,3,128,128]{3,2,1,0:T(8,128)(2,1)}, u32[]{:S(2)}) copy-start(bf16[3,3,128,128]{3,2,1,0:T(8,128)(2,1)} %lk_ref.1) | copy-start | bytes 884740
  29.2 13.6 %copy-start.7 = (bf16[2,18,16,512]{3,2,1,0:T(8,128)(2,1)S(1)}, bf16[2,18,16,512]{3,2,1,0:T(8,128)(2,1)}, u32[]{:S(2)}) copy-start(bf16[2,18,16,512]{3,2,1,0:T(8,128)(2,1)} %copy-done.6) | copy-start | bytes 1769476
  29.2 13.6 %copy-start.9 = (bf16[18,16,768]{2,1,0:T(8,128)(2,1)S(1)}, bf16[18,16,768]{2,1,0:T(8,128)(2,1)}, u32[]{:S(2)}) copy-start(bf16[18,16,768]{2,1,0:T(8,128)(2,1)} %copy-done.8) | copy-start | bytes 1327108
  29.2 31.3 %all-to-all-start = ((bf16[32,160,128]{2,1,0:T(8,128)(2,1)}), bf16[32,160,128]{2,1,0:T(8,128)(2,1)}, u32[]{:S(2)}, u32[]{:S(2)}) async-start(bf16[32,160,128]{2,1,0:T(8,128)(2,1)} %bitcast.30), calls=%async_computation | async-start | bytes 2621440 | tf_op jit(solution)/shard_map/all_to_all | solution.py:423
  62.0 9.2 %collective-permute-start.7 = (bf16[160,128]{1,0:T(8,128)(2,1)S(1)}, bf16[160,128]{1,0:T(8,128)(2,1)S(1)}, u32[]{:S(2)}, u32[]{:S(2)}) collective-permute-start(bf16[160,128]{1,0:T(8,128)(2,1)S(1)} %reduce_sum.12), channel_id=1, source_target_pairs={{0,8},{1,9},{2,10},{3,11},{4,12},{5,13},{6,14},{7,15},{8,0},{9,1},... | collective-permute-start | bytes 122888 | tf_op jit(solution)/shard_map/ppermute | solution.py:432
  68.9 4.0 %collective-permute-start.6 = (bf16[160,128]{1,0:T(8,128)(2,1)S(1)}, bf16[160,128]{1,0:T(8,128)(2,1)S(1)}, u32[]{:S(2)}, u32[]{:S(2)}) collective-permute-start(bf16[160,128]{1,0:T(8,128)(2,1)S(1)} %reduce_sum.12), channel_id=1, source_target_pairs={{0,12},{1,13},{2,14},{3,15},{4,0},{5,1},{6,2},{7,3},{8,4},{9,5},{1... | collective-permute-start | bytes 122888 | tf_op jit(solution)/shard_map/ppermute | solution.py:432
  68.9 5.0 %collective-permute-start.5 = (bf16[160,128]{1,0:T(8,128)(2,1)S(1)}, bf16[160,128]{1,0:T(8,128)(2,1)S(1)}, u32[]{:S(2)}, u32[]{:S(2)}) collective-permute-start(bf16[160,128]{1,0:T(8,128)(2,1)S(1)} %reduce_sum.12), channel_id=1, source_target_pairs={{0,4},{1,5},{2,6},{3,7},{4,8},{5,9},{6,10},{7,11},{8,12},{9,13},{1... | collective-permute-start | bytes 122888 | tf_op jit(solution)/shard_map/ppermute | solution.py:432
  97.2 6.8 %collective-permute-start.8 = (bf16[5120,128]{1,0:T(8,128)(2,1)S(1)}, bf16[5120,128]{1,0:T(8,128)(2,1)S(1)}, u32[]{:S(2)}, u32[]{:S(2)}) collective-permute-start(bf16[5120,128]{1,0:T(8,128)(2,1)S(1)} %bitcast.28), channel_id=1, source_target_pairs={{0,16},{16,0},{32,48},{48,32},{64,80},{80,64},{96,112},{112,96},{1... | collective-permute-start | bytes 3932168 | tf_op jit(solution)/shard_map/ppermute | solution.py:442

commit v5 on v4

--- a/solution.py
+++ b/solution.py
@@ -15,6 +15,7 @@
 PITCH = 32
 CORE = 8
 MAIN_LIMIT = 40 << 20
+EDGE_LIMIT = 56 << 20
 HALF = 5120
 
 
@@ -22,11 +23,6 @@
     row = (((y >> 1) & 1) * 4 + x % 4) * 2 + core
     col = (z % 8) * 2 + (y & 1)
     return row * 16 + col
-
-
-def device_xyz(device):
-    row, col = divmod(device, 16)
-    return (row >> 1) & 3, ((row >> 3) << 1) | (col & 1), col >> 1, row & 1
 
 
 BLOCK = 32
@@ -37,21 +33,75 @@
 ]
 
 
-def depth_shift(step):
-    moves = []
-    for device in range(256):
-        x, y, z, core = device_xyz(device)
-        moves.append((device, place(x, y, z + step, core)))
-    return moves
-
-
+PAIR_GROUPS = [
+    [place(x, y, z + dz, core) for z in range(0, 8, 2)]
+    for dz in range(2)
+    for x in range(4)
+    for y in range(4)
+    for core in range(2)
+]
 CORE_SWAP = [(i, i ^ 1) for i in range(16)]
 INNER_PAIRS = CORE_SWAP
 OUTER_PAIRS = [pair for i in range(1, 15, 2) for pair in ((i, i + 1), (i + 1, i))]
 
 
-def split_kernel(bot, skip, cot, out_ref, inner_ref, outer_ref, wide):
+def edge_kernel(
+    bot_hbm, skip_hbm, cot_hbm, inner_ref, outer_ref, bot, fine, wide, sems
+):
+    copies = [
+        pltpu.make_async_copy(src, dst, sems.at[i])
+        for i, (src, dst) in enumerate(
+            (
+                (cot_hbm.at[pl.ds(0, 4)], fine.at[pl.ds(0, 4)]),
+                (cot_hbm.at[pl.ds(2 * TILE - 4, 4)], fine.at[pl.ds(4, 4)]),
+                (skip_hbm.at[pl.ds(0, 1)], fine.at[pl.ds(8, 1)]),
+                (skip_hbm.at[pl.ds(2 * TILE - 1, 1)], fine.at[pl.ds(9, 1)]),
+                (bot_hbm.at[pl.ds(0, 2)], bot.at[pl.ds(0, 2)]),
+                (bot_hbm.at[pl.ds(TILE - 2, 2)], bot.at[pl.ds(2, 2)]),
+            )
+        )
+    ]
+    for copy in copies:
+        copy.start()
     even = lax.rem(lax.axis_index("row"), 2) == 0
+
+    def put(at, lanes, first, last):
+        inner_ref[at, :, lanes] = jnp.where(even, last, first)
+        outer_ref[at, :, lanes] = jnp.where(even, first, last)
+
+    for copy in copies:
+        copy.wait()
+    put(slice(0, 2), slice(0, 256), bot[0:2], bot[2:4])
+    wide[...] = fine[...].astype(F32)
+    for col_par in range(2):
+        lanes = slice(col_par * 128, col_par * 128 + 128)
+        part = wide[:, pl.ds(col_par, TILE, stride=2), :].astype(BF16)
+        for par in range(2):
+            for step in range(2):
+                row = 2 * step + par
+                put(2 + 2 * par + step, lanes, part[row], part[4 + row])
+        put(6, lanes, part[8], part[9])
+
+
+def edges(bottom_in, skip_feat, cotangent):
+    vmem = pl.BlockSpec(memory_space=pltpu.VMEM)
+    strip = jax.ShapeDtypeStruct((7, TILE, 256), BF16)
+    return pl.pallas_call(
+        edge_kernel,
+        out_shape=(strip, strip),
+        in_specs=[pl.BlockSpec(memory_space=pl.ANY)] * 3,
+        out_specs=(vmem, vmem),
+        scratch_shapes=[
+            pltpu.VMEM((4, TILE, 256), BF16),
+            pltpu.VMEM((10, 2 * TILE, 128), BF16),
+            pltpu.VMEM((10, 2 * TILE, 128), F32),
+            pltpu.SemaphoreType.DMA((6,)),
+        ],
+        compiler_params=pltpu.CompilerParams(vmem_limit_bytes=EDGE_LIMIT),
+    )(bottom_in, skip_feat, cotangent)
+
+
+def split_kernel(bot, skip, cot, out_ref, wide):
     for plane, ref in ((1, cot), (3, skip)):
         wide[...] = ref[...].astype(F32)
         for col_par in range(2):
@@ -61,24 +111,15 @@
             out_ref[plane, :, :, lanes] = part[:, 0]
             out_ref[plane + 1, :, :, lanes] = part[:, 1]
     out_ref[0] = bot[...]
-    for plane in range(3):
-        two = slice(2 * plane, 2 * plane + 2)
-        last, first = out_ref[plane, TILE - 2 : TILE], out_ref[plane, 0:2]
-        inner_ref[two] = jnp.where(even, last, first)
-        outer_ref[two] = jnp.where(even, first, last)
-    last, first = out_ref[4, TILE - 1], out_ref[3, 0]
-    inner_ref[6] = jnp.where(even, last, first)
-    outer_ref[6] = jnp.where(even, first, last)
 
 
 def split(bottom_in, skip_feat, cotangent):
     vmem = pl.BlockSpec(memory_space=pltpu.VMEM)
-    shapes = ((5, TILE, TILE, 256), (7, TILE, 256), (7, TILE, 256))
     return pl.pallas_call(
         split_kernel,
-        out_shape=tuple(jax.ShapeDtypeStruct(shape, BF16) for shape in shapes),
+        out_shape=jax.ShapeDtypeStruct((5, TILE, TILE, 256), BF16),
         in_specs=[vmem] * 3,
-        out_specs=(vmem,) * 3,
+        out_specs=vmem,
         scratch_shapes=[pltpu.VMEM((2 * TILE, 2 * TILE, 128), F32)],
         compiler_params=pltpu.CompilerParams(vmem_limit_bytes=16 << 20),
     )(bottom_in, skip_feat, cotangent)
@@ -419,33 +460,29 @@
     return jnp.where(even, got_outer, got_inner), jnp.where(even, got_inner, got_outer)
 
 
-def exchange(x):
-    return lax.all_to_all(x, AXES, 0, 0, axis_index_groups=BLOCK_GROUPS)
+def exchange(x, groups):
+    return lax.all_to_all(x, AXES, 0, 0, axis_index_groups=groups)
 
 
 def total_over_devices(keep, send, rest):
-    got = lax.ppermute(send, "row", CORE_SWAP)
+    got, rest = lax.optimization_barrier((lax.ppermute(send, "row", CORE_SWAP), rest))
     half = (keep.astype(F32) + got.astype(F32)).astype(BF16)
-    parts = exchange(half.reshape(BLOCK, HALF // BLOCK, 128))
+    parts = exchange(half.reshape(BLOCK, HALF // BLOCK, 128), BLOCK_GROUPS)
     part = jnp.sum(parts.astype(F32), axis=0).astype(BF16)
-    part, rest = lax.optimization_barrier((part, rest))
-    planes = [lax.ppermute(part, AXES, depth_shift(step)) for step in (2, 6, 4)]
-    pair = lax.axis_index("col") // 4
-    terms = [part] + planes
-    places = [pair, (pair + 3) % 4, (pair + 1) % 4, (pair + 2) % 4]
-    total = jnp.zeros(part.shape, F32)
-    for slot in range(4):
-        for term, where in zip(terms, places):
-            total = total + jnp.where(where == slot, term.astype(F32), 0.0)
-    total = total.astype(BF16)
-    half = exchange(jnp.broadcast_to(total[None], parts.shape)).reshape(HALF, 128)
+    pairs = exchange(jnp.broadcast_to(part[None], (4,) + part.shape), PAIR_GROUPS)
+    total = jnp.sum(pairs.astype(F32), axis=0).astype(BF16)
+    half = exchange(jnp.broadcast_to(total[None], parts.shape), BLOCK_GROUPS).reshape(HALF, 128)
     return half, lax.ppermute(half, "row", CORE_SWAP), rest
 
 
 def on_device(bottom_in, skip_feat, cotangent, bot_kernel, up_kernel, lvl_kernel):
     rows, cols = lax.axis_size("row"), lax.axis_size("col")
     scale = 1.0 / float(2 * TILE * rows * 2 * TILE * cols) ** 0.5
-    z, inner, outer = split(bottom_in, skip_feat, cotangent)
+    inner, outer = edges(bottom_in, skip_feat, cotangent)
+    inner, outer, *fields = lax.optimization_barrier(
+        (inner, outer, bottom_in, skip_feat, cotangent)
+    )
+    z = split(*fields)
     up, down = swapped(inner, outer, "row")
 
     def side(cols, skip_col):

time: 106 us -> 106 us (level)
  blocking collectives: 23 us -> 67.4 us
  waiting for transfers between devices: 25.2 us -> 2.75 us
  starting transfers between devices: 34.5 us -> 13.3 us
  Pallas kernels: 14.5 us -> 16 us
  other arithmetic: 3.6 us -> 2.11 us
    all_to_all x1 -> x3, blocking collectives: 23 us -> 67.4 us  [exchange(): return lax.all_to_all(x, AXES, 0, 0, axis_index_groups=groups)]
    all_to_all x1 -> x0, waiting for transfers between devices: 15.9 us -> none  [exchange(): return lax.all_to_all(x, AXES, 0, 0, axis_index_groups=BLOCK_GROUPS)]
    all_to_all x1 -> x0, starting transfers between devices: 13.6 us -> none  [exchange(): return lax.all_to_all(x, AXES, 0, 0, axis_index_groups=BLOCK_GROUPS)]
    ppermute x4 -> x1, starting transfers between devices: 9.96 us -> 1.76 us  [total_over_devices(): lax.ppermute(send, 'row', CORE_SWAP)]
    ppermute x4 -> x1, waiting for transfers between devices: 5.29 us -> 0.97 us  [total_over_devices(): lax.ppermute(send, 'row', CORE_SWAP)]
    pallas_call x1 -> x2, Pallas kernels: 0.17 us -> 1.73 us  [the longest x1 1.57 us: edges(): pl.pallas_call(edge_kernel, out_shape=(strip, strip), in_specs=[pl.BlockS...]
    ppermute x2, waiting for transfers between devices: 2.76 us -> 1.22 us  [swapped(): got_inner = lax.ppermute(inner, axis, INNER_PAIRS)]
    reduce_sum x1, other arithmetic: 1.5 us -> 0.19 us  [total_over_devices(): part = jnp.sum(parts.astype(F32), axis=0).astype(BF16)]
  transfers between devices with their start and end apart: 10 -> 6, of which waited for: 7 -> 3; matrix products, arithmetic and copies ran while one was open for 1% -> 0% of each run, Pallas kernels for 4% -> 4%
where the time goes in v5:
time: 106 us
  blocking collectives  67.4 us (64%)
  Pallas kernels  16 us (15%)
  starting transfers between devices  13.3 us (13%)
  local copies, waits for them, and re-layouts  3.3 us (3%)
  waiting for transfers between devices  2.75 us (3%)
  other arithmetic  2.11 us (2%)
    all_to_all x3, blocking collectives, exchange(): return lax.all_to_all(x, AXES, 0, 0, axis_index_groups=groups)  67.4 us
    pallas_call x1, Pallas kernels, local_work(): pl.pallas_call(functools.partial(main_kernel, scale), out_shape=tuple((ja...  8.37 us
    ppermute x2, starting transfers between devices, swapped(): got_outer = lax.ppermute(outer, axis, OUTER_PAIRS)  5.16 us
    ppermute x1, starting transfers between devices, total_over_devices(): return (half, lax.ppermute(half, 'row', CORE_SWAP), rest)  4.86 us
    pallas_call x2, Pallas kernels, unpack(): pl.pallas_call(functools.partial(unpack_kernel, 1 if begun else 0), out_s...  4.16 us
    unnamed x21, local copies, waits for them, and re-layouts  3.02 us
  transfers between devices with their start and end apart: 6, of which 3 were waited for; matrix products, arithmetic and copies ran while one was open for 0% of the time, Pallas kernels for 4%

profile of v5, /device:TPU:1, one launch (start us, length us, event | category | flops | bytes accessed | tf_op | source)
XLA Modules:
  0.0 105.7 jit_solution(9122538353598679142)
XLA Ops:
  0.6 1.6 %shard_map.101 = (bf16[7,16,256]{2,1,0:T(8,128)(2,1)}, bf16[7,16,256]{2,1,0:T(8,128)(2,1)}) custom-call(bf16[16,16,256]{2,1,0:T(8,128)(2,1)} %bot, bf16[32,32,128]{2,1,0:T(8,128)(2,1)} %skip, bf16[32,32,128]{2,1,0:T(8,128)(2,1)} %cot), custom_call_target="tpu_custom_call" | custom-call | tf_op jit(solution)/shard_map/pallas_call | solution.py:89
  2.2 4.5 %collective-permute-start = (bf16[7,16,256]{2,1,0:T(8,128)(2,1)}, bf16[7,16,256]{2,1,0:T(8,128)(2,1)}, u32[]{:S(2)}, u32[]{:S(2)}) collective-permute-start(bf16[7,16,256]{2,1,0:T(8,128)(2,1)} %get-tuple-element.32), channel_id=1, source_target_pairs={{16,32},{32,16},{48,64},{64,48},{80,96},{96,80},{112,128},{128,112... | collective-permute-start | bytes 172040 | tf_op jit(solution)/shard_map/ppermute | solution.py:458
  6.9 0.9 copy-done.2
  7.8 0.9 copy-done.3
  8.7 0.9 copy-done.4
  9.6 0.2 shard_map.102.z_ref
  10.0 1.0 broadcast_select_fusion.4
  11.6 1.4 %collective-permute-start.3 = (bf16[78,2,256]{2,1,0:T(2,128)(2,1)S(1)}, bf16[78,2,256]{2,1,0:T(2,128)(2,1)S(1)}, u32[]{:S(2)}, u32[]{:S(2)}) collective-permute-start(bf16[78,2,256]{2,1,0:T(2,128)(2,1)S(1)} %get-tuple-element.61), channel_id=1, source_target_pairs={{0,1},{1,0},{2,3},{3,2},{4,5},{5,4},{6,7},{7,6},{8,9},{9,8},{10,11... | collective-permute-start | bytes 239624 | tf_op jit(solution)/shard_map/ppermute | solution.py:457
  13.0 0.7 collective-permute-start.2
  13.8 1.2 %collective-permute-done.3 = bf16[78,2,256]{2,1,0:T(2,128)(2,1)S(1)} collective-permute-done((bf16[78,2,256]{2,1,0:T(2,128)(2,1)S(1)}, bf16[78,2,256]{2,1,0:T(2,128)(2,1)S(1)}, u32[]{:S(2)}, u32[]{:S(2)}) %collective-permute-start.3) | collective-permute-done | bytes 79904 | tf_op jit(solution)/shard_map/ppermute | solution.py:457
  15.1 8.4 %shard_map.103 = (bf16[2,18,16,512]{3,2,1,0:T(8,128)(2,1)S(1)}, bf16[18,16,768]{2,1,0:T(8,128)(2,1)S(1)}, bf16[5120,128]{1,0:T(8,128)(2,1)S(1)}, bf16[5120,128]{1,0:T(8,128)(2,1)S(1)}) custom-call(s32[5]{0:T(128)S(1)} %pad_add_fusion.pos_ref, bf16[5,16,16,256]{3,2,1,0:T(8,128)(2,1)S(1)} %shard_map.102.z_ref, ...), custom_call_target="tpu_custom_call" | custom-call | tf_op jit(solution)/shard_map/pallas_call | solution.py:381
  23.5 1.8 %collective-permute-start.4 = (bf16[5120,128]{1,0:T(8,128)(2,1)S(1)}, bf16[5120,128]{1,0:T(8,128)(2,1)S(1)}, u32[]{:S(2)}, u32[]{:S(2)}) collective-permute-start(bf16[5120,128]{1,0:T(8,128)(2,1)S(1)} %get-tuple-element.34), channel_id=1, source_target_pairs={{0,16},{16,0},{32,48},{48,32},{64,80},{80,64},{96,112},{112,96},{1... | collective-permute-start | bytes 3932168 | tf_op jit(solution)/shard_map/ppermute | solution.py:468
  25.3 1.7 %shard_map.104 = (bf16[32,32,128]{2,1,0:T(8,128)(2,1)}, bf16[16,16,256]{2,1,0:T(8,128)(2,1)}) custom-call(bf16[2,18,16,512]{3,2,1,0:T(8,128)(2,1)S(1)} %get-tuple-element.35.mix4c, bf16[18,16,768]{2,1,0:T(8,128)(2,1)S(1)} %get-tuple-element.36.pg3c, bf16[3,3,256,256]{3,2,1,0:T(8,128)(2,1)S(1)} %copy-done, bf16[3,3,128,128]{3,2,1,0:T(8,128)(2,1)S(1)} %copy-done.5), custom_call_target="tpu_custom_call" | custom-call | flops 1000000000 | bytes 3000000 | tf_op jit(solution)/shard_map/pallas_call | solution.py:363
  27.0 1.0 collective-permute-done.4
  27.9 0.3 add_convert_fusion
  28.3 31.4 %all_to_all.15 = bf16[32,160,128]{2,1,0:T(8,128)(2,1)S(1)} all-to-all(bf16[32,160,128]{2,1,0:T(8,128)(2,1)S(1)} %bitcast.42), channel_id=1, replica_groups={{0,1,128,129,32,33,160,161,64,65,192,193,96,97,224,225,2,3,130,131,34,3..., dimensions={0} | all-to-all | bytes 2621440 | tf_op jit(solution)/shard_map/all_to_all | solution.py:464
  59.7 0.2 reduce_sum.24
  59.9 16.0 %all_to_all.16 = bf16[4,160,128]{2,1,0:T(8,128)(2,1)S(1)} all-to-all(bf16[4,160,128]{2,1,0:T(8,128)(2,1)S(1)} %broadcast_in_dim.4), channel_id=1, replica_groups={{0,4,8,12},{16,20,24,28},{1,5,9,13},{17,21,25,29},{128,132,136,140},{14..., dimensions={0} | all-to-all | bytes 327680 | tf_op jit(solution)/shard_map/all_to_all | solution.py:464
  75.9 0.2 broadcast_in_dim.5
  76.1 20.0 %all_to_all.17 = bf16[32,160,128]{2,1,0:T(8,128)(2,1)S(1)} all-to-all(bf16[32,160,128]{2,1,0:T(8,128)(2,1)S(1)} %broadcast_in_dim.5), channel_id=1, replica_groups={{0,1,128,129,32,33,160,161,64,65,192,193,96,97,224,225,2,3,130,131,34,3..., dimensions={0} | all-to-all | bytes 2621440 | tf_op jit(solution)/shard_map/all_to_all | solution.py:464
  96.1 4.9 %collective-permute-start.5 = (bf16[5120,128]{1,0:T(8,128)(2,1)S(1)}, bf16[5120,128]{1,0:T(8,128)(2,1)S(1)}, u32[]{:S(2)}, u32[]{:S(2)}) collective-permute-start(bf16[5120,128]{1,0:T(8,128)(2,1)S(1)} %bitcast.40), channel_id=1, source_target_pairs={{0,16},{16,0},{32,48},{48,32},{64,80},{80,64},{96,112},{112,96},{1... | collective-permute-start | bytes 3932168 | tf_op jit(solution)/shard_map/ppermute | solution.py:475
  101.0 2.1 %shard_map.105 = (f32[4096,128]{1,0:T(8,128)}, f32[2304,256]{1,0:T(8,128)}, f32[1152,128]{1,0:T(8,128)}) custom-call(s32[5]{0:T(128)S(1)} %pad_add_fusion.pos_ref, bf16[5120,128]{1,0:T(8,128)(2,1)S(1)} %bitcast.41), custom_call_target="tpu_custom_call" | custom-call | bytes 4000000 | tf_op jit(solution)/shard_map/pallas_call | solution.py:443
  103.1 0.6 collective-permute-done.5.half
  103.7 2.1 %shard_map.106 = (f32[4096,128]{1,0:T(8,128)}, f32[2304,256]{1,0:T(8,128)}, f32[1152,128]{1,0:T(8,128)}) custom-call(s32[5]{0:T(128)S(1)} %pad_add_fusion.pos_ref, bf16[5120,128]{1,0:T(8,128)(2,1)S(1)} %collective-permute-done.5.half, f32[4096,128]{1,0:T(8,128)} %get-tuple-element.43.refs_0_, ...), custom_call_target="tpu_custom_call", output_to_operand_aliasing={{0}: (2, {}), {1}: (3, {}), {2}: (4, {})} | custom-call | bytes 4000000 | tf_op jit(solution)/shard_map/pallas_call | solution.py:443
  (35 shorter events, 1.0 us)
Async XLA Ops:
  0.6 9.3 %copy-start.5 = (bf16[3,3,128,128]{3,2,1,0:T(8,128)(2,1)S(1)}, bf16[3,3,128,128]{3,2,1,0:T(8,128)(2,1)}, u32[]{:S(2)}) copy-start(bf16[3,3,128,128]{3,2,1,0:T(8,128)(2,1)} %lk_ref.1) | copy-start | bytes 884740
  2.2 7.8 %collective-permute-start = (bf16[7,16,256]{2,1,0:T(8,128)(2,1)}, bf16[7,16,256]{2,1,0:T(8,128)(2,1)}, u32[]{:S(2)}, u32[]{:S(2)}) collective-permute-start(bf16[7,16,256]{2,1,0:T(8,128)(2,1)} %get-tuple-element.32), channel_id=1, source_target_pairs={{16,32},{32,16},{48,64},{64,48},{80,96},{96,80},{112,128},{128,112... | collective-permute-start | bytes 172040 | tf_op jit(solution)/shard_map/ppermute | solution.py:458
  6.7 3.2 %collective-permute-start.1 = (bf16[7,16,256]{2,1,0:T(8,128)(2,1)}, bf16[7,16,256]{2,1,0:T(8,128)(2,1)}, u32[]{:S(2)}, u32[]{:S(2)}) collective-permute-start(bf16[7,16,256]{2,1,0:T(8,128)(2,1)} %get-tuple-element.33), channel_id=1, source_target_pairs={{0,16},{16,0},{32,48},{48,32},{64,80},{80,64},{96,112},{112,96},{1... | collective-permute-start | bytes 172040 | tf_op jit(solution)/shard_map/ppermute | solution.py:457
  6.8 1.0 copy-start.2
  7.8 0.9 copy-start.3
  8.7 0.9 copy-start.4
  9.8 5.3 %copy-start = (bf16[3,3,256,256]{3,2,1,0:T(8,128)(2,1)S(1)}, bf16[3,3,256,256]{3,2,1,0:T(8,128)(2,1)}, u32[]{:S(2)}) copy-start(bf16[3,3,256,256]{3,2,1,0:T(8,128)(2,1)} %bk_ref.3) | copy-start | bytes 3538948
  9.8 5.3 %copy-start.1 = (bf16[4,4,256,128]{3,2,1,0:T(8,128)(2,1)S(1)}, bf16[4,4,256,128]{3,2,1,0:T(8,128)(2,1)}, u32[]{:S(2)}) copy-start(bf16[4,4,256,128]{3,2,1,0:T(8,128)(2,1)} %uk_ref.1) | copy-start | bytes 3145732
  11.6 3.4 %collective-permute-start.3 = (bf16[78,2,256]{2,1,0:T(2,128)(2,1)S(1)}, bf16[78,2,256]{2,1,0:T(2,128)(2,1)S(1)}, u32[]{:S(2)}, u32[]{:S(2)}) collective-permute-start(bf16[78,2,256]{2,1,0:T(2,128)(2,1)S(1)} %get-tuple-element.61), channel_id=1, source_target_pairs={{0,1},{1,0},{2,3},{3,2},{4,5},{5,4},{6,7},{7,6},{8,9},{9,8},{10,11... | collective-permute-start | bytes 239624 | tf_op jit(solution)/shard_map/ppermute | solution.py:457
  13.0 2.0 %collective-permute-start.2 = (bf16[78,2,256]{2,1,0:T(2,128)(2,1)S(1)}, bf16[78,2,256]{2,1,0:T(2,128)(2,1)S(1)}, u32[]{:S(2)}, u32[]{:S(2)}) collective-permute-start(bf16[78,2,256]{2,1,0:T(2,128)(2,1)S(1)} %get-tuple-element.62), channel_id=1, source_target_pairs={{1,2},{2,1},{3,4},{4,3},{5,6},{6,5},{7,8},{8,7},{9,10},{10,9},{11,... | collective-permute-start | bytes 239624 | tf_op jit(solution)/shard_map/ppermute | solution.py:458
  23.5 4.4 %collective-permute-start.4 = (bf16[5120,128]{1,0:T(8,128)(2,1)S(1)}, bf16[5120,128]{1,0:T(8,128)(2,1)S(1)}, u32[]{:S(2)}, u32[]{:S(2)}) collective-permute-start(bf16[5120,128]{1,0:T(8,128)(2,1)S(1)} %get-tuple-element.34), channel_id=1, source_target_pairs={{0,16},{16,0},{32,48},{48,32},{64,80},{80,64},{96,112},{112,96},{1... | collective-permute-start | bytes 3932168 | tf_op jit(solution)/shard_map/ppermute | solution.py:468
  96.1 7.5 %collective-permute-start.5 = (bf16[5120,128]{1,0:T(8,128)(2,1)S(1)}, bf16[5120,128]{1,0:T(8,128)(2,1)S(1)}, u32[]{:S(2)}, u32[]{:S(2)}) collective-permute-start(bf16[5120,128]{1,0:T(8,128)(2,1)S(1)} %bitcast.40), channel_id=1, source_target_pairs={{0,16},{16,0},{32,48},{48,32},{64,80},{80,64},{96,112},{112,96},{1... | collective-permute-start | bytes 3932168 | tf_op jit(solution)/shard_map/ppermute | solution.py:475

commit v6 on v5

--- a/solution.py
+++ b/solution.py
@@ -15,7 +15,7 @@
 PITCH = 32
 CORE = 8
 MAIN_LIMIT = 40 << 20
-EDGE_LIMIT = 56 << 20
+FIRST_LIMIT = 56 << 20
 HALF = 5120
 
 
@@ -45,84 +45,137 @@
 OUTER_PAIRS = [pair for i in range(1, 15, 2) for pair in ((i, i + 1), (i + 1, i))]
 
 
-def edge_kernel(
-    bot_hbm, skip_hbm, cot_hbm, inner_ref, outer_ref, bot, fine, wide, sems
+COLUMNS = 3 * EXT + 18
+
+
+def is_even(axis):
+    return lax.rem(lax.axis_index(axis), 2) == 0
+
+
+def both(even, first, last):
+    return jnp.where(even, last, first).astype(BF16), jnp.where(even, first, last).astype(BF16)
+
+
+def pair_of(first, second):
+    shape = (first.shape[0], 2, 256)
+    odd = lax.broadcasted_iota(jnp.int32, shape, 1) == 1
+    return jnp.where(odd, jnp.broadcast_to(second, shape), jnp.broadcast_to(first, shape))
+
+
+def split_kernel(
+    bot_hbm, skip_hbm, cot_hbm, z_hbm, inner_hbm, outer_hbm, own_hbm,
+    bot, skip, cot, wide, z, inner, outer, own, sems, out_sems,
 ):
     copies = [
         pltpu.make_async_copy(src, dst, sems.at[i])
-        for i, (src, dst) in enumerate(
-            (
-                (cot_hbm.at[pl.ds(0, 4)], fine.at[pl.ds(0, 4)]),
-                (cot_hbm.at[pl.ds(2 * TILE - 4, 4)], fine.at[pl.ds(4, 4)]),
-                (skip_hbm.at[pl.ds(0, 1)], fine.at[pl.ds(8, 1)]),
-                (skip_hbm.at[pl.ds(2 * TILE - 1, 1)], fine.at[pl.ds(9, 1)]),
-                (bot_hbm.at[pl.ds(0, 2)], bot.at[pl.ds(0, 2)]),
-                (bot_hbm.at[pl.ds(TILE - 2, 2)], bot.at[pl.ds(2, 2)]),
-            )
-        )
+        for i, (src, dst) in enumerate(((cot_hbm, cot), (skip_hbm, skip), (bot_hbm, bot)))
     ]
     for copy in copies:
         copy.start()
-    even = lax.rem(lax.axis_index("row"), 2) == 0
-
-    def put(at, lanes, first, last):
-        inner_ref[at, :, lanes] = jnp.where(even, last, first)
-        outer_ref[at, :, lanes] = jnp.where(even, first, last)
-
-    for copy in copies:
+    for plane, ref, copy in ((1, cot, copies[0]), (3, skip, copies[1])):
         copy.wait()
-    put(slice(0, 2), slice(0, 256), bot[0:2], bot[2:4])
-    wide[...] = fine[...].astype(F32)
-    for col_par in range(2):
-        lanes = slice(col_par * 128, col_par * 128 + 128)
-        part = wide[:, pl.ds(col_par, TILE, stride=2), :].astype(BF16)
-        for par in range(2):
-            for step in range(2):
-                row = 2 * step + par
-                put(2 + 2 * par + step, lanes, part[row], part[4 + row])
-        put(6, lanes, part[8], part[9])
-
-
-def edges(bottom_in, skip_feat, cotangent):
-    vmem = pl.BlockSpec(memory_space=pltpu.VMEM)
-    strip = jax.ShapeDtypeStruct((7, TILE, 256), BF16)
-    return pl.pallas_call(
-        edge_kernel,
-        out_shape=(strip, strip),
-        in_specs=[pl.BlockSpec(memory_space=pl.ANY)] * 3,
-        out_specs=(vmem, vmem),
-        scratch_shapes=[
-            pltpu.VMEM((4, TILE, 256), BF16),
-            pltpu.VMEM((10, 2 * TILE, 128), BF16),
-            pltpu.VMEM((10, 2 * TILE, 128), F32),
-            pltpu.SemaphoreType.DMA((6,)),
-        ],
-        compiler_params=pltpu.CompilerParams(vmem_limit_bytes=EDGE_LIMIT),
-    )(bottom_in, skip_feat, cotangent)
-
-
-def split_kernel(bot, skip, cot, out_ref, wide):
-    for plane, ref in ((1, cot), (3, skip)):
         wide[...] = ref[...].astype(F32)
         for col_par in range(2):
             part = wide[:, pl.ds(col_par, TILE, stride=2), :].astype(BF16)
             part = part.reshape(TILE, 2, TILE, 128)
             lanes = slice(col_par * 128, col_par * 128 + 128)
-            out_ref[plane, :, :, lanes] = part[:, 0]
-            out_ref[plane + 1, :, :, lanes] = part[:, 1]
-    out_ref[0] = bot[...]
+            z[plane, :, :, lanes] = part[:, 0]
+            z[plane + 1, :, :, lanes] = part[:, 1]
+    copies[2].wait()
+    z[0] = bot[...]
+
+    even = is_even("row")
+    for plane in range(3):
+        two = slice(2 * plane, 2 * plane + 2)
+        inner[two], outer[two] = both(even, z[plane, 0:2], z[plane, TILE - 2 : TILE])
+    inner[6], outer[6] = both(even, z[3, 0], z[4, TILE - 1])
+    outs = [
+        pltpu.make_async_copy(src, dst, out_sems.at[i])
+        for i, (src, dst) in enumerate(
+            (
+                (inner, inner_hbm),
+                (outer, outer_hbm),
+                (z, z_hbm),
+                (own, own_hbm),
+            )
+        )
+    ]
+    for copy in outs[:3]:
+        copy.start()
+
+    even = is_even("col")
+    own[...] = jnp.zeros((2, COLUMNS, 2, 256), BF16)
+    for plane in range(3):
+        rows = slice(EXT * plane + 2, EXT * plane + 2 + TILE)
+        x = z[plane].astype(F32)
+        own[0, rows], own[1, rows] = both(even, x[:, 0:2], x[:, TILE - 2 : TILE])
+    x, y = z[3].astype(F32), z[4].astype(F32)
+    rows = slice(3 * EXT + 1, 3 * EXT + 1 + TILE)
+    own[0, rows], own[1, rows] = both(
+        even, pair_of(x[:, 0:1], y[:, 0:1]), pair_of(x[:, TILE - 1 : TILE], y[:, TILE - 1 : TILE])
+    )
+    for copy in outs[3:]:
+        copy.start()
+    for copy in outs:
+        copy.wait()
 
 
 def split(bottom_in, skip_feat, cotangent):
-    vmem = pl.BlockSpec(memory_space=pltpu.VMEM)
+    anywhere = pl.BlockSpec(memory_space=pl.ANY)
+    fine = (2 * TILE, 2 * TILE, 128)
+    shapes = ((5, TILE, TILE, 256),) + ((7, TILE, 256),) * 2 + ((2, COLUMNS, 2, 256),)
     return pl.pallas_call(
         split_kernel,
-        out_shape=jax.ShapeDtypeStruct((5, TILE, TILE, 256), BF16),
+        out_shape=tuple(jax.ShapeDtypeStruct(shape, BF16) for shape in shapes),
+        in_specs=[anywhere] * 3,
+        out_specs=(anywhere,) * len(shapes),
+        scratch_shapes=[
+            pltpu.VMEM((TILE, TILE, 256), BF16),
+            pltpu.VMEM(fine, BF16),
+            pltpu.VMEM(fine, BF16),
+            pltpu.VMEM(fine, F32),
+        ]
+        + [pltpu.VMEM(shape, BF16) for shape in shapes]
+        + [pltpu.SemaphoreType.DMA((3,)), pltpu.SemaphoreType.DMA((len(shapes),))],
+        compiler_params=pltpu.CompilerParams(vmem_limit_bytes=FIRST_LIMIT),
+    )(bottom_in, skip_feat, cotangent)
+
+
+def ends_kernel(own, got_inner, got_outer, inner_ref, outer_ref):
+    inner_ref[...] = own[1]
+    outer_ref[...] = own[0]
+    got = got_inner[...].astype(F32), got_outer[...].astype(F32)
+    even = is_even("row")
+    up, down = jnp.where(even, got[1], got[0]), jnp.where(even, got[0], got[1])
+    even = is_even("col")
+    for plane in range(3):
+        for x, at in ((up, EXT * plane), (down, EXT * plane + 2 + TILE)):
+            x = x[2 * plane : 2 * plane + 2]
+            inner_ref[at : at + 2], outer_ref[at : at + 2] = both(
+                even, x[:, 0:2], x[:, TILE - 2 : TILE]
+            )
+    zero = jnp.zeros((1, 1, 256), F32)
+    x, at = up[6:7], slice(3 * EXT, 3 * EXT + 1)
+    inner_ref[at], outer_ref[at] = both(
+        even, pair_of(zero, x[:, 0:1]), pair_of(zero, x[:, TILE - 1 : TILE])
+    )
+    x, at = down[6:7], slice(3 * EXT + 17, 3 * EXT + 18)
+    inner_ref[at], outer_ref[at] = both(
+        even, pair_of(x[:, 0:1], zero), pair_of(x[:, TILE - 1 : TILE], zero)
+    )
+
+
+def with_ends(*strips):
+    vmem = pl.BlockSpec(memory_space=pltpu.VMEM)
+    shape = jax.ShapeDtypeStruct((COLUMNS, 2, 256), BF16)
+    return pl.pallas_call(
+        ends_kernel,
+        out_shape=(shape, shape),
         in_specs=[vmem] * 3,
-        out_specs=vmem,
-        scratch_shapes=[pltpu.VMEM((2 * TILE, 2 * TILE, 128), F32)],
-        compiler_params=pltpu.CompilerParams(vmem_limit_bytes=16 << 20),
-    )(bottom_in, skip_feat, cotangent)
+        out_specs=(vmem, vmem),
+        compiler_params=pltpu.CompilerParams(vmem_limit_bytes=8 << 20),
+        cost_estimate=pl.CostEstimate(flops=0, bytes_accessed=20000000, transcendentals=0),
+    )(*strips)
 
 
 def nn(a, b):
@@ -179,7 +232,7 @@
 
 
 def main_kernel(
-    scale, pos_ref, z_ref, up_ref, down_ref, lo_ref, hi_ref, bk_ref, uk_ref, flip_ref,
+    scale, pos_ref, z_ref, row_in, row_out, col_in, col_out, bk_ref, uk_ref, flip_ref,
     mix4c, pg3c, keep_ref, send_ref,
     ext, bot3, botc, act3, actc, dsilu, cot4, mg4, mg4c, pgc, packed, sems,
 ):
@@ -189,24 +242,32 @@
     image_w = pos_ref[3]
     mine = pos_ref[4]
 
+    def before_behind(inner, outer, even):
+        inner, outer = inner.astype(F32), outer.astype(F32)
+        return jnp.where(even, outer, inner), jnp.where(even, inner, outer)
+
     core = slice(CORE, CORE + TILE)
+    low, high = slice(CORE - 2, CORE), slice(CORE + TILE, CORE + TILE + 2)
+    even_row, even_col = is_even("row"), is_even("col")
     ext[...] = jnp.zeros_like(ext)
-    ext[:, 2 : 2 + TILE, core, :] = z_ref[...].astype(F32)
+    for plane in range(5):
+        ext[plane, 2 : 2 + TILE, core, :] = z_ref[4 - plane].astype(F32)
     for plane in range(3):
         two = slice(2 * plane, 2 * plane + 2)
-        ext[plane, 0:2, core, :] = up_ref[two].astype(F32)
-        ext[plane, 2 + TILE : EXT, core, :] = down_ref[two].astype(F32)
+        ext[plane, 0:2, core, :], ext[plane, 2 + TILE : EXT, core, :] = before_behind(
+            row_in[two], row_out[two], even_row
+        )
         side = slice(EXT * plane, EXT * plane + EXT)
-        ext[plane, :, CORE - 2 : CORE, :] = lo_ref[side].astype(F32)
-        ext[plane, :, CORE + TILE : CORE + TILE + 2, :] = hi_ref[side].astype(F32)
-    ext[4, 1, core, :] = up_ref[6].astype(F32)
-    ext[3, 2 + TILE, core, :] = down_ref[6].astype(F32)
+        ext[plane, :, low, :], ext[plane, :, high, :] = before_behind(
+            col_in[side], col_out[side], even_col
+        )
+    ext[4, 1, core, :], ext[3, 2 + TILE, core, :] = before_behind(row_in[6], row_out[6], even_row)
+    low, high = slice(CORE - 1, CORE), slice(CORE + TILE, CORE + TILE + 1)
     for par in range(2):
         side = slice(3 * EXT, 3 * EXT + 18)
-        ext[3 + par, 1:19, CORE - 1 : CORE, :] = lo_ref[side, par : par + 1].astype(F32)
-        ext[3 + par, 1:19, CORE + TILE : CORE + TILE + 1, :] = hi_ref[
-            side, par : par + 1
-        ].astype(F32)
+        ext[3 + par, 1:19, low, :], ext[3 + par, 1:19, high, :] = before_behind(
+            col_in[side, par : par + 1], col_out[side, par : par + 1], even_col
+        )
 
     def masked(x, first):
         rows = x.shape[0] // PITCH
@@ -282,7 +343,7 @@
     agrad = jnp.zeros((18 * PITCH, 256), F32)
     for a in range(4):
         src, shift = fine_row(a - 1)
-        weight = jnp.concatenate([uk_ref[a, b] for b in range(4)], axis=1)
+        weight = jnp.concatenate([uk_ref[a, 3 - b] for b in range(4)], axis=1)
         agrad = agrad + nt(flat(mg4[src, 1 + shift : 19 + shift]), weight)
     pgrad = masked((agrad * dsilu[...]).astype(BF16).astype(F32), 1)
     for b, part in enumerate(three(pgrad)):
@@ -298,7 +359,7 @@
     for par in range(2):
         total = flat(ext[3 + par, 1:19])
         for row_k, shift in (((1, 0), (3, -1)), ((0, 1), (2, 0)))[par]:
-            k = [uk_ref[row_k, b] for b in range(4)]
+            k = [uk_ref[row_k, 3 - b] for b in range(4)]
             none = jnp.zeros((256, 128), BF16)
             weight = jnp.concatenate(
                 [
@@ -319,7 +380,7 @@
         for par in range(2):
             src, shift = fine_row(par + a - 1)
             prod = prod + tn(
-                flat(mix4c[src, 1 + shift : 17 + shift]), flat(z_ref[1 + par])
+                flat(mix4c[src, 1 + shift : 17 + shift]), flat(z_ref[3 - par])
             )
         for b in range(3):
             tap = prod[128 * b : 128 * b + 128, :128] + prod[128 * b + 128 : 128 * b + 256, 128:]
@@ -454,10 +515,7 @@
 
 
 def swapped(inner, outer, axis):
-    got_inner = lax.ppermute(inner, axis, INNER_PAIRS)
-    got_outer = lax.ppermute(outer, axis, OUTER_PAIRS)
-    even = lax.rem(lax.axis_index(axis), 2) == 0
-    return jnp.where(even, got_outer, got_inner), jnp.where(even, got_inner, got_outer)
+    return lax.ppermute(inner, axis, INNER_PAIRS), lax.ppermute(outer, axis, OUTER_PAIRS)
 
 
 def exchange(x, groups):
@@ -478,36 +536,18 @@
 def on_device(bottom_in, skip_feat, cotangent, bot_kernel, up_kernel, lvl_kernel):
     rows, cols = lax.axis_size("row"), lax.axis_size("col")
     scale = 1.0 / float(2 * TILE * rows * 2 * TILE * cols) ** 0.5
-    inner, outer = edges(bottom_in, skip_feat, cotangent)
-    inner, outer, *fields = lax.optimization_barrier(
-        (inner, outer, bottom_in, skip_feat, cotangent)
-    )
-    z = split(*fields)
-    up, down = swapped(inner, outer, "row")
-
-    def side(cols, skip_col):
-        parts = [
-            jnp.concatenate(
-                [up[2 * p : 2 * p + 2, cols], z[p, :, cols], down[2 * p : 2 * p + 2, cols]], axis=0
-            )
-            for p in range(3)
-        ]
-        blank = jnp.zeros((1, 1, 256), BF16)
-        even = jnp.concatenate([blank, z[3, :, skip_col], down[6:7, skip_col]], axis=0)
-        odd = jnp.concatenate([up[6:7, skip_col], z[4, :, skip_col], blank], axis=0)
-        return jnp.concatenate(parts + [jnp.concatenate([even, odd], axis=1)], axis=0)
-
-    last = side(slice(TILE - 2, TILE), slice(TILE - 1, TILE))
-    first = side(slice(0, 2), slice(0, 1))
-    even = lax.rem(lax.axis_index("col"), 2) == 0
-    lo, hi = swapped(jnp.where(even, last, first), jnp.where(even, first, last), "col")
+    z, inner, outer, own = split(bottom_in, skip_feat, cotangent)
+    row_strips = swapped(inner, outer, "row")
+    row_strips, z, turned = lax.optimization_barrier((row_strips, z, up_kernel))
+    z, turned = z[::-1], turned[:, ::-1]
+    col_strips = swapped(*with_ends(own[::-1], *row_strips), "col")
     row = lax.axis_index("row")
     pos = jnp.stack(
         [row, lax.axis_index("col"), jnp.int32(TILE * rows), jnp.int32(TILE * cols), row % 2]
     ).astype(jnp.int32)
     flip = lvl_kernel[::-1, ::-1]
     mix4c, pg3c, keep, send = local_work(
-        scale, pos, z, up, down, lo, hi, bot_kernel, up_kernel, flip
+        scale, pos, z, *row_strips, *col_strips, bot_kernel, turned, flip
     )
     rest = rest_work(mix4c, pg3c, bot_kernel, lvl_kernel)
     half, other, (level_out, bottom_grad) = total_over_devices(keep, send, rest)

time: 106 us -> 106 us (level)
  starting transfers between devices: 13.3 us -> 10.8 us
  waiting for transfers between devices: 2.75 us -> 4.84 us
  other arithmetic: 2.11 us -> 0.63 us
  Pallas kernels: 16 us -> 17.1 us
    unnamed x21 -> x6, local copies, waits for them, and re-layouts: 3.02 us -> 0.02 us
    rev x0 -> x3, local copies, waits for them, and re-layouts: none -> 2.47 us  [the longest x2 1.45 us: on_device(): z, turned = (z[::-1], turned[:, ::-1])]
    ppermute x4, waiting for transfers between devices: 1.23 us -> 2.97 us  [the longest x2 1.74 us: swapped(): lax.ppermute(outer, axis, OUTER_PAIRS)]
    ppermute x1, starting transfers between devices: 1.76 us -> 0.09 us  [total_over_devices(): lax.ppermute(send, 'row', CORE_SWAP)]
    select_n x3 -> x0, other arithmetic: 1.25 us -> none  [the longest x2 1.12 us: swapped(): jnp.where(even, got_inner, got_outer)]
    pallas_call x2, Pallas kernels: 1.73 us -> 2.85 us  [the longest x1 2.16 us: split(): pl.pallas_call(split_kernel, out_shape=tuple((jax.ShapeDtypeStruct(shape,...]
  transfers between devices with their start and end apart: 6 -> 6, of which waited for: 3 -> 4; matrix products, arithmetic and copies ran while one was open for 0% -> 3% of each run, Pallas kernels for 4% -> 4%
where the time goes in v6:
time: 106 us; the launch traced here: 105 us
  blocking collectives  67.5 us (64%)
  Pallas kernels  17.1 us (16%)
  starting transfers between devices  10.8 us (10%)
  waiting for transfers between devices  4.84 us (5%)
  local copies, waits for them, and re-layouts  3.67 us (3%)
    all_to_all x3, blocking collectives, exchange(): return lax.all_to_all(x, AXES, 0, 0, axis_index_groups=groups)  67.5 us
    pallas_call x1, Pallas kernels, local_work(): pl.pallas_call(functools.partial(main_kernel, scale), out_shape=tuple((ja...  8.43 us
    ppermute x1, starting transfers between devices, total_over_devices(): return (half, lax.ppermute(half, 'row', CORE_SWAP), rest)  4.86 us
    pallas_call x2, Pallas kernels, unpack(): pl.pallas_call(functools.partial(unpack_kernel, 1 if begun else 0), out_s...  4.16 us
    ppermute x2, starting transfers between devices, swapped(): lax.ppermute(inner, axis, INNER_PAIRS)  3.33 us
    ppermute x2, starting transfers between devices, swapped(): lax.ppermute(outer, axis, OUTER_PAIRS)  2.56 us
    pallas_call x1, Pallas kernels, split(): pl.pallas_call(split_kernel, out_shape=tuple((jax.ShapeDtypeStruct(shape,...  2.16 us
  transfers between devices with their start and end apart: 6, of which 4 were waited for; matrix products, arithmetic and copies ran while one was open for 3% of the time, Pallas kernels for 4%

profile of v6, /device:TPU:1, one launch (start us, length us, event | category | flops | bytes accessed | tf_op | source)
XLA Modules:
  0.0 105.5 jit_solution(13133850544004748733)
XLA Ops:
  0.6 2.2 %shard_map.101 = (bf16[5,16,16,256]{3,2,1,0:T(8,128)(2,1)}, bf16[7,16,256]{2,1,0:T(8,128)(2,1)}, bf16[7,16,256]{2,1,0:T(8,128)(2,1)}, bf16[2,78,2,256]{3,2,1,0:T(2,128)(2,1)}) custom-call(bf16[16,16,256]{2,1,0:T(8,128)(2,1)} %bot_hbm.1, bf16[32,32,128]{2,1,0:T(8,128)(2,1)} %skip_hbm.1, bf16[32,32,128]{2,1,0:T(8,128)(2,1)} %cot_hbm.1), custom_call_target="tpu_custom_call" | custom-call | tf_op jit(solution)/shard_map/pallas_call | solution.py:127
  2.8 3.3 %collective-permute-start = (bf16[7,16,256]{2,1,0:T(8,128)(2,1)}, bf16[7,16,256]{2,1,0:T(8,128)(2,1)S(1)}, u32[]{:S(2)}, u32[]{:S(2)}) collective-permute-start(bf16[7,16,256]{2,1,0:T(8,128)(2,1)} %get-tuple-element.30), channel_id=1, source_target_pairs={{0,16},{16,0},{32,48},{48,32},{64,80},{80,64},{96,112},{112,96},{1... | collective-permute-start | bytes 172040 | tf_op jit(solution)/shard_map/ppermute | solution.py:518
  6.1 1.9 %collective-permute-start.1 = (bf16[7,16,256]{2,1,0:T(8,128)(2,1)}, bf16[7,16,256]{2,1,0:T(8,128)(2,1)S(1)}, u32[]{:S(2)}, u32[]{:S(2)}) collective-permute-start(bf16[7,16,256]{2,1,0:T(8,128)(2,1)} %get-tuple-element.31), channel_id=1, source_target_pairs={{16,32},{32,16},{48,64},{64,48},{80,96},{96,80},{112,128},{128,112... | collective-permute-start | bytes 172040 | tf_op jit(solution)/shard_map/ppermute | solution.py:518
  8.1 1.0 rev.15.flip_ref
  9.0 1.0 rev.13.own
  10.1 1.7 %collective-permute-done.1.got_outer.row_out = bf16[7,16,256]{2,1,0:T(8,128)(2,1)S(1)} collective-permute-done((bf16[7,16,256]{2,1,0:T(8,128)(2,1)}, bf16[7,16,256]{2,1,0:T(8,128)(2,1)S(1)}, u32[]{:S(2)}, u32[]{:S(2)}) %collective-permute-start.1) | collective-permute-done | bytes 57376 | tf_op jit(solution)/shard_map/ppermute | solution.py:518
  11.8 0.7 shard_map.102
  12.5 0.7 collective-permute-start.3
  13.4 1.4 %rev.14.uk_ref = bf16[4,4,256,128]{3,2,1,0:T(8,128)(2,1)S(1)} reverse(bf16[4,4,256,128]{3,2,1,0:T(8,128)(2,1)} %param.10), dimensions={1} | reverse | bytes 2097152 | tf_op jit(solution)/shard_map/rev | solution.py:542
  14.8 1.2 %collective-permute-done.2.col_in = bf16[78,2,256]{2,1,0:T(2,128)(2,1)S(1)} collective-permute-done((bf16[78,2,256]{2,1,0:T(2,128)(2,1)}, bf16[78,2,256]{2,1,0:T(2,128)(2,1)S(1)}, u32[]{:S(2)}, u32[]{:S(2)}) %collective-permute-start.2) | collective-permute-done | bytes 79904 | tf_op jit(solution)/shard_map/ppermute | solution.py:518
  16.0 8.4 %shard_map.103 = (bf16[2,18,16,512]{3,2,1,0:T(8,128)(2,1)S(1)}, bf16[18,16,768]{2,1,0:T(8,128)(2,1)S(1)}, bf16[5120,128]{1,0:T(8,128)(2,1)S(1)}, bf16[5120,128]{1,0:T(8,128)(2,1)S(1)}) custom-call(s32[5]{0:T(128)S(1)} %pad_add_fusion.pos_ref, bf16[5,16,16,256]{3,2,1,0:T(8,128)(2,1)S(1)} %rev.12.z_ref, ...), custom_call_target="tpu_custom_call" | custom-call | tf_op jit(solution)/shard_map/pallas_call | solution.py:442
  24.5 0.1 collective-permute-start.4
  24.6 1.7 %shard_map.104 = (bf16[32,32,128]{2,1,0:T(8,128)(2,1)}, bf16[16,16,256]{2,1,0:T(8,128)(2,1)}) custom-call(bf16[2,18,16,512]{3,2,1,0:T(8,128)(2,1)S(1)} %get-tuple-element.41.mix4c, bf16[18,16,768]{2,1,0:T(8,128)(2,1)S(1)} %get-tuple-element.42.pg3c, bf16[3,3,256,256]{3,2,1,0:T(8,128)(2,1)S(1)} %copy-done, bf16[3,3,128,128]{3,2,1,0:T(8,128)(2,1)S(1)} %copy-done.1), custom_call_target="tpu_custom_call" | custom-call | flops 1000000000 | bytes 3000000 | tf_op jit(solution)/shard_map/pallas_call | solution.py:424
  26.3 1.3 %collective-permute-done.4 = bf16[5120,128]{1,0:T(8,128)(2,1)S(1)} collective-permute-done((bf16[5120,128]{1,0:T(8,128)(2,1)S(1)}, bf16[5120,128]{1,0:T(8,128)(2,1)S(1)}, u32[]{:S(2)}, u32[]{:S(2)}) %collective-permute-start.4) | collective-permute-done | bytes 1310752 | tf_op jit(solution)/shard_map/ppermute | solution.py:526
  27.6 0.3 add_convert_fusion
  27.9 31.5 %all_to_all.15 = bf16[32,160,128]{2,1,0:T(8,128)(2,1)S(1)} all-to-all(bf16[32,160,128]{2,1,0:T(8,128)(2,1)S(1)} %bitcast.10), channel_id=1, replica_groups={{0,1,128,129,32,33,160,161,64,65,192,193,96,97,224,225,2,3,130,131,34,3..., dimensions={0} | all-to-all | bytes 2621440 | tf_op jit(solution)/shard_map/all_to_all | solution.py:522
  59.4 0.2 reduce_sum.24
  59.6 16.0 %all_to_all.16 = bf16[4,160,128]{2,1,0:T(8,128)(2,1)S(1)} all-to-all(bf16[4,160,128]{2,1,0:T(8,128)(2,1)S(1)} %broadcast_in_dim.4), channel_id=1, replica_groups={{0,4,8,12},{16,20,24,28},{1,5,9,13},{17,21,25,29},{128,132,136,140},{14..., dimensions={0} | all-to-all | bytes 327680 | tf_op jit(solution)/shard_map/all_to_all | solution.py:522
  75.7 0.2 broadcast_in_dim.5
  75.9 20.0 %all_to_all.17 = bf16[32,160,128]{2,1,0:T(8,128)(2,1)S(1)} all-to-all(bf16[32,160,128]{2,1,0:T(8,128)(2,1)S(1)} %broadcast_in_dim.5), channel_id=1, replica_groups={{0,1,128,129,32,33,160,161,64,65,192,193,96,97,224,225,2,3,130,131,34,3..., dimensions={0} | all-to-all | bytes 2621440 | tf_op jit(solution)/shard_map/all_to_all | solution.py:522
  95.9 4.9 %collective-permute-start.5 = (bf16[5120,128]{1,0:T(8,128)(2,1)S(1)}, bf16[5120,128]{1,0:T(8,128)(2,1)S(1)}, u32[]{:S(2)}, u32[]{:S(2)}) collective-permute-start(bf16[5120,128]{1,0:T(8,128)(2,1)S(1)} %bitcast.8), channel_id=1, source_target_pairs={{0,16},{16,0},{32,48},{48,32},{64,80},{80,64},{96,112},{112,96},{1... | collective-permute-start | bytes 3932168 | tf_op jit(solution)/shard_map/ppermute | solution.py:533
  100.7 2.1 %shard_map.105 = (f32[4096,128]{1,0:T(8,128)}, f32[2304,256]{1,0:T(8,128)}, f32[1152,128]{1,0:T(8,128)}) custom-call(s32[5]{0:T(128)S(1)} %pad_add_fusion.pos_ref, bf16[5120,128]{1,0:T(8,128)(2,1)S(1)} %bitcast.9), custom_call_target="tpu_custom_call" | custom-call | bytes 4000000 | tf_op jit(solution)/shard_map/pallas_call | solution.py:504
  102.9 0.6 collective-permute-done.5.half
  103.4 2.1 %shard_map.106 = (f32[4096,128]{1,0:T(8,128)}, f32[2304,256]{1,0:T(8,128)}, f32[1152,128]{1,0:T(8,128)}) custom-call(s32[5]{0:T(128)S(1)} %pad_add_fusion.pos_ref, bf16[5120,128]{1,0:T(8,128)(2,1)S(1)} %collective-permute-done.5.half, f32[4096,128]{1,0:T(8,128)} %get-tuple-element.49.refs_0_, ...), custom_call_target="tpu_custom_call", output_to_operand_aliasing={{0}: (2, {}), {1}: (3, {}), {2}: (4, {})} | custom-call | bytes 4000000 | tf_op jit(solution)/shard_map/pallas_call | solution.py:504
  (14 shorter events, 0.2 us)
Async XLA Ops:
  2.8 10.5 %copy-start.2 = (bf16[5,16,16,256]{3,2,1,0:T(8,128)(2,1)S(1)}, bf16[5,16,16,256]{3,2,1,0:T(8,128)(2,1)}, u32[]{:S(2)}) copy-start(bf16[5,16,16,256]{3,2,1,0:T(8,128)(2,1)} %get-tuple-element.33) | copy-start | bytes 1966084
  2.8 7.3 %collective-permute-start = (bf16[7,16,256]{2,1,0:T(8,128)(2,1)}, bf16[7,16,256]{2,1,0:T(8,128)(2,1)S(1)}, u32[]{:S(2)}, u32[]{:S(2)}) collective-permute-start(bf16[7,16,256]{2,1,0:T(8,128)(2,1)} %get-tuple-element.30), channel_id=1, source_target_pairs={{0,16},{16,0},{32,48},{48,32},{64,80},{80,64},{96,112},{112,96},{1... | collective-permute-start | bytes 172040 | tf_op jit(solution)/shard_map/ppermute | solution.py:518
  6.1 5.7 %collective-permute-start.1 = (bf16[7,16,256]{2,1,0:T(8,128)(2,1)}, bf16[7,16,256]{2,1,0:T(8,128)(2,1)S(1)}, u32[]{:S(2)}, u32[]{:S(2)}) collective-permute-start(bf16[7,16,256]{2,1,0:T(8,128)(2,1)} %get-tuple-element.31), channel_id=1, source_target_pairs={{16,32},{32,16},{48,64},{64,48},{80,96},{96,80},{112,128},{128,112... | collective-permute-start | bytes 172040 | tf_op jit(solution)/shard_map/ppermute | solution.py:518
  12.5 3.5 %collective-permute-start.2 = (bf16[78,2,256]{2,1,0:T(2,128)(2,1)}, bf16[78,2,256]{2,1,0:T(2,128)(2,1)S(1)}, u32[]{:S(2)}, u32[]{:S(2)}) collective-permute-start(bf16[78,2,256]{2,1,0:T(2,128)(2,1)} %get-tuple-element.37), channel_id=1, source_target_pairs={{0,1},{1,0},{2,3},{3,2},{4,5},{5,4},{6,7},{7,6},{8,9},{9,8},{10,11... | collective-permute-start | bytes 239624 | tf_op jit(solution)/shard_map/ppermute | solution.py:518
  12.5 3.5 %collective-permute-start.3 = (bf16[78,2,256]{2,1,0:T(2,128)(2,1)S(1)}, bf16[78,2,256]{2,1,0:T(2,128)(2,1)S(1)}, u32[]{:S(2)}, u32[]{:S(2)}) collective-permute-start(bf16[78,2,256]{2,1,0:T(2,128)(2,1)S(1)} %get-tuple-element.38), channel_id=1, source_target_pairs={{1,2},{2,1},{3,4},{4,3},{5,6},{6,5},{7,8},{8,7},{9,10},{10,9},{11,... | collective-permute-start | bytes 239624 | tf_op jit(solution)/shard_map/ppermute | solution.py:518
  13.3 2.7 %copy-start = (bf16[3,3,256,256]{3,2,1,0:T(8,128)(2,1)S(1)}, bf16[3,3,256,256]{3,2,1,0:T(8,128)(2,1)}, u32[]{:S(2)}) copy-start(bf16[3,3,256,256]{3,2,1,0:T(8,128)(2,1)} %bk_ref.3) | copy-start | bytes 3538948
  14.8 9.8 %copy-start.1 = (bf16[3,3,128,128]{3,2,1,0:T(8,128)(2,1)S(1)}, bf16[3,3,128,128]{3,2,1,0:T(8,128)(2,1)}, u32[]{:S(2)}) copy-start(bf16[3,3,128,128]{3,2,1,0:T(8,128)(2,1)} %lk_ref.1) | copy-start | bytes 884740
  24.5 3.1 %collective-permute-start.4 = (bf16[5120,128]{1,0:T(8,128)(2,1)S(1)}, bf16[5120,128]{1,0:T(8,128)(2,1)S(1)}, u32[]{:S(2)}, u32[]{:S(2)}) collective-permute-start(bf16[5120,128]{1,0:T(8,128)(2,1)S(1)} %get-tuple-element.40), channel_id=1, source_target_pairs={{0,16},{16,0},{32,48},{48,32},{64,80},{80,64},{96,112},{112,96},{1... | collective-permute-start | bytes 3932168 | tf_op jit(solution)/shard_map/ppermute | solution.py:526
  95.9 7.5 %collective-permute-start.5 = (bf16[5120,128]{1,0:T(8,128)(2,1)S(1)}, bf16[5120,128]{1,0:T(8,128)(2,1)S(1)}, u32[]{:S(2)}, u32[]{:S(2)}) collective-permute-start(bf16[5120,128]{1,0:T(8,128)(2,1)S(1)} %bitcast.8), channel_id=1, source_target_pairs={{0,16},{16,0},{32,48},{48,32},{64,80},{80,64},{96,112},{112,96},{1... | collective-permute-start | bytes 3932168 | tf_op jit(solution)/shard_map/ppermute | solution.py:533

commit v7 on v6

--- a/solution.py
+++ b/solution.py
@@ -25,21 +25,12 @@
     return row * 16 + col
 
 
-BLOCK = 32
-BLOCK_GROUPS = [
-    [place(x, y, z + dz, core) for dz in range(2) for x in range(4) for y in range(4)]
-    for z in range(0, 8, 2)
-    for core in range(2)
-]
-
-
-PAIR_GROUPS = [
-    [place(x, y, z + dz, core) for z in range(0, 8, 2)]
-    for dz in range(2)
-    for x in range(4)
-    for y in range(4)
-    for core in range(2)
-]
+LINE = 4
+LINE_GROUPS = [[place(x, y, z, 0) for x in range(4)] for y in range(4) for z in range(8)]
+LINE_GROUPS += [[place(x, y, z, 1) for y in range(4)] for x in range(4) for z in range(8)]
+SHEET = 32
+SHEET_GROUPS = [[place(x, y, z, 0) for y in range(4) for z in range(8)] for x in range(4)]
+SHEET_GROUPS += [[place(x, y, z, 1) for x in range(4) for z in range(8)] for y in range(4)]
 CORE_SWAP = [(i, i ^ 1) for i in range(16)]
 INNER_PAIRS = CORE_SWAP
 OUTER_PAIRS = [pair for i in range(1, 15, 2) for pair in ((i, i + 1), (i + 1, i))]
@@ -525,11 +516,12 @@
 def total_over_devices(keep, send, rest):
     got, rest = lax.optimization_barrier((lax.ppermute(send, "row", CORE_SWAP), rest))
     half = (keep.astype(F32) + got.astype(F32)).astype(BF16)
-    parts = exchange(half.reshape(BLOCK, HALF // BLOCK, 128), BLOCK_GROUPS)
-    part = jnp.sum(parts.astype(F32), axis=0).astype(BF16)
-    pairs = exchange(jnp.broadcast_to(part[None], (4,) + part.shape), PAIR_GROUPS)
-    total = jnp.sum(pairs.astype(F32), axis=0).astype(BF16)
-    half = exchange(jnp.broadcast_to(total[None], parts.shape), BLOCK_GROUPS).reshape(HALF, 128)
+    for groups, count in ((LINE_GROUPS, LINE), (SHEET_GROUPS, SHEET)):
+        parts = exchange(half.reshape(count, -1, 128), groups)
+        half = jnp.sum(parts.astype(F32), axis=0).astype(BF16)
+    for groups, count in ((SHEET_GROUPS, SHEET), (LINE_GROUPS, LINE)):
+        copies = jnp.broadcast_to(half[None], (count,) + half.shape)
+        half = exchange(copies, groups).reshape(-1, 128)
     return half, lax.ppermute(half, "row", CORE_SWAP), rest
 
 

time: 106 us -> 112 us (1.057)
  blocking collectives: 67.5 us -> 73 us
    all_to_all x3 -> x4, blocking collectives: 67.5 us -> 73 us  [exchange(): return lax.all_to_all(x, AXES, 0, 0, axis_index_groups=groups)]
  transfers between devices with their start and end apart: 6 -> 6, of which waited for: 4 -> 4; matrix products, arithmetic and copies ran while one was open for 3% -> 3% of each run, Pallas kernels for 4% -> 3%
where the time goes in v7:
time: 112 us; the launch traced here: 111 us
  blocking collectives  73 us (65%)
  Pallas kernels  17.1 us (15%)
  starting transfers between devices  10.9 us (10%)
  waiting for transfers between devices  4.84 us (4%)
  local copies, waits for them, and re-layouts  3.69 us (3%)
    all_to_all x4, blocking collectives, exchange(): return lax.all_to_all(x, AXES, 0, 0, axis_index_groups=groups)  73 us
    pallas_call x1, Pallas kernels, local_work(): pl.pallas_call(functools.partial(main_kernel, scale), out_shape=tuple((ja...  8.43 us
    ppermute x1, starting transfers between devices, total_over_devices(): return (half, lax.ppermute(half, 'row', CORE_SWAP), rest)  4.87 us
    pallas_call x2, Pallas kernels, unpack(): pl.pallas_call(functools.partial(unpack_kernel, 1 if begun else 0), out_s...  4.16 us
    ppermute x2, starting transfers between devices, swapped(): lax.ppermute(inner, axis, INNER_PAIRS)  3.33 us
    ppermute x2, starting transfers between devices, swapped(): lax.ppermute(outer, axis, OUTER_PAIRS)  2.56 us
  transfers between devices with their start and end apart: 6, of which 4 were waited for; matrix products, arithmetic and copies ran while one was open for 3% of the time, Pallas kernels for 3%

profile of v7, /device:TPU:1, one launch (start us, length us, event | category | flops | bytes accessed | tf_op | source)
XLA Modules:
  0.0 111.2 jit_solution(13001081771884024615)
XLA Ops:
  0.6 2.2 %shard_map.101 = (bf16[5,16,16,256]{3,2,1,0:T(8,128)(2,1)}, bf16[7,16,256]{2,1,0:T(8,128)(2,1)}, bf16[7,16,256]{2,1,0:T(8,128)(2,1)}, bf16[2,78,2,256]{3,2,1,0:T(2,128)(2,1)}) custom-call(bf16[16,16,256]{2,1,0:T(8,128)(2,1)} %bot_hbm.1, bf16[32,32,128]{2,1,0:T(8,128)(2,1)} %skip_hbm.1, bf16[32,32,128]{2,1,0:T(8,128)(2,1)} %cot_hbm.1), custom_call_target="tpu_custom_call" | custom-call | tf_op jit(solution)/shard_map/pallas_call | solution.py:118
  2.8 3.3 %collective-permute-start = (bf16[7,16,256]{2,1,0:T(8,128)(2,1)}, bf16[7,16,256]{2,1,0:T(8,128)(2,1)S(1)}, u32[]{:S(2)}, u32[]{:S(2)}) collective-permute-start(bf16[7,16,256]{2,1,0:T(8,128)(2,1)} %get-tuple-element.30), channel_id=1, source_target_pairs={{0,16},{16,0},{32,48},{48,32},{64,80},{80,64},{96,112},{112,96},{1... | collective-permute-start | bytes 172040 | tf_op jit(solution)/shard_map/ppermute | solution.py:509
  6.1 1.9 %collective-permute-start.1 = (bf16[7,16,256]{2,1,0:T(8,128)(2,1)}, bf16[7,16,256]{2,1,0:T(8,128)(2,1)S(1)}, u32[]{:S(2)}, u32[]{:S(2)}) collective-permute-start(bf16[7,16,256]{2,1,0:T(8,128)(2,1)} %get-tuple-element.31), channel_id=1, source_target_pairs={{16,32},{32,16},{48,64},{64,48},{80,96},{96,80},{112,128},{128,112... | collective-permute-start | bytes 172040 | tf_op jit(solution)/shard_map/ppermute | solution.py:509
  8.1 1.0 rev.15.flip_ref
  9.0 1.0 rev.13.own
  10.1 1.7 %collective-permute-done.1.got_outer.row_out = bf16[7,16,256]{2,1,0:T(8,128)(2,1)S(1)} collective-permute-done((bf16[7,16,256]{2,1,0:T(8,128)(2,1)}, bf16[7,16,256]{2,1,0:T(8,128)(2,1)S(1)}, u32[]{:S(2)}, u32[]{:S(2)}) %collective-permute-start.1) | collective-permute-done | bytes 57376 | tf_op jit(solution)/shard_map/ppermute | solution.py:509
  11.8 0.7 shard_map.102
  12.5 0.7 collective-permute-start.3
  13.4 1.4 %rev.14.uk_ref = bf16[4,4,256,128]{3,2,1,0:T(8,128)(2,1)S(1)} reverse(bf16[4,4,256,128]{3,2,1,0:T(8,128)(2,1)} %param.10), dimensions={1} | reverse | bytes 2097152 | tf_op jit(solution)/shard_map/rev | solution.py:534
  14.8 1.2 %collective-permute-done.2.col_in = bf16[78,2,256]{2,1,0:T(2,128)(2,1)S(1)} collective-permute-done((bf16[78,2,256]{2,1,0:T(2,128)(2,1)}, bf16[78,2,256]{2,1,0:T(2,128)(2,1)S(1)}, u32[]{:S(2)}, u32[]{:S(2)}) %collective-permute-start.2) | collective-permute-done | bytes 79904 | tf_op jit(solution)/shard_map/ppermute | solution.py:509
  16.0 8.4 %shard_map.103 = (bf16[2,18,16,512]{3,2,1,0:T(8,128)(2,1)S(1)}, bf16[18,16,768]{2,1,0:T(8,128)(2,1)S(1)}, bf16[5120,128]{1,0:T(8,128)(2,1)S(1)}, bf16[5120,128]{1,0:T(8,128)(2,1)S(1)}) custom-call(s32[5]{0:T(128)S(1)} %pad_add_fusion.pos_ref, bf16[5,16,16,256]{3,2,1,0:T(8,128)(2,1)S(1)} %rev.12.z_ref, ...), custom_call_target="tpu_custom_call" | custom-call | tf_op jit(solution)/shard_map/pallas_call | solution.py:433
  24.6 1.7 %shard_map.104 = (bf16[32,32,128]{2,1,0:T(8,128)(2,1)}, bf16[16,16,256]{2,1,0:T(8,128)(2,1)}) custom-call(bf16[2,18,16,512]{3,2,1,0:T(8,128)(2,1)S(1)} %get-tuple-element.41.mix4c, bf16[18,16,768]{2,1,0:T(8,128)(2,1)S(1)} %get-tuple-element.42.pg3c, bf16[3,3,256,256]{3,2,1,0:T(8,128)(2,1)S(1)} %copy-done, bf16[3,3,128,128]{3,2,1,0:T(8,128)(2,1)S(1)} %copy-done.1), custom_call_target="tpu_custom_call" | custom-call | flops 1000000000 | bytes 3000000 | tf_op jit(solution)/shard_map/pallas_call | solution.py:415
  26.3 1.3 %collective-permute-done.4 = bf16[5120,128]{1,0:T(8,128)(2,1)S(1)} collective-permute-done((bf16[5120,128]{1,0:T(8,128)(2,1)S(1)}, bf16[5120,128]{1,0:T(8,128)(2,1)S(1)}, u32[]{:S(2)}, u32[]{:S(2)}) %collective-permute-start.4) | collective-permute-done | bytes 1310752 | tf_op jit(solution)/shard_map/ppermute | solution.py:517
  27.6 0.3 add_convert_fusion
  27.9 21.1 %all_to_all.20 = bf16[4,1280,128]{2,1,0:T(8,128)(2,1)S(1)} all-to-all(bf16[4,1280,128]{2,1,0:T(8,128)(2,1)S(1)} %bitcast.12), channel_id=1, replica_groups={{0,32,64,96},{2,34,66,98},{4,36,68,100},{6,38,70,102},{8,40,72,104},{10..., dimensions={0} | all-to-all | bytes 2621440 | tf_op jit(solution)/shard_map/all_to_all | solution.py:513
  49.0 0.4 reduce_sum.24
  49.4 21.0 %all_to_all.21 = bf16[32,40,128]{2,1,0:T(8,128)(2,1)S(1)} all-to-all(bf16[32,40,128]{2,1,0:T(8,128)(2,1)S(1)} %bitcast.15), channel_id=1, replica_groups={{0,2,4,6,8,10,12,14,1,3,5,7,9,11,13,15,128,130,132,134,136,138,140,142,..., dimensions={0} | all-to-all | bytes 655360 | tf_op jit(solution)/shard_map/all_to_all | solution.py:513
  70.5 17.1 %all_to_all.22 = bf16[32,40,128]{2,1,0:T(8,128)(2,1)S(1)} all-to-all(bf16[32,40,128]{2,1,0:T(8,128)(2,1)S(1)} %broadcast_in_dim.6), channel_id=1, replica_groups={{0,2,4,6,8,10,12,14,1,3,5,7,9,11,13,15,128,130,132,134,136,138,140,142,..., dimensions={0} | all-to-all | bytes 655360 | tf_op jit(solution)/shard_map/all_to_all | solution.py:513
  87.5 0.2 broadcast_in_dim.15
  87.7 13.9 %all_to_all.23 = bf16[4,1280,128]{2,1,0:T(8,128)(2,1)S(1)} all-to-all(bf16[4,1280,128]{2,1,0:T(8,128)(2,1)S(1)} %broadcast_in_dim.15), channel_id=1, replica_groups={{0,32,64,96},{2,34,66,98},{4,36,68,100},{6,38,70,102},{8,40,72,104},{10..., dimensions={0} | all-to-all | bytes 2621440 | tf_op jit(solution)/shard_map/all_to_all | solution.py:513
  101.6 4.9 %collective-permute-start.5 = (bf16[5120,128]{1,0:T(8,128)(2,1)S(1)}, bf16[5120,128]{1,0:T(8,128)(2,1)S(1)}, u32[]{:S(2)}, u32[]{:S(2)}) collective-permute-start(bf16[5120,128]{1,0:T(8,128)(2,1)S(1)} %bitcast.10), channel_id=1, source_target_pairs={{0,16},{16,0},{32,48},{48,32},{64,80},{80,64},{96,112},{112,96},{1... | collective-permute-start | bytes 3932168 | tf_op jit(solution)/shard_map/ppermute | solution.py:525
  106.4 2.1 %shard_map.105 = (f32[4096,128]{1,0:T(8,128)}, f32[2304,256]{1,0:T(8,128)}, f32[1152,128]{1,0:T(8,128)}) custom-call(s32[5]{0:T(128)S(1)} %pad_add_fusion.pos_ref, bf16[5120,128]{1,0:T(8,128)(2,1)S(1)} %bitcast.11), custom_call_target="tpu_custom_call" | custom-call | bytes 4000000 | tf_op jit(solution)/shard_map/pallas_call | solution.py:495
  108.6 0.6 collective-permute-done.5.half
  109.1 2.1 %shard_map.106 = (f32[4096,128]{1,0:T(8,128)}, f32[2304,256]{1,0:T(8,128)}, f32[1152,128]{1,0:T(8,128)}) custom-call(s32[5]{0:T(128)S(1)} %pad_add_fusion.pos_ref, bf16[5120,128]{1,0:T(8,128)(2,1)S(1)} %collective-permute-done.5.half, f32[4096,128]{1,0:T(8,128)} %get-tuple-element.49.refs_0_, ...), custom_call_target="tpu_custom_call", output_to_operand_aliasing={{0}: (2, {}), {1}: (3, {}), {2}: (4, {})} | custom-call | bytes 4000000 | tf_op jit(solution)/shard_map/pallas_call | solution.py:495
  (15 shorter events, 0.4 us)
Async XLA Ops:
  2.8 10.5 %copy-start.2 = (bf16[5,16,16,256]{3,2,1,0:T(8,128)(2,1)S(1)}, bf16[5,16,16,256]{3,2,1,0:T(8,128)(2,1)}, u32[]{:S(2)}) copy-start(bf16[5,16,16,256]{3,2,1,0:T(8,128)(2,1)} %get-tuple-element.33) | copy-start | bytes 1966084
  2.8 7.3 %collective-permute-start = (bf16[7,16,256]{2,1,0:T(8,128)(2,1)}, bf16[7,16,256]{2,1,0:T(8,128)(2,1)S(1)}, u32[]{:S(2)}, u32[]{:S(2)}) collective-permute-start(bf16[7,16,256]{2,1,0:T(8,128)(2,1)} %get-tuple-element.30), channel_id=1, source_target_pairs={{0,16},{16,0},{32,48},{48,32},{64,80},{80,64},{96,112},{112,96},{1... | collective-permute-start | bytes 172040 | tf_op jit(solution)/shard_map/ppermute | solution.py:509
  6.1 5.7 %collective-permute-start.1 = (bf16[7,16,256]{2,1,0:T(8,128)(2,1)}, bf16[7,16,256]{2,1,0:T(8,128)(2,1)S(1)}, u32[]{:S(2)}, u32[]{:S(2)}) collective-permute-start(bf16[7,16,256]{2,1,0:T(8,128)(2,1)} %get-tuple-element.31), channel_id=1, source_target_pairs={{16,32},{32,16},{48,64},{64,48},{80,96},{96,80},{112,128},{128,112... | collective-permute-start | bytes 172040 | tf_op jit(solution)/shard_map/ppermute | solution.py:509
  12.5 3.5 %collective-permute-start.2 = (bf16[78,2,256]{2,1,0:T(2,128)(2,1)}, bf16[78,2,256]{2,1,0:T(2,128)(2,1)S(1)}, u32[]{:S(2)}, u32[]{:S(2)}) collective-permute-start(bf16[78,2,256]{2,1,0:T(2,128)(2,1)} %get-tuple-element.37), channel_id=1, source_target_pairs={{0,1},{1,0},{2,3},{3,2},{4,5},{5,4},{6,7},{7,6},{8,9},{9,8},{10,11... | collective-permute-start | bytes 239624 | tf_op jit(solution)/shard_map/ppermute | solution.py:509
  12.5 3.5 %collective-permute-start.3 = (bf16[78,2,256]{2,1,0:T(2,128)(2,1)S(1)}, bf16[78,2,256]{2,1,0:T(2,128)(2,1)S(1)}, u32[]{:S(2)}, u32[]{:S(2)}) collective-permute-start(bf16[78,2,256]{2,1,0:T(2,128)(2,1)S(1)} %get-tuple-element.38), channel_id=1, source_target_pairs={{1,2},{2,1},{3,4},{4,3},{5,6},{6,5},{7,8},{8,7},{9,10},{10,9},{11,... | collective-permute-start | bytes 239624 | tf_op jit(solution)/shard_map/ppermute | solution.py:509
  13.3 2.7 %copy-start = (bf16[3,3,256,256]{3,2,1,0:T(8,128)(2,1)S(1)}, bf16[3,3,256,256]{3,2,1,0:T(8,128)(2,1)}, u32[]{:S(2)}) copy-start(bf16[3,3,256,256]{3,2,1,0:T(8,128)(2,1)} %bk_ref.3) | copy-start | bytes 3538948
  14.8 9.8 %copy-start.1 = (bf16[3,3,128,128]{3,2,1,0:T(8,128)(2,1)S(1)}, bf16[3,3,128,128]{3,2,1,0:T(8,128)(2,1)}, u32[]{:S(2)}) copy-start(bf16[3,3,128,128]{3,2,1,0:T(8,128)(2,1)} %lk_ref.1) | copy-start | bytes 884740
  24.5 3.1 %collective-permute-start.4 = (bf16[5120,128]{1,0:T(8,128)(2,1)S(1)}, bf16[5120,128]{1,0:T(8,128)(2,1)S(1)}, u32[]{:S(2)}, u32[]{:S(2)}) collective-permute-start(bf16[5120,128]{1,0:T(8,128)(2,1)S(1)} %get-tuple-element.40), channel_id=1, source_target_pairs={{0,16},{16,0},{32,48},{48,32},{64,80},{80,64},{96,112},{112,96},{1... | collective-permute-start | bytes 3932168 | tf_op jit(solution)/shard_map/ppermute | solution.py:517
  101.6 7.5 %collective-permute-start.5 = (bf16[5120,128]{1,0:T(8,128)(2,1)S(1)}, bf16[5120,128]{1,0:T(8,128)(2,1)S(1)}, u32[]{:S(2)}, u32[]{:S(2)}) collective-permute-start(bf16[5120,128]{1,0:T(8,128)(2,1)S(1)} %bitcast.10), channel_id=1, source_target_pairs={{0,16},{16,0},{32,48},{48,32},{64,80},{80,64},{96,112},{112,96},{1... | collective-permute-start | bytes 3932168 | tf_op jit(solution)/shard_map/ppermute | solution.py:525

commit v8 on v6

--- a/solution.py
+++ b/solution.py
@@ -33,13 +33,16 @@
 ]
 
 
-PAIR_GROUPS = [
-    [place(x, y, z + dz, core) for z in range(0, 8, 2)]
-    for dz in range(2)
-    for x in range(4)
-    for y in range(4)
-    for core in range(2)
-]
+def depth_shift(step):
+    return [
+        (place(x, y, z, core), place(x, y, z + step, core))
+        for x in range(4)
+        for y in range(4)
+        for z in range(8)
+        for core in range(2)
+    ]
+
+
 CORE_SWAP = [(i, i ^ 1) for i in range(16)]
 INNER_PAIRS = CORE_SWAP
 OUTER_PAIRS = [pair for i in range(1, 15, 2) for pair in ((i, i + 1), (i + 1, i))]
@@ -234,7 +237,7 @@
 def main_kernel(
     scale, pos_ref, z_ref, row_in, row_out, col_in, col_out, bk_ref, uk_ref, flip_ref,
     mix4c, pg3c, keep_ref, send_ref,
-    ext, bot3, botc, act3, actc, dsilu, cot4, mg4, mg4c, pgc, packed, sems,
+    ext, bot3, botc, act3, actc, dsilu, cot4, mg4, mg4c, pgc, packed, inside, sems,
 ):
     row0 = pos_ref[0] * TILE
     col0 = pos_ref[1] * TILE
@@ -249,7 +252,10 @@
     core = slice(CORE, CORE + TILE)
     low, high = slice(CORE - 2, CORE), slice(CORE + TILE, CORE + TILE + 2)
     even_row, even_col = is_even("row"), is_even("col")
-    ext[...] = jnp.zeros_like(ext)
+    ext[:, :, 0:CORE, :] = jnp.zeros((5, EXT, CORE, 256), F32)
+    ext[:, :, CORE + TILE : PITCH, :] = jnp.zeros((5, EXT, PITCH - CORE - TILE, 256), F32)
+    for end in (0, EXT - 2):
+        ext[3:5, end : end + 2, core, :] = jnp.zeros((2, 2, TILE, 256), F32)
     for plane in range(5):
         ext[plane, 2 : 2 + TILE, core, :] = z_ref[4 - plane].astype(F32)
     for plane in range(3):
@@ -269,15 +275,17 @@
             col_in[side, par : par + 1], col_out[side, par : par + 1], even_col
         )
 
+    shape = (EXT, PITCH, 128)
+    i = lax.broadcasted_iota(jnp.int32, shape, 0) + (row0 - 2)
+    w = lax.broadcasted_iota(jnp.int32, shape, 1)
+    j = w + (col0 - CORE)
+    keep = (i >= 0) & (i < image_h) & (j >= 0) & (j < image_w)
+    keep = keep & (w >= CORE - 2) & (w < CORE + TILE + 2)
+    inside[...] = flat(jnp.where(keep, 1.0, 0.0))
+
     def masked(x, first):
-        rows = x.shape[0] // PITCH
-        x = x.reshape(rows, PITCH, x.shape[1])
-        i = lax.broadcasted_iota(jnp.int32, x.shape, 0) + (row0 + first - 2)
-        w = lax.broadcasted_iota(jnp.int32, x.shape, 1)
-        j = w + (col0 - CORE)
-        keep = (i >= 0) & (i < image_h) & (j >= 0) & (j < image_w)
-        keep = keep & (w >= CORE - 2) & (w < CORE + TILE + 2)
-        return flat(jnp.where(keep, x, 0.0))
+        rows = inside[first * PITCH : first * PITCH + x.shape[0]]
+        return x * jnp.concatenate([rows, rows], axis=1)
 
     zero = jnp.zeros((128, 128), BF16)
 
@@ -456,6 +464,7 @@
             pltpu.VMEM((2, EXT, TILE, 512), BF16),
             pltpu.VMEM((TILE * TILE, 256), BF16),
             pltpu.VMEM((2, HALF, 128), BF16),
+            pltpu.VMEM((EXT * PITCH, 128), F32),
             pltpu.SemaphoreType.DMA((4,)),
         ],
         compiler_params=pltpu.CompilerParams(vmem_limit_bytes=MAIN_LIMIT),
@@ -527,8 +536,9 @@
     half = (keep.astype(F32) + got.astype(F32)).astype(BF16)
     parts = exchange(half.reshape(BLOCK, HALF // BLOCK, 128), BLOCK_GROUPS)
     part = jnp.sum(parts.astype(F32), axis=0).astype(BF16)
-    pairs = exchange(jnp.broadcast_to(part[None], (4,) + part.shape), PAIR_GROUPS)
-    total = jnp.sum(pairs.astype(F32), axis=0).astype(BF16)
+    near = [lax.ppermute(part, AXES, depth_shift(step)).astype(F32) for step in (2, 6)]
+    far = lax.ppermute(part, AXES, depth_shift(4)).astype(F32)
+    total = ((part.astype(F32) + far) + (near[0] + near[1])).astype(BF16)
     half = exchange(jnp.broadcast_to(total[None], parts.shape), BLOCK_GROUPS).reshape(HALF, 128)
     return half, lax.ppermute(half, "row", CORE_SWAP), rest
 

time: 106 us -> 102 us (0.962)
  blocking collectives: 67.5 us -> 52.5 us
  starting transfers between devices: 10.8 us -> 19.4 us
  waiting for transfers between devices: 4.84 us -> 8.03 us
    all_to_all x3 -> x2, blocking collectives: 67.5 us -> 52.5 us  [exchange(): return lax.all_to_all(x, AXES, 0, 0, axis_index_groups=groups)]
    ppermute x0 -> x3, starting transfers between devices: none -> 9.2 us  [the longest x2 5.19 us: total_over_devices(): lax.ppermute(part, AXES, depth_shift(step)).astype(F32)]
    ppermute x0 -> x3, waiting for transfers between devices: none -> 3.19 us  [the longest x1 2.21 us: total_over_devices(): far = lax.ppermute(part, AXES, depth_shift(4)).astype(F32)]
  transfers between devices with their start and end apart: 6 -> 9, of which waited for: 4 -> 6; matrix products, arithmetic and copies ran while one was open for 3% -> 3% of each run, Pallas kernels for 4% -> 4%
where the time goes in v8:
time: 102 us
  blocking collectives  52.5 us (51%)
  starting transfers between devices  19.4 us (19%)
  Pallas kernels  17.2 us (17%)
  waiting for transfers between devices  8.03 us (8%)
  local copies, waits for them, and re-layouts  3.65 us (4%)
    all_to_all x2, blocking collectives, exchange(): return lax.all_to_all(x, AXES, 0, 0, axis_index_groups=groups)  52.5 us
    pallas_call x1, Pallas kernels, local_work(): pl.pallas_call(functools.partial(main_kernel, scale), out_shape=tuple((ja...  8.49 us
    ppermute x2, starting transfers between devices, total_over_devices(): lax.ppermute(part, AXES, depth_shift(step)).astype(F32)  5.19 us
    ppermute x1, starting transfers between devices, total_over_devices(): return (half, lax.ppermute(half, 'row', CORE_SWAP), rest)  4.17 us
    pallas_call x2, Pallas kernels, unpack(): pl.pallas_call(functools.partial(unpack_kernel, 1 if begun else 0), out_s...  4.16 us
    ppermute x1, starting transfers between devices, total_over_devices(): far = lax.ppermute(part, AXES, depth_shift(4)).astype(F32)  4.01 us
    ppermute x2, starting transfers between devices, swapped(): lax.ppermute(inner, axis, INNER_PAIRS)  3.33 us
    ppermute x2, starting transfers between devices, swapped(): lax.ppermute(outer, axis, OUTER_PAIRS)  2.56 us
  transfers between devices with their start and end apart: 9, of which 6 were waited for; matrix products, arithmetic and copies ran while one was open for 3% of the time, Pallas kernels for 4%

profile of v8, /device:TPU:1, one launch (start us, length us, event | category | flops | bytes accessed | tf_op | source)
XLA Modules:
  0.0 102.1 jit_solution(14084863476894285934)
XLA Ops:
  0.6 2.2 %shard_map.101 = (bf16[5,16,16,256]{3,2,1,0:T(8,128)(2,1)}, bf16[7,16,256]{2,1,0:T(8,128)(2,1)}, bf16[7,16,256]{2,1,0:T(8,128)(2,1)}, bf16[2,78,2,256]{3,2,1,0:T(2,128)(2,1)}) custom-call(bf16[16,16,256]{2,1,0:T(8,128)(2,1)} %bot_hbm.1, bf16[32,32,128]{2,1,0:T(8,128)(2,1)} %skip_hbm.1, bf16[32,32,128]{2,1,0:T(8,128)(2,1)} %cot_hbm.1), custom_call_target="tpu_custom_call" | custom-call | tf_op jit(solution)/shard_map/pallas_call | solution.py:130
  2.8 3.3 %collective-permute-start = (bf16[7,16,256]{2,1,0:T(8,128)(2,1)}, bf16[7,16,256]{2,1,0:T(8,128)(2,1)S(1)}, u32[]{:S(2)}, u32[]{:S(2)}) collective-permute-start(bf16[7,16,256]{2,1,0:T(8,128)(2,1)} %get-tuple-element.30), channel_id=1, source_target_pairs={{0,16},{16,0},{32,48},{48,32},{64,80},{80,64},{96,112},{112,96},{1... | collective-permute-start | bytes 172040 | tf_op jit(solution)/shard_map/ppermute | solution.py:527
  6.1 1.9 %collective-permute-start.1 = (bf16[7,16,256]{2,1,0:T(8,128)(2,1)}, bf16[7,16,256]{2,1,0:T(8,128)(2,1)S(1)}, u32[]{:S(2)}, u32[]{:S(2)}) collective-permute-start(bf16[7,16,256]{2,1,0:T(8,128)(2,1)} %get-tuple-element.31), channel_id=1, source_target_pairs={{16,32},{32,16},{48,64},{64,48},{80,96},{96,80},{112,128},{128,112... | collective-permute-start | bytes 172040 | tf_op jit(solution)/shard_map/ppermute | solution.py:527
  8.1 1.0 rev.15.flip_ref
  9.0 1.0 %rev.13.own = bf16[2,78,2,256]{3,2,1,0:T(2,128)(2,1)S(1)} reverse(bf16[2,78,2,256]{3,2,1,0:T(2,128)(2,1)} %get-tuple-element.36), dimensions={0} | reverse | bytes 319488 | tf_op jit(solution)/shard_map/rev | solution.py:553
  10.1 1.7 %collective-permute-done.1.got_outer.row_out = bf16[7,16,256]{2,1,0:T(8,128)(2,1)S(1)} collective-permute-done((bf16[7,16,256]{2,1,0:T(8,128)(2,1)}, bf16[7,16,256]{2,1,0:T(8,128)(2,1)S(1)}, u32[]{:S(2)}, u32[]{:S(2)}) %collective-permute-start.1) | collective-permute-done | bytes 57376 | tf_op jit(solution)/shard_map/ppermute | solution.py:527
  11.8 0.7 shard_map.102
  12.5 0.7 collective-permute-start.3
  13.4 1.4 %rev.14.uk_ref = bf16[4,4,256,128]{3,2,1,0:T(8,128)(2,1)S(1)} reverse(bf16[4,4,256,128]{3,2,1,0:T(8,128)(2,1)} %param.10), dimensions={1} | reverse | bytes 2097152 | tf_op jit(solution)/shard_map/rev | solution.py:552
  14.8 1.2 %collective-permute-done.2.col_in = bf16[78,2,256]{2,1,0:T(2,128)(2,1)S(1)} collective-permute-done((bf16[78,2,256]{2,1,0:T(2,128)(2,1)}, bf16[78,2,256]{2,1,0:T(2,128)(2,1)S(1)}, u32[]{:S(2)}, u32[]{:S(2)}) %collective-permute-start.2) | collective-permute-done | bytes 79904 | tf_op jit(solution)/shard_map/ppermute | solution.py:527
  16.0 8.5 %shard_map.103 = (bf16[2,18,16,512]{3,2,1,0:T(8,128)(2,1)S(1)}, bf16[18,16,768]{2,1,0:T(8,128)(2,1)S(1)}, bf16[5120,128]{1,0:T(8,128)(2,1)S(1)}, bf16[5120,128]{1,0:T(8,128)(2,1)S(1)}) custom-call(s32[5]{0:T(128)S(1)} %pad_add_fusion.pos_ref, bf16[5,16,16,256]{3,2,1,0:T(8,128)(2,1)S(1)} %rev.12.z_ref, ...), custom_call_target="tpu_custom_call" | custom-call | tf_op jit(solution)/shard_map/pallas_call | solution.py:450
  24.6 1.7 %shard_map.104 = (bf16[32,32,128]{2,1,0:T(8,128)(2,1)}, bf16[16,16,256]{2,1,0:T(8,128)(2,1)}) custom-call(bf16[2,18,16,512]{3,2,1,0:T(8,128)(2,1)S(1)} %get-tuple-element.41.mix4c, bf16[18,16,768]{2,1,0:T(8,128)(2,1)S(1)} %get-tuple-element.42.pg3c, bf16[3,3,256,256]{3,2,1,0:T(8,128)(2,1)S(1)} %copy-done, bf16[3,3,128,128]{3,2,1,0:T(8,128)(2,1)S(1)} %copy-done.1), custom_call_target="tpu_custom_call" | custom-call | flops 1000000000 | bytes 3000000 | tf_op jit(solution)/shard_map/pallas_call | solution.py:432
  26.3 1.3 %collective-permute-done.4 = bf16[5120,128]{1,0:T(8,128)(2,1)S(1)} collective-permute-done((bf16[5120,128]{1,0:T(8,128)(2,1)S(1)}, bf16[5120,128]{1,0:T(8,128)(2,1)S(1)}, u32[]{:S(2)}, u32[]{:S(2)}) %collective-permute-start.4) | collective-permute-done | bytes 1310752 | tf_op jit(solution)/shard_map/ppermute | solution.py:535
  27.6 0.3 add_convert_fusion
  28.0 31.5 %all_to_all.10 = bf16[32,160,128]{2,1,0:T(8,128)(2,1)S(1)} all-to-all(bf16[32,160,128]{2,1,0:T(8,128)(2,1)S(1)} %bitcast.10), channel_id=1, replica_groups={{0,1,128,129,32,33,160,161,64,65,192,193,96,97,224,225,2,3,130,131,34,3..., dimensions={0} | all-to-all | bytes 2621440 | tf_op jit(solution)/shard_map/all_to_all | solution.py:531
  59.7 5.2 %collective-permute-start.7 = (bf16[160,128]{1,0:T(8,128)(2,1)S(1)}, bf16[160,128]{1,0:T(8,128)(2,1)S(1)}, u32[]{:S(2)}, u32[]{:S(2)}) collective-permute-start(bf16[160,128]{1,0:T(8,128)(2,1)S(1)} %reduce_sum.12), channel_id=1, source_target_pairs={{0,12},{16,28},{2,14},{18,30},{4,0},{20,16},{6,2},{22,18},{8,4},{2... | collective-permute-start | bytes 122888 | tf_op jit(solution)/shard_map/ppermute | solution.py:539
  64.9 4.0 %collective-permute-start.5 = (bf16[160,128]{1,0:T(8,128)(2,1)S(1)}, bf16[160,128]{1,0:T(8,128)(2,1)S(1)}, u32[]{:S(2)}, u32[]{:S(2)}) collective-permute-start(bf16[160,128]{1,0:T(8,128)(2,1)S(1)} %reduce_sum.12), channel_id=1, source_target_pairs={{0,8},{16,24},{2,10},{18,26},{4,12},{20,28},{6,14},{22,30},{8,0},{... | collective-permute-start | bytes 122888 | tf_op jit(solution)/shard_map/ppermute | solution.py:540
  68.9 1.0 collective-permute-done.6
  69.9 2.2 %collective-permute-done.5 = bf16[160,128]{1,0:T(8,128)(2,1)S(1)} collective-permute-done((bf16[160,128]{1,0:T(8,128)(2,1)S(1)}, bf16[160,128]{1,0:T(8,128)(2,1)S(1)}, u32[]{:S(2)}, u32[]{:S(2)}) %collective-permute-start.5) | collective-permute-done | bytes 40992 | tf_op jit(solution)/shard_map/ppermute | solution.py:540
  72.3 21.0 %all_to_all.11 = bf16[32,160,128]{2,1,0:T(8,128)(2,1)S(1)} all-to-all(bf16[32,160,128]{2,1,0:T(8,128)(2,1)S(1)} %broadcast_in_dim.2), channel_id=1, replica_groups={{0,1,128,129,32,33,160,161,64,65,192,193,96,97,224,225,2,3,130,131,34,3..., dimensions={0} | all-to-all | bytes 2621440 | tf_op jit(solution)/shard_map/all_to_all | solution.py:531
  93.2 4.2 %collective-permute-start.8 = (bf16[5120,128]{1,0:T(8,128)(2,1)S(1)}, bf16[5120,128]{1,0:T(8,128)(2,1)S(1)}, u32[]{:S(2)}, u32[]{:S(2)}) collective-permute-start(bf16[5120,128]{1,0:T(8,128)(2,1)S(1)} %bitcast.8), channel_id=1, source_target_pairs={{0,16},{16,0},{32,48},{48,32},{64,80},{80,64},{96,112},{112,96},{1... | collective-permute-start | bytes 3932168 | tf_op jit(solution)/shard_map/ppermute | solution.py:543
  97.4 2.1 %shard_map.105 = (f32[4096,128]{1,0:T(8,128)}, f32[2304,256]{1,0:T(8,128)}, f32[1152,128]{1,0:T(8,128)}) custom-call(s32[5]{0:T(128)S(1)} %pad_add_fusion.pos_ref, bf16[5120,128]{1,0:T(8,128)(2,1)S(1)} %bitcast.9), custom_call_target="tpu_custom_call" | custom-call | bytes 4000000 | tf_op jit(solution)/shard_map/pallas_call | solution.py:513
  99.5 0.6 collective-permute-done.8.half
  100.1 2.1 %shard_map.106 = (f32[4096,128]{1,0:T(8,128)}, f32[2304,256]{1,0:T(8,128)}, f32[1152,128]{1,0:T(8,128)}) custom-call(s32[5]{0:T(128)S(1)} %pad_add_fusion.pos_ref, bf16[5120,128]{1,0:T(8,128)(2,1)S(1)} %collective-permute-done.8.half, f32[4096,128]{1,0:T(8,128)} %get-tuple-element.49.refs_0_, ...), custom_call_target="tpu_custom_call", output_to_operand_aliasing={{0}: (2, {}), {1}: (3, {}), {2}: (4, {})} | custom-call | bytes 4000000 | tf_op jit(solution)/shard_map/pallas_call | solution.py:513
  (18 shorter events, 0.6 us)
Async XLA Ops:
  2.8 10.5 %copy-start.2 = (bf16[5,16,16,256]{3,2,1,0:T(8,128)(2,1)S(1)}, bf16[5,16,16,256]{3,2,1,0:T(8,128)(2,1)}, u32[]{:S(2)}) copy-start(bf16[5,16,16,256]{3,2,1,0:T(8,128)(2,1)} %get-tuple-element.33) | copy-start | bytes 1966084
  2.8 7.3 %collective-permute-start = (bf16[7,16,256]{2,1,0:T(8,128)(2,1)}, bf16[7,16,256]{2,1,0:T(8,128)(2,1)S(1)}, u32[]{:S(2)}, u32[]{:S(2)}) collective-permute-start(bf16[7,16,256]{2,1,0:T(8,128)(2,1)} %get-tuple-element.30), channel_id=1, source_target_pairs={{0,16},{16,0},{32,48},{48,32},{64,80},{80,64},{96,112},{112,96},{1... | collective-permute-start | bytes 172040 | tf_op jit(solution)/shard_map/ppermute | solution.py:527
  6.1 5.7 %collective-permute-start.1 = (bf16[7,16,256]{2,1,0:T(8,128)(2,1)}, bf16[7,16,256]{2,1,0:T(8,128)(2,1)S(1)}, u32[]{:S(2)}, u32[]{:S(2)}) collective-permute-start(bf16[7,16,256]{2,1,0:T(8,128)(2,1)} %get-tuple-element.31), channel_id=1, source_target_pairs={{16,32},{32,16},{48,64},{64,48},{80,96},{96,80},{112,128},{128,112... | collective-permute-start | bytes 172040 | tf_op jit(solution)/shard_map/ppermute | solution.py:527
  12.5 3.5 %collective-permute-start.2 = (bf16[78,2,256]{2,1,0:T(2,128)(2,1)}, bf16[78,2,256]{2,1,0:T(2,128)(2,1)S(1)}, u32[]{:S(2)}, u32[]{:S(2)}) collective-permute-start(bf16[78,2,256]{2,1,0:T(2,128)(2,1)} %get-tuple-element.37), channel_id=1, source_target_pairs={{0,1},{1,0},{2,3},{3,2},{4,5},{5,4},{6,7},{7,6},{8,9},{9,8},{10,11... | collective-permute-start | bytes 239624 | tf_op jit(solution)/shard_map/ppermute | solution.py:527
  12.5 3.5 %collective-permute-start.3 = (bf16[78,2,256]{2,1,0:T(2,128)(2,1)S(1)}, bf16[78,2,256]{2,1,0:T(2,128)(2,1)S(1)}, u32[]{:S(2)}, u32[]{:S(2)}) collective-permute-start(bf16[78,2,256]{2,1,0:T(2,128)(2,1)S(1)} %get-tuple-element.38), channel_id=1, source_target_pairs={{1,2},{2,1},{3,4},{4,3},{5,6},{6,5},{7,8},{8,7},{9,10},{10,9},{11,... | collective-permute-start | bytes 239624 | tf_op jit(solution)/shard_map/ppermute | solution.py:527
  13.3 2.7 %copy-start = (bf16[3,3,256,256]{3,2,1,0:T(8,128)(2,1)S(1)}, bf16[3,3,256,256]{3,2,1,0:T(8,128)(2,1)}, u32[]{:S(2)}) copy-start(bf16[3,3,256,256]{3,2,1,0:T(8,128)(2,1)} %bk_ref.3) | copy-start | bytes 3538948
  14.8 9.9 %copy-start.1 = (bf16[3,3,128,128]{3,2,1,0:T(8,128)(2,1)S(1)}, bf16[3,3,128,128]{3,2,1,0:T(8,128)(2,1)}, u32[]{:S(2)}) copy-start(bf16[3,3,128,128]{3,2,1,0:T(8,128)(2,1)} %lk_ref.1) | copy-start | bytes 884740
  24.5 3.1 %collective-permute-start.4 = (bf16[5120,128]{1,0:T(8,128)(2,1)S(1)}, bf16[5120,128]{1,0:T(8,128)(2,1)S(1)}, u32[]{:S(2)}, u32[]{:S(2)}) collective-permute-start(bf16[5120,128]{1,0:T(8,128)(2,1)S(1)} %get-tuple-element.40), channel_id=1, source_target_pairs={{0,16},{16,0},{32,48},{48,32},{64,80},{80,64},{96,112},{112,96},{1... | collective-permute-start | bytes 3932168 | tf_op jit(solution)/shard_map/ppermute | solution.py:535
  59.7 9.2 %collective-permute-start.7 = (bf16[160,128]{1,0:T(8,128)(2,1)S(1)}, bf16[160,128]{1,0:T(8,128)(2,1)S(1)}, u32[]{:S(2)}, u32[]{:S(2)}) collective-permute-start(bf16[160,128]{1,0:T(8,128)(2,1)S(1)} %reduce_sum.12), channel_id=1, source_target_pairs={{0,12},{16,28},{2,14},{18,30},{4,0},{20,16},{6,2},{22,18},{8,4},{2... | collective-permute-start | bytes 122888 | tf_op jit(solution)/shard_map/ppermute | solution.py:539
  64.9 5.0 %collective-permute-start.6 = (bf16[160,128]{1,0:T(8,128)(2,1)S(1)}, bf16[160,128]{1,0:T(8,128)(2,1)S(1)}, u32[]{:S(2)}, u32[]{:S(2)}) collective-permute-start(bf16[160,128]{1,0:T(8,128)(2,1)S(1)} %reduce_sum.12), channel_id=1, source_target_pairs={{0,4},{16,20},{2,6},{18,22},{4,8},{20,24},{6,10},{22,26},{8,12},{2... | collective-permute-start | bytes 122888 | tf_op jit(solution)/shard_map/ppermute | solution.py:539
  64.9 7.2 %collective-permute-start.5 = (bf16[160,128]{1,0:T(8,128)(2,1)S(1)}, bf16[160,128]{1,0:T(8,128)(2,1)S(1)}, u32[]{:S(2)}, u32[]{:S(2)}) collective-permute-start(bf16[160,128]{1,0:T(8,128)(2,1)S(1)} %reduce_sum.12), channel_id=1, source_target_pairs={{0,8},{16,24},{2,10},{18,26},{4,12},{20,28},{6,14},{22,30},{8,0},{... | collective-permute-start | bytes 122888 | tf_op jit(solution)/shard_map/ppermute | solution.py:540
  93.2 6.8 %collective-permute-start.8 = (bf16[5120,128]{1,0:T(8,128)(2,1)S(1)}, bf16[5120,128]{1,0:T(8,128)(2,1)S(1)}, u32[]{:S(2)}, u32[]{:S(2)}) collective-permute-start(bf16[5120,128]{1,0:T(8,128)(2,1)S(1)} %bitcast.8), channel_id=1, source_target_pairs={{0,16},{16,0},{32,48},{48,32},{64,80},{80,64},{96,112},{112,96},{1... | collective-permute-start | bytes 3932168 | tf_op jit(solution)/shard_map/ppermute | solution.py:543

commit v9 on v8

--- a/solution.py
+++ b/solution.py
@@ -536,9 +536,9 @@
     half = (keep.astype(F32) + got.astype(F32)).astype(BF16)
     parts = exchange(half.reshape(BLOCK, HALF // BLOCK, 128), BLOCK_GROUPS)
     part = jnp.sum(parts.astype(F32), axis=0).astype(BF16)
+    far = lax.ppermute(part, AXES, depth_shift(4)).astype(F32)
     near = [lax.ppermute(part, AXES, depth_shift(step)).astype(F32) for step in (2, 6)]
-    far = lax.ppermute(part, AXES, depth_shift(4)).astype(F32)
-    total = ((part.astype(F32) + far) + (near[0] + near[1])).astype(BF16)
+    total = ((near[0] + near[1]) + (far + part.astype(F32))).astype(BF16)
     half = exchange(jnp.broadcast_to(total[None], parts.shape), BLOCK_GROUPS).reshape(HALF, 128)
     return half, lax.ppermute(half, "row", CORE_SWAP), rest
 

time: 102 us -> 102 us (level)
    ppermute x1, starting transfers between devices: 4.01 us -> 6.85 us  [total_over_devices(): far = lax.ppermute(part, AXES, depth_shift(4)).astype(F32)]
    ppermute x2, starting transfers between devices: 5.19 us -> 2.36 us  [total_over_devices(): lax.ppermute(part, AXES, depth_shift(step)).astype(F32)]
    ppermute x1, waiting for transfers between devices: 2.21 us -> 0.01 us  [total_over_devices(): far = lax.ppermute(part, AXES, depth_shift(4)).astype(F32)]
    ppermute x2, waiting for transfers between devices: 0.98 us -> 2.63 us  [total_over_devices(): lax.ppermute(part, AXES, depth_shift(step)).astype(F32)]
where the time goes in v9:
time: 102 us
  blocking collectives  52.5 us (51%)
  starting transfers between devices  19.8 us (19%)
  Pallas kernels  17.2 us (17%)
  waiting for transfers between devices  7.47 us (7%)
  local copies, waits for them, and re-layouts  3.65 us (4%)
    all_to_all x2, blocking collectives, exchange(): return lax.all_to_all(x, AXES, 0, 0, axis_index_groups=groups)  52.5 us
    pallas_call x1, Pallas kernels, local_work(): pl.pallas_call(functools.partial(main_kernel, scale), out_shape=tuple((ja...  8.49 us
    ppermute x1, starting transfers between devices, total_over_devices(): far = lax.ppermute(part, AXES, depth_shift(4)).astype(F32)  6.85 us
    ppermute x1, starting transfers between devices, total_over_devices(): return (half, lax.ppermute(half, 'row', CORE_SWAP), rest)  4.55 us
    pallas_call x2, Pallas kernels, unpack(): pl.pallas_call(functools.partial(unpack_kernel, 1 if begun else 0), out_s...  4.16 us
    ppermute x2, starting transfers between devices, swapped(): lax.ppermute(inner, axis, INNER_PAIRS)  3.33 us
    ppermute x2, waiting for transfers between devices, total_over_devices(): lax.ppermute(part, AXES, depth_shift(step)).astype(F32)  2.63 us
    ppermute x2, starting transfers between devices, swapped(): lax.ppermute(outer, axis, OUTER_PAIRS)  2.56 us
  transfers between devices with their start and end apart: 9, of which 6 were waited for; matrix products, arithmetic and copies ran while one was open for 3% of the time, Pallas kernels for 4%

profile of v9, /device:TPU:1, one launch (start us, length us, event | category | flops | bytes accessed | tf_op | source)
XLA Modules:
  0.0 102.0 jit_solution(15420823118668337333)
XLA Ops:
  0.6 2.2 %shard_map.101 = (bf16[5,16,16,256]{3,2,1,0:T(8,128)(2,1)}, bf16[7,16,256]{2,1,0:T(8,128)(2,1)}, bf16[7,16,256]{2,1,0:T(8,128)(2,1)}, bf16[2,78,2,256]{3,2,1,0:T(2,128)(2,1)}) custom-call(bf16[16,16,256]{2,1,0:T(8,128)(2,1)} %bot_hbm.1, bf16[32,32,128]{2,1,0:T(8,128)(2,1)} %skip_hbm.1, bf16[32,32,128]{2,1,0:T(8,128)(2,1)} %cot_hbm.1), custom_call_target="tpu_custom_call" | custom-call | tf_op jit(solution)/shard_map/pallas_call | solution.py:130
  2.8 3.3 %collective-permute-start = (bf16[7,16,256]{2,1,0:T(8,128)(2,1)}, bf16[7,16,256]{2,1,0:T(8,128)(2,1)S(1)}, u32[]{:S(2)}, u32[]{:S(2)}) collective-permute-start(bf16[7,16,256]{2,1,0:T(8,128)(2,1)} %get-tuple-element.30), channel_id=1, source_target_pairs={{0,16},{16,0},{32,48},{48,32},{64,80},{80,64},{96,112},{112,96},{1... | collective-permute-start | bytes 172040 | tf_op jit(solution)/shard_map/ppermute | solution.py:527
  6.1 1.9 %collective-permute-start.1 = (bf16[7,16,256]{2,1,0:T(8,128)(2,1)}, bf16[7,16,256]{2,1,0:T(8,128)(2,1)S(1)}, u32[]{:S(2)}, u32[]{:S(2)}) collective-permute-start(bf16[7,16,256]{2,1,0:T(8,128)(2,1)} %get-tuple-element.31), channel_id=1, source_target_pairs={{16,32},{32,16},{48,64},{64,48},{80,96},{96,80},{112,128},{128,112... | collective-permute-start | bytes 172040 | tf_op jit(solution)/shard_map/ppermute | solution.py:527
  8.1 1.0 rev.15.flip_ref
  9.0 1.0 %rev.13.own = bf16[2,78,2,256]{3,2,1,0:T(2,128)(2,1)S(1)} reverse(bf16[2,78,2,256]{3,2,1,0:T(2,128)(2,1)} %get-tuple-element.36), dimensions={0} | reverse | bytes 319488 | tf_op jit(solution)/shard_map/rev | solution.py:553
  10.1 1.7 %collective-permute-done.1.got_outer.row_out = bf16[7,16,256]{2,1,0:T(8,128)(2,1)S(1)} collective-permute-done((bf16[7,16,256]{2,1,0:T(8,128)(2,1)}, bf16[7,16,256]{2,1,0:T(8,128)(2,1)S(1)}, u32[]{:S(2)}, u32[]{:S(2)}) %collective-permute-start.1) | collective-permute-done | bytes 57376 | tf_op jit(solution)/shard_map/ppermute | solution.py:527
  11.8 0.7 shard_map.102
  12.5 0.7 collective-permute-start.3
  13.4 1.4 %rev.14.uk_ref = bf16[4,4,256,128]{3,2,1,0:T(8,128)(2,1)S(1)} reverse(bf16[4,4,256,128]{3,2,1,0:T(8,128)(2,1)} %param.10), dimensions={1} | reverse | bytes 2097152 | tf_op jit(solution)/shard_map/rev | solution.py:552
  14.8 1.2 %collective-permute-done.2.col_in = bf16[78,2,256]{2,1,0:T(2,128)(2,1)S(1)} collective-permute-done((bf16[78,2,256]{2,1,0:T(2,128)(2,1)}, bf16[78,2,256]{2,1,0:T(2,128)(2,1)S(1)}, u32[]{:S(2)}, u32[]{:S(2)}) %collective-permute-start.2) | collective-permute-done | bytes 79904 | tf_op jit(solution)/shard_map/ppermute | solution.py:527
  16.0 8.5 %shard_map.103 = (bf16[2,18,16,512]{3,2,1,0:T(8,128)(2,1)S(1)}, bf16[18,16,768]{2,1,0:T(8,128)(2,1)S(1)}, bf16[5120,128]{1,0:T(8,128)(2,1)S(1)}, bf16[5120,128]{1,0:T(8,128)(2,1)S(1)}) custom-call(s32[5]{0:T(128)S(1)} %pad_add_fusion.pos_ref, bf16[5,16,16,256]{3,2,1,0:T(8,128)(2,1)S(1)} %rev.12.z_ref, ...), custom_call_target="tpu_custom_call" | custom-call | tf_op jit(solution)/shard_map/pallas_call | solution.py:450
  24.6 1.7 %shard_map.104 = (bf16[32,32,128]{2,1,0:T(8,128)(2,1)}, bf16[16,16,256]{2,1,0:T(8,128)(2,1)}) custom-call(bf16[2,18,16,512]{3,2,1,0:T(8,128)(2,1)S(1)} %get-tuple-element.41.mix4c, bf16[18,16,768]{2,1,0:T(8,128)(2,1)S(1)} %get-tuple-element.42.pg3c, bf16[3,3,256,256]{3,2,1,0:T(8,128)(2,1)S(1)} %copy-done, bf16[3,3,128,128]{3,2,1,0:T(8,128)(2,1)S(1)} %copy-done.1), custom_call_target="tpu_custom_call" | custom-call | flops 1000000000 | bytes 3000000 | tf_op jit(solution)/shard_map/pallas_call | solution.py:432
  26.3 1.3 %collective-permute-done.4 = bf16[5120,128]{1,0:T(8,128)(2,1)S(1)} collective-permute-done((bf16[5120,128]{1,0:T(8,128)(2,1)S(1)}, bf16[5120,128]{1,0:T(8,128)(2,1)S(1)}, u32[]{:S(2)}, u32[]{:S(2)}) %collective-permute-start.4) | collective-permute-done | bytes 1310752 | tf_op jit(solution)/shard_map/ppermute | solution.py:535
  27.6 0.3 add_convert_fusion
  28.0 31.5 %all_to_all.10 = bf16[32,160,128]{2,1,0:T(8,128)(2,1)S(1)} all-to-all(bf16[32,160,128]{2,1,0:T(8,128)(2,1)S(1)} %bitcast.10), channel_id=1, replica_groups={{0,1,128,129,32,33,160,161,64,65,192,193,96,97,224,225,2,3,130,131,34,3..., dimensions={0} | all-to-all | bytes 2621440 | tf_op jit(solution)/shard_map/all_to_all | solution.py:531
  59.7 6.8 %collective-permute-start.7 = (bf16[160,128]{1,0:T(8,128)(2,1)S(1)}, bf16[160,128]{1,0:T(8,128)(2,1)S(1)}, u32[]{:S(2)}, u32[]{:S(2)}) collective-permute-start(bf16[160,128]{1,0:T(8,128)(2,1)S(1)} %reduce_sum.12), channel_id=1, source_target_pairs={{0,8},{16,24},{2,10},{18,26},{4,12},{20,28},{6,14},{22,30},{8,0},{... | collective-permute-start | bytes 122888 | tf_op jit(solution)/shard_map/ppermute | solution.py:539
  66.5 2.4 %collective-permute-start.5 = (bf16[160,128]{1,0:T(8,128)(2,1)S(1)}, bf16[160,128]{1,0:T(8,128)(2,1)S(1)}, u32[]{:S(2)}, u32[]{:S(2)}) collective-permute-start(bf16[160,128]{1,0:T(8,128)(2,1)S(1)} %reduce_sum.12), channel_id=1, source_target_pairs={{0,4},{16,20},{2,6},{18,22},{4,8},{20,24},{6,10},{22,26},{8,12},{2... | collective-permute-start | bytes 122888 | tf_op jit(solution)/shard_map/ppermute | solution.py:540
  68.9 1.8 %collective-permute-done.6 = bf16[160,128]{1,0:T(8,128)(2,1)S(1)} collective-permute-done((bf16[160,128]{1,0:T(8,128)(2,1)S(1)}, bf16[160,128]{1,0:T(8,128)(2,1)S(1)}, u32[]{:S(2)}, u32[]{:S(2)}) %collective-permute-start.6) | collective-permute-done | bytes 40992 | tf_op jit(solution)/shard_map/ppermute | solution.py:540
  70.6 0.9 collective-permute-done.5
  71.7 21.0 %all_to_all.11 = bf16[32,160,128]{2,1,0:T(8,128)(2,1)S(1)} all-to-all(bf16[32,160,128]{2,1,0:T(8,128)(2,1)S(1)} %broadcast_in_dim.2), channel_id=1, replica_groups={{0,1,128,129,32,33,160,161,64,65,192,193,96,97,224,225,2,3,130,131,34,3..., dimensions={0} | all-to-all | bytes 2621440 | tf_op jit(solution)/shard_map/all_to_all | solution.py:531
  92.8 4.6 %collective-permute-start.8 = (bf16[5120,128]{1,0:T(8,128)(2,1)S(1)}, bf16[5120,128]{1,0:T(8,128)(2,1)S(1)}, u32[]{:S(2)}, u32[]{:S(2)}) collective-permute-start(bf16[5120,128]{1,0:T(8,128)(2,1)S(1)} %bitcast.8), channel_id=1, source_target_pairs={{0,16},{16,0},{32,48},{48,32},{64,80},{80,64},{96,112},{112,96},{1... | collective-permute-start | bytes 3932168 | tf_op jit(solution)/shard_map/ppermute | solution.py:543
  97.3 2.1 %shard_map.105 = (f32[4096,128]{1,0:T(8,128)}, f32[2304,256]{1,0:T(8,128)}, f32[1152,128]{1,0:T(8,128)}) custom-call(s32[5]{0:T(128)S(1)} %pad_add_fusion.pos_ref, bf16[5120,128]{1,0:T(8,128)(2,1)S(1)} %bitcast.9), custom_call_target="tpu_custom_call" | custom-call | bytes 4000000 | tf_op jit(solution)/shard_map/pallas_call | solution.py:513
  99.4 0.6 collective-permute-done.8.half
  100.0 2.1 %shard_map.106 = (f32[4096,128]{1,0:T(8,128)}, f32[2304,256]{1,0:T(8,128)}, f32[1152,128]{1,0:T(8,128)}) custom-call(s32[5]{0:T(128)S(1)} %pad_add_fusion.pos_ref, bf16[5120,128]{1,0:T(8,128)(2,1)S(1)} %collective-permute-done.8.half, f32[4096,128]{1,0:T(8,128)} %get-tuple-element.49.refs_0_, ...), custom_call_target="tpu_custom_call", output_to_operand_aliasing={{0}: (2, {}), {1}: (3, {}), {2}: (4, {})} | custom-call | bytes 4000000 | tf_op jit(solution)/shard_map/pallas_call | solution.py:513
  (18 shorter events, 0.6 us)
Async XLA Ops:
  2.8 10.5 %copy-start.2 = (bf16[5,16,16,256]{3,2,1,0:T(8,128)(2,1)S(1)}, bf16[5,16,16,256]{3,2,1,0:T(8,128)(2,1)}, u32[]{:S(2)}) copy-start(bf16[5,16,16,256]{3,2,1,0:T(8,128)(2,1)} %get-tuple-element.33) | copy-start | bytes 1966084
  2.8 7.3 %collective-permute-start = (bf16[7,16,256]{2,1,0:T(8,128)(2,1)}, bf16[7,16,256]{2,1,0:T(8,128)(2,1)S(1)}, u32[]{:S(2)}, u32[]{:S(2)}) collective-permute-start(bf16[7,16,256]{2,1,0:T(8,128)(2,1)} %get-tuple-element.30), channel_id=1, source_target_pairs={{0,16},{16,0},{32,48},{48,32},{64,80},{80,64},{96,112},{112,96},{1... | collective-permute-start | bytes 172040 | tf_op jit(solution)/shard_map/ppermute | solution.py:527
  6.1 5.7 %collective-permute-start.1 = (bf16[7,16,256]{2,1,0:T(8,128)(2,1)}, bf16[7,16,256]{2,1,0:T(8,128)(2,1)S(1)}, u32[]{:S(2)}, u32[]{:S(2)}) collective-permute-start(bf16[7,16,256]{2,1,0:T(8,128)(2,1)} %get-tuple-element.31), channel_id=1, source_target_pairs={{16,32},{32,16},{48,64},{64,48},{80,96},{96,80},{112,128},{128,112... | collective-permute-start | bytes 172040 | tf_op jit(solution)/shard_map/ppermute | solution.py:527
  12.5 3.5 %collective-permute-start.2 = (bf16[78,2,256]{2,1,0:T(2,128)(2,1)}, bf16[78,2,256]{2,1,0:T(2,128)(2,1)S(1)}, u32[]{:S(2)}, u32[]{:S(2)}) collective-permute-start(bf16[78,2,256]{2,1,0:T(2,128)(2,1)} %get-tuple-element.37), channel_id=1, source_target_pairs={{0,1},{1,0},{2,3},{3,2},{4,5},{5,4},{6,7},{7,6},{8,9},{9,8},{10,11... | collective-permute-start | bytes 239624 | tf_op jit(solution)/shard_map/ppermute | solution.py:527
  12.5 3.5 %collective-permute-start.3 = (bf16[78,2,256]{2,1,0:T(2,128)(2,1)S(1)}, bf16[78,2,256]{2,1,0:T(2,128)(2,1)S(1)}, u32[]{:S(2)}, u32[]{:S(2)}) collective-permute-start(bf16[78,2,256]{2,1,0:T(2,128)(2,1)S(1)} %get-tuple-element.38), channel_id=1, source_target_pairs={{1,2},{2,1},{3,4},{4,3},{5,6},{6,5},{7,8},{8,7},{9,10},{10,9},{11,... | collective-permute-start | bytes 239624 | tf_op jit(solution)/shard_map/ppermute | solution.py:527
  13.3 2.7 %copy-start = (bf16[3,3,256,256]{3,2,1,0:T(8,128)(2,1)S(1)}, bf16[3,3,256,256]{3,2,1,0:T(8,128)(2,1)}, u32[]{:S(2)}) copy-start(bf16[3,3,256,256]{3,2,1,0:T(8,128)(2,1)} %bk_ref.3) | copy-start | bytes 3538948
  14.8 9.9 %copy-start.1 = (bf16[3,3,128,128]{3,2,1,0:T(8,128)(2,1)S(1)}, bf16[3,3,128,128]{3,2,1,0:T(8,128)(2,1)}, u32[]{:S(2)}) copy-start(bf16[3,3,128,128]{3,2,1,0:T(8,128)(2,1)} %lk_ref.1) | copy-start | bytes 884740
  24.5 3.1 %collective-permute-start.4 = (bf16[5120,128]{1,0:T(8,128)(2,1)S(1)}, bf16[5120,128]{1,0:T(8,128)(2,1)S(1)}, u32[]{:S(2)}, u32[]{:S(2)}) collective-permute-start(bf16[5120,128]{1,0:T(8,128)(2,1)S(1)} %get-tuple-element.40), channel_id=1, source_target_pairs={{0,16},{16,0},{32,48},{48,32},{64,80},{80,64},{96,112},{112,96},{1... | collective-permute-start | bytes 3932168 | tf_op jit(solution)/shard_map/ppermute | solution.py:535
  59.7 9.2 %collective-permute-start.7 = (bf16[160,128]{1,0:T(8,128)(2,1)S(1)}, bf16[160,128]{1,0:T(8,128)(2,1)S(1)}, u32[]{:S(2)}, u32[]{:S(2)}) collective-permute-start(bf16[160,128]{1,0:T(8,128)(2,1)S(1)} %reduce_sum.12), channel_id=1, source_target_pairs={{0,8},{16,24},{2,10},{18,26},{4,12},{20,28},{6,14},{22,30},{8,0},{... | collective-permute-start | bytes 122888 | tf_op jit(solution)/shard_map/ppermute | solution.py:539
  66.5 4.1 %collective-permute-start.6 = (bf16[160,128]{1,0:T(8,128)(2,1)S(1)}, bf16[160,128]{1,0:T(8,128)(2,1)S(1)}, u32[]{:S(2)}, u32[]{:S(2)}) collective-permute-start(bf16[160,128]{1,0:T(8,128)(2,1)S(1)} %reduce_sum.12), channel_id=1, source_target_pairs={{0,12},{16,28},{2,14},{18,30},{4,0},{20,16},{6,2},{22,18},{8,4},{2... | collective-permute-start | bytes 122888 | tf_op jit(solution)/shard_map/ppermute | solution.py:540
  66.5 5.0 %collective-permute-start.5 = (bf16[160,128]{1,0:T(8,128)(2,1)S(1)}, bf16[160,128]{1,0:T(8,128)(2,1)S(1)}, u32[]{:S(2)}, u32[]{:S(2)}) collective-permute-start(bf16[160,128]{1,0:T(8,128)(2,1)S(1)} %reduce_sum.12), channel_id=1, source_target_pairs={{0,4},{16,20},{2,6},{18,22},{4,8},{20,24},{6,10},{22,26},{8,12},{2... | collective-permute-start | bytes 122888 | tf_op jit(solution)/shard_map/ppermute | solution.py:540
  92.8 7.2 %collective-permute-start.8 = (bf16[5120,128]{1,0:T(8,128)(2,1)S(1)}, bf16[5120,128]{1,0:T(8,128)(2,1)S(1)}, u32[]{:S(2)}, u32[]{:S(2)}) collective-permute-start(bf16[5120,128]{1,0:T(8,128)(2,1)S(1)} %bitcast.8), channel_id=1, source_target_pairs={{0,16},{16,0},{32,48},{48,32},{64,80},{80,64},{96,112},{112,96},{1... | collective-permute-start | bytes 3932168 | tf_op jit(solution)/shard_map/ppermute | solution.py:543

commit v10 on v9

--- a/solution.py
+++ b/solution.py
@@ -12,8 +12,8 @@
 BF16 = jnp.bfloat16
 TILE = 16
 EXT = TILE + 4
-PITCH = 32
-CORE = 8
+PITCH = 24
+CORE = 2
 MAIN_LIMIT = 40 << 20
 FIRST_LIMIT = 56 << 20
 HALF = 5120
@@ -207,7 +207,12 @@
 
 def core_of(x):
     rows = x.shape[0] // PITCH
-    return x.reshape(rows, PITCH, x.shape[1])[:, CORE : CORE + TILE]
+    x = pltpu.roll(x, x.shape[0] - CORE, 0)
+    return x.reshape(rows, PITCH, x.shape[1])[:, :TILE]
+
+
+def rows_of(ref, first, count):
+    return ref[first * PITCH : first * PITCH + count * PITCH].astype(BF16)
 
 
 def three(x):
@@ -252,10 +257,7 @@
     core = slice(CORE, CORE + TILE)
     low, high = slice(CORE - 2, CORE), slice(CORE + TILE, CORE + TILE + 2)
     even_row, even_col = is_even("row"), is_even("col")
-    ext[:, :, 0:CORE, :] = jnp.zeros((5, EXT, CORE, 256), F32)
-    ext[:, :, CORE + TILE : PITCH, :] = jnp.zeros((5, EXT, PITCH - CORE - TILE, 256), F32)
-    for end in (0, EXT - 2):
-        ext[3:5, end : end + 2, core, :] = jnp.zeros((2, 2, TILE, 256), F32)
+    ext[...] = jnp.zeros_like(ext)
     for plane in range(5):
         ext[plane, 2 : 2 + TILE, core, :] = z_ref[4 - plane].astype(F32)
     for plane in range(3):
@@ -291,37 +293,42 @@
 
     for b, part in enumerate(three(flat(ext[0]))):
         lanes = slice(256 * b, 256 * b + 256)
-        bot3[:, :, lanes] = part.reshape(EXT, PITCH, 256).astype(BF16)
+        bot3[:, lanes] = part
         botc[:, :, lanes] = core_of(part)[1 : 19].astype(BF16)
     pre = jnp.zeros((18 * PITCH, 256), F32)
     for a in range(3):
-        pre = pre + nn(flat(bot3[a : a + 18]), bk_ref[a].reshape(768, 256))
+        pre = pre + nn(rows_of(bot3, a, 18), bk_ref[a].reshape(768, 256))
     sigma = jax.nn.sigmoid(pre)
     dsilu[...] = sigma * (1.0 + pre * (1.0 - sigma))
     activ = masked((pre * sigma).astype(BF16).astype(F32), 1)
-    act3[0] = jnp.zeros((PITCH, 768), BF16)
-    act3[EXT - 1] = jnp.zeros((PITCH, 768), BF16)
+    act3[0:PITCH] = jnp.zeros((PITCH, 768), F32)
+    act3[19 * PITCH : EXT * PITCH] = jnp.zeros((PITCH, 768), F32)
     for b, part in enumerate(three(activ)):
-        act3[1:19, :, 256 * b : 256 * b + 256] = part.reshape(18, PITCH, 256).astype(BF16)
+        act3[PITCH : 19 * PITCH, 256 * b : 256 * b + 256] = part
     actc[...] = flat(core_of(activ)[1:17]).astype(BF16)
 
     for par in range(2):
         a, b, c = four(flat(ext[1 + par]))
-        cot4[par, :, :, 0:128] = a.reshape(EXT, PITCH, 128).astype(BF16)
-        cot4[par, :, :, 128:384] = b.reshape(EXT, PITCH, 256).astype(BF16)
-        cot4[par, :, :, 384:512] = c.reshape(EXT, PITCH, 128).astype(BF16)
+        cot4[par, 0 : EXT * PITCH, 0:128] = a
+        cot4[par, 0 : EXT * PITCH, 128:384] = b
+        cot4[par, 0 : EXT * PITCH, 384:512] = c
+        cot4[par, EXT * PITCH :] = jnp.zeros((8, 512), F32)
     for par in range(2):
         first = 1 - par
-        total = jnp.zeros((19 * PITCH, 256), F32)
+        total = jnp.zeros((19 * PITCH + 8, 256), F32)
         for a in range(3):
             src, shift = fine_row(par + a - 1)
             weight = pair_weight_back([flip_ref[a, b] for b in range(3)], zero)
-            total = total + nt(flat(cot4[src, first + shift : first + shift + 19]), weight)
+            start = (first + shift) * PITCH
+            rows = cot4[src, start : start + 19 * PITCH + 8].astype(BF16)
+            total = total + nt(rows, weight)
+        total = total[: 19 * PITCH]
         grad = masked(total.astype(BF16).astype(F32), first)
         a, b, c = four(grad)
-        mg4[par, first : first + 19, :, 0:128] = a.reshape(19, PITCH, 128).astype(BF16)
-        mg4[par, first : first + 19, :, 128:384] = b.reshape(19, PITCH, 256).astype(BF16)
-        mg4[par, first : first + 19, :, 384:512] = c.reshape(19, PITCH, 128).astype(BF16)
+        rows = slice(first * PITCH, (first + 19) * PITCH)
+        mg4[par, rows, 0:128] = a
+        mg4[par, rows, 128:384] = b
+        mg4[par, rows, 384:512] = c
         mg4c[par, first : first + 19, :, 0:128] = core_of(a).astype(BF16)
         mg4c[par, first : first + 19, :, 128:384] = core_of(b).astype(BF16)
         mg4c[par, first : first + 19, :, 384:512] = core_of(c).astype(BF16)
@@ -352,7 +359,7 @@
     for a in range(4):
         src, shift = fine_row(a - 1)
         weight = jnp.concatenate([uk_ref[a, 3 - b] for b in range(4)], axis=1)
-        agrad = agrad + nt(flat(mg4[src, 1 + shift : 19 + shift]), weight)
+        agrad = agrad + nt(rows_of(mg4.at[src], 1 + shift, 18), weight)
     pgrad = masked((agrad * dsilu[...]).astype(BF16).astype(F32), 1)
     for b, part in enumerate(three(pgrad)):
         pg3c[:, :, 256 * b : 256 * b + 256] = core_of(part).astype(BF16)
@@ -376,7 +383,7 @@
                 ],
                 axis=1,
             )
-            total = total + nn(flat(act3[1 + shift : 19 + shift]), weight)
+            total = total + nn(rows_of(act3, 1 + shift, 18), weight)
         mixed = masked(total.astype(BF16).astype(F32), 1)
         a, b, c = four(mixed)
         mix4c[par, :, :, 0:128] = core_of(a).astype(BF16)
@@ -454,13 +461,13 @@
         out_specs=(vmem, vmem, anywhere, anywhere),
         scratch_shapes=[
             pltpu.VMEM((5, EXT, PITCH, 256), F32),
-            pltpu.VMEM((EXT, PITCH, 768), BF16),
+            pltpu.VMEM((EXT * PITCH, 768), F32),
             pltpu.VMEM((18, TILE, 768), BF16),
-            pltpu.VMEM((EXT, PITCH, 768), BF16),
+            pltpu.VMEM((EXT * PITCH, 768), F32),
             pltpu.VMEM((TILE * TILE, 256), BF16),
             pltpu.VMEM((18 * PITCH, 256), F32),
-            pltpu.VMEM((2, EXT, PITCH, 512), BF16),
-            pltpu.VMEM((2, EXT, PITCH, 512), BF16),
+            pltpu.VMEM((2, EXT * PITCH + 8, 512), F32),
+            pltpu.VMEM((2, EXT * PITCH, 512), F32),
             pltpu.VMEM((2, EXT, TILE, 512), BF16),
             pltpu.VMEM((TILE * TILE, 256), BF16),
             pltpu.VMEM((2, HALF, 128), BF16),

time: 102 us -> 102 us (level)
  no operation moved by 1% of the time
where the time goes in v10:
time: 102 us; the launch traced here: 101 us
  blocking collectives  52.5 us (51%)
  starting transfers between devices  19.8 us (19%)
  Pallas kernels  16.4 us (16%)
  waiting for transfers between devices  7.47 us (7%)
  local copies, waits for them, and re-layouts  3.65 us (4%)
    all_to_all x2, blocking collectives, exchange(): return lax.all_to_all(x, AXES, 0, 0, axis_index_groups=groups)  52.5 us
    pallas_call x1, Pallas kernels, local_work(): pl.pallas_call(functools.partial(main_kernel, scale), out_shape=tuple((ja...  7.65 us
    ppermute x1, starting transfers between devices, total_over_devices(): far = lax.ppermute(part, AXES, depth_shift(4)).astype(F32)  6.85 us
    ppermute x1, starting transfers between devices, total_over_devices(): return (half, lax.ppermute(half, 'row', CORE_SWAP), rest)  4.55 us
    pallas_call x2, Pallas kernels, unpack(): pl.pallas_call(functools.partial(unpack_kernel, 1 if begun else 0), out_s...  4.16 us
    ppermute x2, starting transfers between devices, swapped(): lax.ppermute(inner, axis, INNER_PAIRS)  3.33 us
    ppermute x2, waiting for transfers between devices, total_over_devices(): lax.ppermute(part, AXES, depth_shift(step)).astype(F32)  2.63 us
    ppermute x2, starting transfers between devices, swapped(): lax.ppermute(outer, axis, OUTER_PAIRS)  2.56 us
  transfers between devices with their start and end apart: 9, of which 6 were waited for; matrix products, arithmetic and copies ran while one was open for 3% of the time, Pallas kernels for 4%

profile of v10, /device:TPU:1, one launch (start us, length us, event | category | flops | bytes accessed | tf_op | source)
XLA Modules:
  0.0 101.2 jit_solution(3593434630588090056)
XLA Ops:
  0.6 2.2 %shard_map.101 = (bf16[5,16,16,256]{3,2,1,0:T(8,128)(2,1)}, bf16[7,16,256]{2,1,0:T(8,128)(2,1)}, bf16[7,16,256]{2,1,0:T(8,128)(2,1)}, bf16[2,78,2,256]{3,2,1,0:T(2,128)(2,1)}) custom-call(bf16[16,16,256]{2,1,0:T(8,128)(2,1)} %bot_hbm.1, bf16[32,32,128]{2,1,0:T(8,128)(2,1)} %skip_hbm.1, bf16[32,32,128]{2,1,0:T(8,128)(2,1)} %cot_hbm.1), custom_call_target="tpu_custom_call" | custom-call | tf_op jit(solution)/shard_map/pallas_call | solution.py:130
  2.8 3.3 %collective-permute-start = (bf16[7,16,256]{2,1,0:T(8,128)(2,1)}, bf16[7,16,256]{2,1,0:T(8,128)(2,1)S(1)}, u32[]{:S(2)}, u32[]{:S(2)}) collective-permute-start(bf16[7,16,256]{2,1,0:T(8,128)(2,1)} %get-tuple-element.30), channel_id=1, source_target_pairs={{0,16},{16,0},{32,48},{48,32},{64,80},{80,64},{96,112},{112,96},{1... | collective-permute-start | bytes 172040 | tf_op jit(solution)/shard_map/ppermute | solution.py:534
  6.1 1.9 %collective-permute-start.1 = (bf16[7,16,256]{2,1,0:T(8,128)(2,1)}, bf16[7,16,256]{2,1,0:T(8,128)(2,1)S(1)}, u32[]{:S(2)}, u32[]{:S(2)}) collective-permute-start(bf16[7,16,256]{2,1,0:T(8,128)(2,1)} %get-tuple-element.31), channel_id=1, source_target_pairs={{16,32},{32,16},{48,64},{64,48},{80,96},{96,80},{112,128},{128,112... | collective-permute-start | bytes 172040 | tf_op jit(solution)/shard_map/ppermute | solution.py:534
  8.1 1.0 rev.15.flip_ref
  9.0 1.0 %rev.13.own = bf16[2,78,2,256]{3,2,1,0:T(2,128)(2,1)S(1)} reverse(bf16[2,78,2,256]{3,2,1,0:T(2,128)(2,1)} %get-tuple-element.36), dimensions={0} | reverse | bytes 319488 | tf_op jit(solution)/shard_map/rev | solution.py:560
  10.1 1.7 %collective-permute-done.1.got_outer.row_out = bf16[7,16,256]{2,1,0:T(8,128)(2,1)S(1)} collective-permute-done((bf16[7,16,256]{2,1,0:T(8,128)(2,1)}, bf16[7,16,256]{2,1,0:T(8,128)(2,1)S(1)}, u32[]{:S(2)}, u32[]{:S(2)}) %collective-permute-start.1) | collective-permute-done | bytes 57376 | tf_op jit(solution)/shard_map/ppermute | solution.py:534
  11.8 0.7 shard_map.102
  12.5 0.7 collective-permute-start.3
  13.4 1.4 %rev.14.uk_ref = bf16[4,4,256,128]{3,2,1,0:T(8,128)(2,1)S(1)} reverse(bf16[4,4,256,128]{3,2,1,0:T(8,128)(2,1)} %param.10), dimensions={1} | reverse | bytes 2097152 | tf_op jit(solution)/shard_map/rev | solution.py:559
  14.8 1.2 %collective-permute-done.2.col_in = bf16[78,2,256]{2,1,0:T(2,128)(2,1)S(1)} collective-permute-done((bf16[78,2,256]{2,1,0:T(2,128)(2,1)}, bf16[78,2,256]{2,1,0:T(2,128)(2,1)S(1)}, u32[]{:S(2)}, u32[]{:S(2)}) %collective-permute-start.2) | collective-permute-done | bytes 79904 | tf_op jit(solution)/shard_map/ppermute | solution.py:534
  16.0 7.7 %shard_map.103 = (bf16[2,18,16,512]{3,2,1,0:T(8,128)(2,1)S(1)}, bf16[18,16,768]{2,1,0:T(8,128)(2,1)S(1)}, bf16[5120,128]{1,0:T(8,128)(2,1)S(1)}, bf16[5120,128]{1,0:T(8,128)(2,1)S(1)}) custom-call(s32[5]{0:T(128)S(1)} %pad_add_fusion.pos_ref, bf16[5,16,16,256]{3,2,1,0:T(8,128)(2,1)S(1)} %rev.12.z_ref, ...), custom_call_target="tpu_custom_call" | custom-call | tf_op jit(solution)/shard_map/pallas_call | solution.py:457
  23.8 1.7 %shard_map.104 = (bf16[32,32,128]{2,1,0:T(8,128)(2,1)}, bf16[16,16,256]{2,1,0:T(8,128)(2,1)}) custom-call(bf16[2,18,16,512]{3,2,1,0:T(8,128)(2,1)S(1)} %get-tuple-element.41.mix4c, bf16[18,16,768]{2,1,0:T(8,128)(2,1)S(1)} %get-tuple-element.42.pg3c, bf16[3,3,256,256]{3,2,1,0:T(8,128)(2,1)S(1)} %copy-done, bf16[3,3,128,128]{3,2,1,0:T(8,128)(2,1)S(1)} %copy-done.1), custom_call_target="tpu_custom_call" | custom-call | flops 1000000000 | bytes 3000000 | tf_op jit(solution)/shard_map/pallas_call | solution.py:439
  25.5 1.3 %collective-permute-done.4 = bf16[5120,128]{1,0:T(8,128)(2,1)S(1)} collective-permute-done((bf16[5120,128]{1,0:T(8,128)(2,1)S(1)}, bf16[5120,128]{1,0:T(8,128)(2,1)S(1)}, u32[]{:S(2)}, u32[]{:S(2)}) %collective-permute-start.4) | collective-permute-done | bytes 1310752 | tf_op jit(solution)/shard_map/ppermute | solution.py:542
  26.8 0.3 add_convert_fusion
  27.1 31.5 %all_to_all.10 = bf16[32,160,128]{2,1,0:T(8,128)(2,1)S(1)} all-to-all(bf16[32,160,128]{2,1,0:T(8,128)(2,1)S(1)} %bitcast.10), channel_id=1, replica_groups={{0,1,128,129,32,33,160,161,64,65,192,193,96,97,224,225,2,3,130,131,34,3..., dimensions={0} | all-to-all | bytes 2621440 | tf_op jit(solution)/shard_map/all_to_all | solution.py:538
  58.8 6.9 %collective-permute-start.7 = (bf16[160,128]{1,0:T(8,128)(2,1)S(1)}, bf16[160,128]{1,0:T(8,128)(2,1)S(1)}, u32[]{:S(2)}, u32[]{:S(2)}) collective-permute-start(bf16[160,128]{1,0:T(8,128)(2,1)S(1)} %reduce_sum.12), channel_id=1, source_target_pairs={{0,8},{16,24},{2,10},{18,26},{4,12},{20,28},{6,14},{22,30},{8,0},{... | collective-permute-start | bytes 122888 | tf_op jit(solution)/shard_map/ppermute | solution.py:546
  65.7 2.4 %collective-permute-start.5 = (bf16[160,128]{1,0:T(8,128)(2,1)S(1)}, bf16[160,128]{1,0:T(8,128)(2,1)S(1)}, u32[]{:S(2)}, u32[]{:S(2)}) collective-permute-start(bf16[160,128]{1,0:T(8,128)(2,1)S(1)} %reduce_sum.12), channel_id=1, source_target_pairs={{0,4},{16,20},{2,6},{18,22},{4,8},{20,24},{6,10},{22,26},{8,12},{2... | collective-permute-start | bytes 122888 | tf_op jit(solution)/shard_map/ppermute | solution.py:547
  68.0 1.8 %collective-permute-done.6 = bf16[160,128]{1,0:T(8,128)(2,1)S(1)} collective-permute-done((bf16[160,128]{1,0:T(8,128)(2,1)S(1)}, bf16[160,128]{1,0:T(8,128)(2,1)S(1)}, u32[]{:S(2)}, u32[]{:S(2)}) %collective-permute-start.6) | collective-permute-done | bytes 40992 | tf_op jit(solution)/shard_map/ppermute | solution.py:547
  69.8 0.9 collective-permute-done.5
  70.9 21.0 %all_to_all.11 = bf16[32,160,128]{2,1,0:T(8,128)(2,1)S(1)} all-to-all(bf16[32,160,128]{2,1,0:T(8,128)(2,1)S(1)} %broadcast_in_dim.2), channel_id=1, replica_groups={{0,1,128,129,32,33,160,161,64,65,192,193,96,97,224,225,2,3,130,131,34,3..., dimensions={0} | all-to-all | bytes 2621440 | tf_op jit(solution)/shard_map/all_to_all | solution.py:538
  91.9 4.6 %collective-permute-start.8 = (bf16[5120,128]{1,0:T(8,128)(2,1)S(1)}, bf16[5120,128]{1,0:T(8,128)(2,1)S(1)}, u32[]{:S(2)}, u32[]{:S(2)}) collective-permute-start(bf16[5120,128]{1,0:T(8,128)(2,1)S(1)} %bitcast.8), channel_id=1, source_target_pairs={{0,16},{16,0},{32,48},{48,32},{64,80},{80,64},{96,112},{112,96},{1... | collective-permute-start | bytes 3932168 | tf_op jit(solution)/shard_map/ppermute | solution.py:550
  96.5 2.1 %shard_map.105 = (f32[4096,128]{1,0:T(8,128)}, f32[2304,256]{1,0:T(8,128)}, f32[1152,128]{1,0:T(8,128)}) custom-call(s32[5]{0:T(128)S(1)} %pad_add_fusion.pos_ref, bf16[5120,128]{1,0:T(8,128)(2,1)S(1)} %bitcast.9), custom_call_target="tpu_custom_call" | custom-call | bytes 4000000 | tf_op jit(solution)/shard_map/pallas_call | solution.py:520
  98.6 0.6 collective-permute-done.8.half
  99.1 2.1 %shard_map.106 = (f32[4096,128]{1,0:T(8,128)}, f32[2304,256]{1,0:T(8,128)}, f32[1152,128]{1,0:T(8,128)}) custom-call(s32[5]{0:T(128)S(1)} %pad_add_fusion.pos_ref, bf16[5120,128]{1,0:T(8,128)(2,1)S(1)} %collective-permute-done.8.half, f32[4096,128]{1,0:T(8,128)} %get-tuple-element.49.refs_0_, ...), custom_call_target="tpu_custom_call", output_to_operand_aliasing={{0}: (2, {}), {1}: (3, {}), {2}: (4, {})} | custom-call | bytes 4000000 | tf_op jit(solution)/shard_map/pallas_call | solution.py:520
  (18 shorter events, 0.6 us)
Async XLA Ops:
  2.8 10.5 %copy-start.2 = (bf16[5,16,16,256]{3,2,1,0:T(8,128)(2,1)S(1)}, bf16[5,16,16,256]{3,2,1,0:T(8,128)(2,1)}, u32[]{:S(2)}) copy-start(bf16[5,16,16,256]{3,2,1,0:T(8,128)(2,1)} %get-tuple-element.33) | copy-start | bytes 1966084
  2.8 7.3 %collective-permute-start = (bf16[7,16,256]{2,1,0:T(8,128)(2,1)}, bf16[7,16,256]{2,1,0:T(8,128)(2,1)S(1)}, u32[]{:S(2)}, u32[]{:S(2)}) collective-permute-start(bf16[7,16,256]{2,1,0:T(8,128)(2,1)} %get-tuple-element.30), channel_id=1, source_target_pairs={{0,16},{16,0},{32,48},{48,32},{64,80},{80,64},{96,112},{112,96},{1... | collective-permute-start | bytes 172040 | tf_op jit(solution)/shard_map/ppermute | solution.py:534
  6.1 5.7 %collective-permute-start.1 = (bf16[7,16,256]{2,1,0:T(8,128)(2,1)}, bf16[7,16,256]{2,1,0:T(8,128)(2,1)S(1)}, u32[]{:S(2)}, u32[]{:S(2)}) collective-permute-start(bf16[7,16,256]{2,1,0:T(8,128)(2,1)} %get-tuple-element.31), channel_id=1, source_target_pairs={{16,32},{32,16},{48,64},{64,48},{80,96},{96,80},{112,128},{128,112... | collective-permute-start | bytes 172040 | tf_op jit(solution)/shard_map/ppermute | solution.py:534
  12.5 3.5 %collective-permute-start.2 = (bf16[78,2,256]{2,1,0:T(2,128)(2,1)}, bf16[78,2,256]{2,1,0:T(2,128)(2,1)S(1)}, u32[]{:S(2)}, u32[]{:S(2)}) collective-permute-start(bf16[78,2,256]{2,1,0:T(2,128)(2,1)} %get-tuple-element.37), channel_id=1, source_target_pairs={{0,1},{1,0},{2,3},{3,2},{4,5},{5,4},{6,7},{7,6},{8,9},{9,8},{10,11... | collective-permute-start | bytes 239624 | tf_op jit(solution)/shard_map/ppermute | solution.py:534
  12.5 3.5 %collective-permute-start.3 = (bf16[78,2,256]{2,1,0:T(2,128)(2,1)S(1)}, bf16[78,2,256]{2,1,0:T(2,128)(2,1)S(1)}, u32[]{:S(2)}, u32[]{:S(2)}) collective-permute-start(bf16[78,2,256]{2,1,0:T(2,128)(2,1)S(1)} %get-tuple-element.38), channel_id=1, source_target_pairs={{1,2},{2,1},{3,4},{4,3},{5,6},{6,5},{7,8},{8,7},{9,10},{10,9},{11,... | collective-permute-start | bytes 239624 | tf_op jit(solution)/shard_map/ppermute | solution.py:534
  13.3 2.7 %copy-start = (bf16[3,3,256,256]{3,2,1,0:T(8,128)(2,1)S(1)}, bf16[3,3,256,256]{3,2,1,0:T(8,128)(2,1)}, u32[]{:S(2)}) copy-start(bf16[3,3,256,256]{3,2,1,0:T(8,128)(2,1)} %bk_ref.3) | copy-start | bytes 3538948
  14.8 9.0 %copy-start.1 = (bf16[3,3,128,128]{3,2,1,0:T(8,128)(2,1)S(1)}, bf16[3,3,128,128]{3,2,1,0:T(8,128)(2,1)}, u32[]{:S(2)}) copy-start(bf16[3,3,128,128]{3,2,1,0:T(8,128)(2,1)} %lk_ref.1) | copy-start | bytes 884740
  23.7 3.1 %collective-permute-start.4 = (bf16[5120,128]{1,0:T(8,128)(2,1)S(1)}, bf16[5120,128]{1,0:T(8,128)(2,1)S(1)}, u32[]{:S(2)}, u32[]{:S(2)}) collective-permute-start(bf16[5120,128]{1,0:T(8,128)(2,1)S(1)} %get-tuple-element.40), channel_id=1, source_target_pairs={{0,16},{16,0},{32,48},{48,32},{64,80},{80,64},{96,112},{112,96},{1... | collective-permute-start | bytes 3932168 | tf_op jit(solution)/shard_map/ppermute | solution.py:542
  58.8 9.2 %collective-permute-start.7 = (bf16[160,128]{1,0:T(8,128)(2,1)S(1)}, bf16[160,128]{1,0:T(8,128)(2,1)S(1)}, u32[]{:S(2)}, u32[]{:S(2)}) collective-permute-start(bf16[160,128]{1,0:T(8,128)(2,1)S(1)} %reduce_sum.12), channel_id=1, source_target_pairs={{0,8},{16,24},{2,10},{18,26},{4,12},{20,28},{6,14},{22,30},{8,0},{... | collective-permute-start | bytes 122888 | tf_op jit(solution)/shard_map/ppermute | solution.py:546
  65.7 4.1 %collective-permute-start.6 = (bf16[160,128]{1,0:T(8,128)(2,1)S(1)}, bf16[160,128]{1,0:T(8,128)(2,1)S(1)}, u32[]{:S(2)}, u32[]{:S(2)}) collective-permute-start(bf16[160,128]{1,0:T(8,128)(2,1)S(1)} %reduce_sum.12), channel_id=1, source_target_pairs={{0,12},{16,28},{2,14},{18,30},{4,0},{20,16},{6,2},{22,18},{8,4},{2... | collective-permute-start | bytes 122888 | tf_op jit(solution)/shard_map/ppermute | solution.py:547
  65.7 5.0 %collective-permute-start.5 = (bf16[160,128]{1,0:T(8,128)(2,1)S(1)}, bf16[160,128]{1,0:T(8,128)(2,1)S(1)}, u32[]{:S(2)}, u32[]{:S(2)}) collective-permute-start(bf16[160,128]{1,0:T(8,128)(2,1)S(1)} %reduce_sum.12), channel_id=1, source_target_pairs={{0,4},{16,20},{2,6},{18,22},{4,8},{20,24},{6,10},{22,26},{8,12},{2... | collective-permute-start | bytes 122888 | tf_op jit(solution)/shard_map/ppermute | solution.py:547
  91.9 7.2 %collective-permute-start.8 = (bf16[5120,128]{1,0:T(8,128)(2,1)S(1)}, bf16[5120,128]{1,0:T(8,128)(2,1)S(1)}, u32[]{:S(2)}, u32[]{:S(2)}) collective-permute-start(bf16[5120,128]{1,0:T(8,128)(2,1)S(1)} %bitcast.8), channel_id=1, source_target_pairs={{0,16},{16,0},{32,48},{48,32},{64,80},{80,64},{96,112},{112,96},{1... | collective-permute-start | bytes 3932168 | tf_op jit(solution)/shard_map/ppermute | solution.py:550

commit v11 on v10

--- a/solution.py
+++ b/solution.py
@@ -144,7 +144,7 @@
     )(bottom_in, skip_feat, cotangent)
 
 
-def ends_kernel(own, got_inner, got_outer, inner_ref, outer_ref):
+def ends_kernel(own, got_outer, got_inner, inner_ref, outer_ref):
     inner_ref[...] = own[1]
     outer_ref[...] = own[0]
     got = got_inner[...].astype(F32), got_outer[...].astype(F32)
@@ -240,7 +240,7 @@
 
 
 def main_kernel(
-    scale, pos_ref, z_ref, row_in, row_out, col_in, col_out, bk_ref, uk_ref, flip_ref,
+    scale, pos_ref, z_ref, row_out, row_in, col_out, col_in, bk_ref, uk_ref, flip_ref,
     mix4c, pg3c, keep_ref, send_ref,
     ext, bot3, botc, act3, actc, dsilu, cot4, mg4, mg4c, pgc, packed, inside, sems,
 ):
@@ -531,7 +531,8 @@
 
 
 def swapped(inner, outer, axis):
-    return lax.ppermute(inner, axis, INNER_PAIRS), lax.ppermute(outer, axis, OUTER_PAIRS)
+    got_outer = lax.ppermute(outer, axis, OUTER_PAIRS)
+    return got_outer, lax.ppermute(inner, axis, INNER_PAIRS)
 
 
 def exchange(x, groups):

time: 102 us -> 102 us (level)
  starting transfers between devices: 19.8 us -> 22.7 us
  blocking collectives: 52.5 us -> 50 us
    ppermute x4, starting transfers between devices: 5.89 us -> 9.54 us  [the longest x2 5.29 us: swapped(): got_outer = lax.ppermute(outer, axis, OUTER_PAIRS)]
    all_to_all x2, blocking collectives: 52.5 us -> 50 us  [exchange(): return lax.all_to_all(x, AXES, 0, 0, axis_index_groups=groups)]
    ppermute x2, waiting for transfers between devices: 2.63 us -> 4.53 us  [total_over_devices(): lax.ppermute(part, AXES, depth_shift(step)).astype(F32)]
    ppermute x4, waiting for transfers between devices: 2.97 us -> 1.69 us  [the longest x2 1.69 us: swapped(): return (got_outer, lax.ppermute(inner, axis, INNER_PAIRS))]
  transfers between devices with their start and end apart: 9 -> 9, of which waited for: 6 -> 5; matrix products, arithmetic and copies ran while one was open for 3% -> 3% of each run, Pallas kernels for 4% -> 4%
where the time goes in v11:
time: 102 us
  blocking collectives  50 us (49%)
  starting transfers between devices  22.7 us (22%)
  Pallas kernels  16.4 us (16%)
  waiting for transfers between devices  7.73 us (8%)
  local copies, waits for them, and re-layouts  3.65 us (4%)
    all_to_all x2, blocking collectives, exchange(): return lax.all_to_all(x, AXES, 0, 0, axis_index_groups=groups)  50 us
    pallas_call x1, Pallas kernels, local_work(): pl.pallas_call(functools.partial(main_kernel, scale), out_shape=tuple((ja...  7.65 us
    ppermute x1, starting transfers between devices, total_over_devices(): far = lax.ppermute(part, AXES, depth_shift(4)).astype(F32)  6.03 us
    ppermute x2, starting transfers between devices, swapped(): got_outer = lax.ppermute(outer, axis, OUTER_PAIRS)  5.29 us
    ppermute x2, waiting for transfers between devices, total_over_devices(): lax.ppermute(part, AXES, depth_shift(step)).astype(F32)  4.53 us
    ppermute x2, starting transfers between devices, swapped(): return (got_outer, lax.ppermute(inner, axis, INNER_PAIRS))  4.24 us
    pallas_call x2, Pallas kernels, unpack(): pl.pallas_call(functools.partial(unpack_kernel, 1 if begun else 0), out_s...  4.16 us
    ppermute x1, starting transfers between devices, total_over_devices(): return (half, lax.ppermute(half, 'row', CORE_SWAP), rest)  4.15 us
  transfers between devices with their start and end apart: 9, of which 5 were waited for; matrix products, arithmetic and copies ran while one was open for 3% of the time, Pallas kernels for 4%

profile of v11, /device:TPU:1, one launch (start us, length us, event | category | flops | bytes accessed | tf_op | source)
XLA Modules:
  0.0 101.9 jit_solution(411654177377449919)
XLA Ops:
  0.6 2.2 %shard_map.101 = (bf16[5,16,16,256]{3,2,1,0:T(8,128)(2,1)}, bf16[7,16,256]{2,1,0:T(8,128)(2,1)}, bf16[7,16,256]{2,1,0:T(8,128)(2,1)}, bf16[2,78,2,256]{3,2,1,0:T(2,128)(2,1)}) custom-call(bf16[16,16,256]{2,1,0:T(8,128)(2,1)} %bot_hbm.1, bf16[32,32,128]{2,1,0:T(8,128)(2,1)} %skip_hbm.1, bf16[32,32,128]{2,1,0:T(8,128)(2,1)} %cot_hbm.1), custom_call_target="tpu_custom_call" | custom-call | tf_op jit(solution)/shard_map/pallas_call | solution.py:130
  2.8 4.6 %collective-permute-start = (bf16[7,16,256]{2,1,0:T(8,128)(2,1)}, bf16[7,16,256]{2,1,0:T(8,128)(2,1)S(1)}, u32[]{:S(2)}, u32[]{:S(2)}) collective-permute-start(bf16[7,16,256]{2,1,0:T(8,128)(2,1)} %get-tuple-element.30), channel_id=1, source_target_pairs={{16,32},{32,16},{48,64},{64,48},{80,96},{96,80},{112,128},{128,112... | collective-permute-start | bytes 172040 | tf_op jit(solution)/shard_map/ppermute | solution.py:534
  7.6 1.0 rev.15.flip_ref
  8.6 1.0 %rev.13.own = bf16[2,78,2,256]{3,2,1,0:T(2,128)(2,1)S(1)} reverse(bf16[2,78,2,256]{3,2,1,0:T(2,128)(2,1)} %get-tuple-element.36), dimensions={0} | reverse | bytes 319488 | tf_op jit(solution)/shard_map/rev | solution.py:561
  9.6 0.7 shard_map.102
  10.3 0.7 collective-permute-start.2
  11.0 4.1 %collective-permute-start.3 = (bf16[78,2,256]{2,1,0:T(2,128)(2,1)S(1)}, bf16[78,2,256]{2,1,0:T(2,128)(2,1)S(1)}, u32[]{:S(2)}, u32[]{:S(2)}) collective-permute-start(bf16[78,2,256]{2,1,0:T(2,128)(2,1)S(1)} %get-tuple-element.38), channel_id=1, source_target_pairs={{0,1},{1,0},{2,3},{3,2},{4,5},{5,4},{6,7},{7,6},{8,9},{9,8},{10,11... | collective-permute-start | bytes 239624 | tf_op jit(solution)/shard_map/ppermute | solution.py:535
  15.3 1.4 %rev.14.uk_ref = bf16[4,4,256,128]{3,2,1,0:T(8,128)(2,1)S(1)} reverse(bf16[4,4,256,128]{3,2,1,0:T(8,128)(2,1)} %param.10), dimensions={1} | reverse | bytes 2097152 | tf_op jit(solution)/shard_map/rev | solution.py:560
  16.7 1.7 %collective-permute-done.3.col_in = bf16[78,2,256]{2,1,0:T(2,128)(2,1)S(1)} collective-permute-done((bf16[78,2,256]{2,1,0:T(2,128)(2,1)S(1)}, bf16[78,2,256]{2,1,0:T(2,128)(2,1)S(1)}, u32[]{:S(2)}, u32[]{:S(2)}) %collective-permute-start.3) | collective-permute-done | bytes 79904 | tf_op jit(solution)/shard_map/ppermute | solution.py:535
  18.4 7.6 %shard_map.103 = (bf16[2,18,16,512]{3,2,1,0:T(8,128)(2,1)S(1)}, bf16[18,16,768]{2,1,0:T(8,128)(2,1)S(1)}, bf16[5120,128]{1,0:T(8,128)(2,1)S(1)}, bf16[5120,128]{1,0:T(8,128)(2,1)S(1)}) custom-call(s32[5]{0:T(128)S(1)} %pad_add_fusion.pos_ref, bf16[5,16,16,256]{3,2,1,0:T(8,128)(2,1)S(1)} %rev.12.z_ref, ...), custom_call_target="tpu_custom_call" | custom-call | tf_op jit(solution)/shard_map/pallas_call | solution.py:457
  26.0 0.7 collective-permute-start.4
  26.7 1.7 %shard_map.104 = (bf16[32,32,128]{2,1,0:T(8,128)(2,1)}, bf16[16,16,256]{2,1,0:T(8,128)(2,1)}) custom-call(bf16[2,18,16,512]{3,2,1,0:T(8,128)(2,1)S(1)} %get-tuple-element.41.mix4c, bf16[18,16,768]{2,1,0:T(8,128)(2,1)S(1)} %get-tuple-element.42.pg3c, bf16[3,3,256,256]{3,2,1,0:T(8,128)(2,1)S(1)} %copy-done, bf16[3,3,128,128]{3,2,1,0:T(8,128)(2,1)S(1)} %copy-done.1), custom_call_target="tpu_custom_call" | custom-call | flops 1000000000 | bytes 3000000 | tf_op jit(solution)/shard_map/pallas_call | solution.py:439
  28.4 1.0 collective-permute-done.4
  29.7 28.7 %all_to_all.10 = bf16[32,160,128]{2,1,0:T(8,128)(2,1)S(1)} all-to-all(bf16[32,160,128]{2,1,0:T(8,128)(2,1)S(1)} %bitcast.10), channel_id=1, replica_groups={{0,1,128,129,32,33,160,161,64,65,192,193,96,97,224,225,2,3,130,131,34,3..., dimensions={0} | all-to-all | bytes 2621440 | tf_op jit(solution)/shard_map/all_to_all | solution.py:539
  58.6 6.0 %collective-permute-start.7 = (bf16[160,128]{1,0:T(8,128)(2,1)S(1)}, bf16[160,128]{1,0:T(8,128)(2,1)S(1)}, u32[]{:S(2)}, u32[]{:S(2)}) collective-permute-start(bf16[160,128]{1,0:T(8,128)(2,1)S(1)} %reduce_sum.12), channel_id=1, source_target_pairs={{0,8},{16,24},{2,10},{18,26},{4,12},{20,28},{6,14},{22,30},{8,0},{... | collective-permute-start | bytes 122888 | tf_op jit(solution)/shard_map/ppermute | solution.py:547
  64.6 1.5 %collective-permute-start.6 = (bf16[160,128]{1,0:T(8,128)(2,1)S(1)}, bf16[160,128]{1,0:T(8,128)(2,1)S(1)}, u32[]{:S(2)}, u32[]{:S(2)}) collective-permute-start(bf16[160,128]{1,0:T(8,128)(2,1)S(1)} %reduce_sum.12), channel_id=1, source_target_pairs={{0,12},{16,28},{2,14},{18,30},{4,0},{20,16},{6,2},{22,18},{8,4},{2... | collective-permute-start | bytes 122888 | tf_op jit(solution)/shard_map/ppermute | solution.py:548
  66.1 0.8 collective-permute-start.5
  67.0 2.5 %collective-permute-done.6 = bf16[160,128]{1,0:T(8,128)(2,1)S(1)} collective-permute-done((bf16[160,128]{1,0:T(8,128)(2,1)S(1)}, bf16[160,128]{1,0:T(8,128)(2,1)S(1)}, u32[]{:S(2)}, u32[]{:S(2)}) %collective-permute-start.6) | collective-permute-done | bytes 40992 | tf_op jit(solution)/shard_map/ppermute | solution.py:548
  69.5 2.0 %collective-permute-done.5 = bf16[160,128]{1,0:T(8,128)(2,1)S(1)} collective-permute-done((bf16[160,128]{1,0:T(8,128)(2,1)S(1)}, bf16[160,128]{1,0:T(8,128)(2,1)S(1)}, u32[]{:S(2)}, u32[]{:S(2)}) %collective-permute-start.5) | collective-permute-done | bytes 40992 | tf_op jit(solution)/shard_map/ppermute | solution.py:548
  71.7 21.3 %all_to_all.11 = bf16[32,160,128]{2,1,0:T(8,128)(2,1)S(1)} all-to-all(bf16[32,160,128]{2,1,0:T(8,128)(2,1)S(1)} %broadcast_in_dim.2), channel_id=1, replica_groups={{0,1,128,129,32,33,160,161,64,65,192,193,96,97,224,225,2,3,130,131,34,3..., dimensions={0} | all-to-all | bytes 2621440 | tf_op jit(solution)/shard_map/all_to_all | solution.py:539
  93.0 4.1 %collective-permute-start.8 = (bf16[5120,128]{1,0:T(8,128)(2,1)S(1)}, bf16[5120,128]{1,0:T(8,128)(2,1)S(1)}, u32[]{:S(2)}, u32[]{:S(2)}) collective-permute-start(bf16[5120,128]{1,0:T(8,128)(2,1)S(1)} %bitcast.8), channel_id=1, source_target_pairs={{0,16},{16,0},{32,48},{48,32},{64,80},{80,64},{96,112},{112,96},{1... | collective-permute-start | bytes 3932168 | tf_op jit(solution)/shard_map/ppermute | solution.py:551
  97.2 2.1 %shard_map.105 = (f32[4096,128]{1,0:T(8,128)}, f32[2304,256]{1,0:T(8,128)}, f32[1152,128]{1,0:T(8,128)}) custom-call(s32[5]{0:T(128)S(1)} %pad_add_fusion.pos_ref, bf16[5120,128]{1,0:T(8,128)(2,1)S(1)} %bitcast.9), custom_call_target="tpu_custom_call" | custom-call | bytes 4000000 | tf_op jit(solution)/shard_map/pallas_call | solution.py:520
  99.3 0.6 collective-permute-done.8.half
  99.8 2.1 %shard_map.106 = (f32[4096,128]{1,0:T(8,128)}, f32[2304,256]{1,0:T(8,128)}, f32[1152,128]{1,0:T(8,128)}) custom-call(s32[5]{0:T(128)S(1)} %pad_add_fusion.pos_ref, bf16[5120,128]{1,0:T(8,128)(2,1)S(1)} %collective-permute-done.8.half, f32[4096,128]{1,0:T(8,128)} %get-tuple-element.49.refs_0_, ...), custom_call_target="tpu_custom_call", output_to_operand_aliasing={{0}: (2, {}), {1}: (3, {}), {2}: (4, {})} | custom-call | bytes 4000000 | tf_op jit(solution)/shard_map/pallas_call | solution.py:520
  (18 shorter events, 1.0 us)
Async XLA Ops:
  2.8 12.4 %copy-start.2 = (bf16[5,16,16,256]{3,2,1,0:T(8,128)(2,1)S(1)}, bf16[5,16,16,256]{3,2,1,0:T(8,128)(2,1)}, u32[]{:S(2)}) copy-start(bf16[5,16,16,256]{3,2,1,0:T(8,128)(2,1)} %get-tuple-element.33) | copy-start | bytes 1966084
  2.8 6.8 %collective-permute-start = (bf16[7,16,256]{2,1,0:T(8,128)(2,1)}, bf16[7,16,256]{2,1,0:T(8,128)(2,1)S(1)}, u32[]{:S(2)}, u32[]{:S(2)}) collective-permute-start(bf16[7,16,256]{2,1,0:T(8,128)(2,1)} %get-tuple-element.30), channel_id=1, source_target_pairs={{16,32},{32,16},{48,64},{64,48},{80,96},{96,80},{112,128},{128,112... | collective-permute-start | bytes 172040 | tf_op jit(solution)/shard_map/ppermute | solution.py:534
  7.5 2.1 %collective-permute-start.1 = (bf16[7,16,256]{2,1,0:T(8,128)(2,1)}, bf16[7,16,256]{2,1,0:T(8,128)(2,1)S(1)}, u32[]{:S(2)}, u32[]{:S(2)}) collective-permute-start(bf16[7,16,256]{2,1,0:T(8,128)(2,1)} %get-tuple-element.31), channel_id=1, source_target_pairs={{0,16},{16,0},{32,48},{48,32},{64,80},{80,64},{96,112},{112,96},{1... | collective-permute-start | bytes 172040 | tf_op jit(solution)/shard_map/ppermute | solution.py:535
  10.3 6.4 %collective-permute-start.2 = (bf16[78,2,256]{2,1,0:T(2,128)(2,1)}, bf16[78,2,256]{2,1,0:T(2,128)(2,1)S(1)}, u32[]{:S(2)}, u32[]{:S(2)}) collective-permute-start(bf16[78,2,256]{2,1,0:T(2,128)(2,1)} %get-tuple-element.37), channel_id=1, source_target_pairs={{1,2},{2,1},{3,4},{4,3},{5,6},{6,5},{7,8},{8,7},{9,10},{10,9},{11,... | collective-permute-start | bytes 239624 | tf_op jit(solution)/shard_map/ppermute | solution.py:534
  11.0 7.4 %collective-permute-start.3 = (bf16[78,2,256]{2,1,0:T(2,128)(2,1)S(1)}, bf16[78,2,256]{2,1,0:T(2,128)(2,1)S(1)}, u32[]{:S(2)}, u32[]{:S(2)}) collective-permute-start(bf16[78,2,256]{2,1,0:T(2,128)(2,1)S(1)} %get-tuple-element.38), channel_id=1, source_target_pairs={{0,1},{1,0},{2,3},{3,2},{4,5},{5,4},{6,7},{7,6},{8,9},{9,8},{10,11... | collective-permute-start | bytes 239624 | tf_op jit(solution)/shard_map/ppermute | solution.py:535
  15.3 3.1 %copy-start = (bf16[3,3,256,256]{3,2,1,0:T(8,128)(2,1)S(1)}, bf16[3,3,256,256]{3,2,1,0:T(8,128)(2,1)}, u32[]{:S(2)}) copy-start(bf16[3,3,256,256]{3,2,1,0:T(8,128)(2,1)} %bk_ref.3) | copy-start | bytes 3538948
  16.7 10.0 %copy-start.1 = (bf16[3,3,128,128]{3,2,1,0:T(8,128)(2,1)S(1)}, bf16[3,3,128,128]{3,2,1,0:T(8,128)(2,1)}, u32[]{:S(2)}) copy-start(bf16[3,3,128,128]{3,2,1,0:T(8,128)(2,1)} %lk_ref.1) | copy-start | bytes 884740
  26.0 3.3 %collective-permute-start.4 = (bf16[5120,128]{1,0:T(8,128)(2,1)S(1)}, bf16[5120,128]{1,0:T(8,128)(2,1)S(1)}, u32[]{:S(2)}, u32[]{:S(2)}) collective-permute-start(bf16[5120,128]{1,0:T(8,128)(2,1)S(1)} %get-tuple-element.40), channel_id=1, source_target_pairs={{0,16},{16,0},{32,48},{48,32},{64,80},{80,64},{96,112},{112,96},{1... | collective-permute-start | bytes 3932168 | tf_op jit(solution)/shard_map/ppermute | solution.py:543
  58.6 8.4 %collective-permute-start.7 = (bf16[160,128]{1,0:T(8,128)(2,1)S(1)}, bf16[160,128]{1,0:T(8,128)(2,1)S(1)}, u32[]{:S(2)}, u32[]{:S(2)}) collective-permute-start(bf16[160,128]{1,0:T(8,128)(2,1)S(1)} %reduce_sum.12), channel_id=1, source_target_pairs={{0,8},{16,24},{2,10},{18,26},{4,12},{20,28},{6,14},{22,30},{8,0},{... | collective-permute-start | bytes 122888 | tf_op jit(solution)/shard_map/ppermute | solution.py:547
  64.6 4.9 %collective-permute-start.6 = (bf16[160,128]{1,0:T(8,128)(2,1)S(1)}, bf16[160,128]{1,0:T(8,128)(2,1)S(1)}, u32[]{:S(2)}, u32[]{:S(2)}) collective-permute-start(bf16[160,128]{1,0:T(8,128)(2,1)S(1)} %reduce_sum.12), channel_id=1, source_target_pairs={{0,12},{16,28},{2,14},{18,30},{4,0},{20,16},{6,2},{22,18},{8,4},{2... | collective-permute-start | bytes 122888 | tf_op jit(solution)/shard_map/ppermute | solution.py:548
  66.1 5.4 %collective-permute-start.5 = (bf16[160,128]{1,0:T(8,128)(2,1)S(1)}, bf16[160,128]{1,0:T(8,128)(2,1)S(1)}, u32[]{:S(2)}, u32[]{:S(2)}) collective-permute-start(bf16[160,128]{1,0:T(8,128)(2,1)S(1)} %reduce_sum.12), channel_id=1, source_target_pairs={{0,4},{16,20},{2,6},{18,22},{4,8},{20,24},{6,10},{22,26},{8,12},{2... | collective-permute-start | bytes 122888 | tf_op jit(solution)/shard_map/ppermute | solution.py:548
  93.0 6.8 %collective-permute-start.8 = (bf16[5120,128]{1,0:T(8,128)(2,1)S(1)}, bf16[5120,128]{1,0:T(8,128)(2,1)S(1)}, u32[]{:S(2)}, u32[]{:S(2)}) collective-permute-start(bf16[5120,128]{1,0:T(8,128)(2,1)S(1)} %bitcast.8), channel_id=1, source_target_pairs={{0,16},{16,0},{32,48},{48,32},{64,80},{80,64},{96,112},{112,96},{1... | collective-permute-start | bytes 3932168 | tf_op jit(solution)/shard_map/ppermute | solution.py:551

commit v12 on v11

--- a/solution.py
+++ b/solution.py
@@ -33,9 +33,9 @@
 ]
 
 
-def depth_shift(step):
+def depth_swap(bit):
     return [
-        (place(x, y, z, core), place(x, y, z + step, core))
+        (place(x, y, z, core), place(x, y, z ^ bit, core))
         for x in range(4)
         for y in range(4)
         for z in range(8)
@@ -544,9 +544,10 @@
     half = (keep.astype(F32) + got.astype(F32)).astype(BF16)
     parts = exchange(half.reshape(BLOCK, HALF // BLOCK, 128), BLOCK_GROUPS)
     part = jnp.sum(parts.astype(F32), axis=0).astype(BF16)
-    far = lax.ppermute(part, AXES, depth_shift(4)).astype(F32)
-    near = [lax.ppermute(part, AXES, depth_shift(step)).astype(F32) for step in (2, 6)]
-    total = ((near[0] + near[1]) + (far + part.astype(F32))).astype(BF16)
+    total = part
+    for bit in (2, 4):
+        got = lax.ppermute(total, AXES, depth_swap(bit))
+        total = (total.astype(F32) + got.astype(F32)).astype(BF16)
     half = exchange(jnp.broadcast_to(total[None], parts.shape), BLOCK_GROUPS).reshape(HALF, 128)
     return half, lax.ppermute(half, "row", CORE_SWAP), rest
 

time: 102 us -> 102 us (level)
  starting transfers between devices: 22.7 us -> 24.1 us
  blocking collectives: 50 us -> 48.7 us
    ppermute x1, starting transfers between devices: 4.15 us -> 5.46 us  [total_over_devices(): return (half, lax.ppermute(half, 'row', CORE_SWAP), rest)]
    all_to_all x2, blocking collectives: 50 us -> 48.7 us  [exchange(): return lax.all_to_all(x, AXES, 0, 0, axis_index_groups=groups)]
    ppermute x3 -> x2, waiting for transfers between devices: 4.53 us -> 4.05 us  [total_over_devices(): got = lax.ppermute(total, AXES, depth_swap(bit))]
    ppermute x3 -> x2, starting transfers between devices: 8.4 us -> 8.48 us  [total_over_devices(): got = lax.ppermute(total, AXES, depth_swap(bit))]
  transfers between devices with their start and end apart: 9 -> 8, of which waited for: 5 -> 5; matrix products, arithmetic and copies ran while one was open for 3% -> 3% of each run, Pallas kernels for 4% -> 4%
where the time goes in v12:
time: 102 us
  blocking collectives  48.7 us (48%)
  starting transfers between devices  24.1 us (24%)
  Pallas kernels  16.4 us (16%)
  waiting for transfers between devices  7.26 us (7%)
  local copies, waits for them, and re-layouts  3.65 us (4%)
    all_to_all x2, blocking collectives, exchange(): return lax.all_to_all(x, AXES, 0, 0, axis_index_groups=groups)  48.7 us
    ppermute x2, starting transfers between devices, total_over_devices(): got = lax.ppermute(total, AXES, depth_swap(bit))  8.48 us
    pallas_call x1, Pallas kernels, local_work(): pl.pallas_call(functools.partial(main_kernel, scale), out_shape=tuple((ja...  7.65 us
    ppermute x1, starting transfers between devices, total_over_devices(): return (half, lax.ppermute(half, 'row', CORE_SWAP), rest)  5.46 us
    ppermute x2, starting transfers between devices, swapped(): got_outer = lax.ppermute(outer, axis, OUTER_PAIRS)  5.29 us
    ppermute x2, starting transfers between devices, swapped(): return (got_outer, lax.ppermute(inner, axis, INNER_PAIRS))  4.24 us
    pallas_call x2, Pallas kernels, unpack(): pl.pallas_call(functools.partial(unpack_kernel, 1 if begun else 0), out_s...  4.16 us
    ppermute x2, waiting for transfers between devices, total_over_devices(): got = lax.ppermute(total, AXES, depth_swap(bit))  4.05 us
  transfers between devices with their start and end apart: 8, of which 5 were waited for; matrix products, arithmetic and copies ran while one was open for 3% of the time, Pallas kernels for 4%

profile of v12, /device:TPU:1, one launch (start us, length us, event | category | flops | bytes accessed | tf_op | source)
XLA Modules:
  0.0 101.5 jit_solution(13869557466156903294)
XLA Ops:
  0.6 2.2 %shard_map.101 = (bf16[5,16,16,256]{3,2,1,0:T(8,128)(2,1)}, bf16[7,16,256]{2,1,0:T(8,128)(2,1)}, bf16[7,16,256]{2,1,0:T(8,128)(2,1)}, bf16[2,78,2,256]{3,2,1,0:T(2,128)(2,1)}) custom-call(bf16[16,16,256]{2,1,0:T(8,128)(2,1)} %bot_hbm.1, bf16[32,32,128]{2,1,0:T(8,128)(2,1)} %skip_hbm.1, bf16[32,32,128]{2,1,0:T(8,128)(2,1)} %cot_hbm.1), custom_call_target="tpu_custom_call" | custom-call | tf_op jit(solution)/shard_map/pallas_call | solution.py:130
  2.8 4.6 %collective-permute-start = (bf16[7,16,256]{2,1,0:T(8,128)(2,1)}, bf16[7,16,256]{2,1,0:T(8,128)(2,1)S(1)}, u32[]{:S(2)}, u32[]{:S(2)}) collective-permute-start(bf16[7,16,256]{2,1,0:T(8,128)(2,1)} %get-tuple-element.30), channel_id=1, source_target_pairs={{16,32},{32,16},{48,64},{64,48},{80,96},{96,80},{112,128},{128,112... | collective-permute-start | bytes 172040 | tf_op jit(solution)/shard_map/ppermute | solution.py:534
  7.6 1.0 rev.15.flip_ref
  8.6 1.0 %rev.13.own = bf16[2,78,2,256]{3,2,1,0:T(2,128)(2,1)S(1)} reverse(bf16[2,78,2,256]{3,2,1,0:T(2,128)(2,1)} %get-tuple-element.36), dimensions={0} | reverse | bytes 319488 | tf_op jit(solution)/shard_map/rev | solution.py:562
  9.6 0.7 shard_map.102
  10.3 0.7 collective-permute-start.2
  11.0 4.1 %collective-permute-start.3 = (bf16[78,2,256]{2,1,0:T(2,128)(2,1)S(1)}, bf16[78,2,256]{2,1,0:T(2,128)(2,1)S(1)}, u32[]{:S(2)}, u32[]{:S(2)}) collective-permute-start(bf16[78,2,256]{2,1,0:T(2,128)(2,1)S(1)} %get-tuple-element.38), channel_id=1, source_target_pairs={{0,1},{1,0},{2,3},{3,2},{4,5},{5,4},{6,7},{7,6},{8,9},{9,8},{10,11... | collective-permute-start | bytes 239624 | tf_op jit(solution)/shard_map/ppermute | solution.py:535
  15.3 1.4 %rev.14.uk_ref = bf16[4,4,256,128]{3,2,1,0:T(8,128)(2,1)S(1)} reverse(bf16[4,4,256,128]{3,2,1,0:T(8,128)(2,1)} %param.10), dimensions={1} | reverse | bytes 2097152 | tf_op jit(solution)/shard_map/rev | solution.py:561
  16.7 1.7 %collective-permute-done.3.col_in = bf16[78,2,256]{2,1,0:T(2,128)(2,1)S(1)} collective-permute-done((bf16[78,2,256]{2,1,0:T(2,128)(2,1)S(1)}, bf16[78,2,256]{2,1,0:T(2,128)(2,1)S(1)}, u32[]{:S(2)}, u32[]{:S(2)}) %collective-permute-start.3) | collective-permute-done | bytes 79904 | tf_op jit(solution)/shard_map/ppermute | solution.py:535
  18.4 7.6 %shard_map.103 = (bf16[2,18,16,512]{3,2,1,0:T(8,128)(2,1)S(1)}, bf16[18,16,768]{2,1,0:T(8,128)(2,1)S(1)}, bf16[5120,128]{1,0:T(8,128)(2,1)S(1)}, bf16[5120,128]{1,0:T(8,128)(2,1)S(1)}) custom-call(s32[5]{0:T(128)S(1)} %pad_add_fusion.pos_ref, bf16[5,16,16,256]{3,2,1,0:T(8,128)(2,1)S(1)} %rev.12.z_ref, ...), custom_call_target="tpu_custom_call" | custom-call | tf_op jit(solution)/shard_map/pallas_call | solution.py:457
  26.0 0.7 collective-permute-start.4
  26.7 1.7 %shard_map.104 = (bf16[32,32,128]{2,1,0:T(8,128)(2,1)}, bf16[16,16,256]{2,1,0:T(8,128)(2,1)}) custom-call(bf16[2,18,16,512]{3,2,1,0:T(8,128)(2,1)S(1)} %get-tuple-element.41.mix4c, bf16[18,16,768]{2,1,0:T(8,128)(2,1)S(1)} %get-tuple-element.42.pg3c, bf16[3,3,256,256]{3,2,1,0:T(8,128)(2,1)S(1)} %copy-done, bf16[3,3,128,128]{3,2,1,0:T(8,128)(2,1)S(1)} %copy-done.1), custom_call_target="tpu_custom_call" | custom-call | flops 1000000000 | bytes 3000000 | tf_op jit(solution)/shard_map/pallas_call | solution.py:439
  28.4 1.0 collective-permute-done.4
  29.4 0.3 add_convert_fusion
  29.7 28.7 %all_to_all.10 = bf16[32,160,128]{2,1,0:T(8,128)(2,1)S(1)} all-to-all(bf16[32,160,128]{2,1,0:T(8,128)(2,1)S(1)} %bitcast.10), channel_id=1, replica_groups={{0,1,128,129,32,33,160,161,64,65,192,193,96,97,224,225,2,3,130,131,34,3..., dimensions={0} | all-to-all | bytes 2621440 | tf_op jit(solution)/shard_map/all_to_all | solution.py:539
  58.6 4.3 %collective-permute-start.5 = (bf16[160,128]{1,0:T(8,128)(2,1)S(1)}, bf16[160,128]{1,0:T(8,128)(2,1)S(1)}, u32[]{:S(2)}, u32[]{:S(2)}) collective-permute-start(bf16[160,128]{1,0:T(8,128)(2,1)S(1)} %reduce_sum.12), channel_id=1, source_target_pairs={{0,4},{16,20},{2,6},{18,22},{4,0},{20,16},{6,2},{22,18},{8,12},{24... | collective-permute-start | bytes 122888 | tf_op jit(solution)/shard_map/ppermute | solution.py:549
  62.8 1.4 %collective-permute-done.5 = bf16[160,128]{1,0:T(8,128)(2,1)S(1)} collective-permute-done((bf16[160,128]{1,0:T(8,128)(2,1)S(1)}, bf16[160,128]{1,0:T(8,128)(2,1)S(1)}, u32[]{:S(2)}, u32[]{:S(2)}) %collective-permute-start.5) | collective-permute-done | bytes 40992 | tf_op jit(solution)/shard_map/ppermute | solution.py:549
  64.3 4.2 %collective-permute-start.6 = (bf16[160,128]{1,0:T(8,128)(2,1)S(1)}, bf16[160,128]{1,0:T(8,128)(2,1)S(1)}, u32[]{:S(2)}, u32[]{:S(2)}) collective-permute-start(bf16[160,128]{1,0:T(8,128)(2,1)S(1)} %add_convert_fusion.2), channel_id=1, source_target_pairs={{0,8},{16,24},{2,10},{18,26},{4,12},{20,28},{6,14},{22,30},{8,0},{... | collective-permute-start | bytes 122888 | tf_op jit(solution)/shard_map/ppermute | solution.py:549
  68.5 2.7 %collective-permute-done.6 = bf16[160,128]{1,0:T(8,128)(2,1)S(1)} collective-permute-done((bf16[160,128]{1,0:T(8,128)(2,1)S(1)}, bf16[160,128]{1,0:T(8,128)(2,1)S(1)}, u32[]{:S(2)}, u32[]{:S(2)}) %collective-permute-start.6) | collective-permute-done | bytes 40992 | tf_op jit(solution)/shard_map/ppermute | solution.py:549
  71.3 20.0 %all_to_all.11 = bf16[32,160,128]{2,1,0:T(8,128)(2,1)S(1)} all-to-all(bf16[32,160,128]{2,1,0:T(8,128)(2,1)S(1)} %broadcast_in_dim.2), channel_id=1, replica_groups={{0,1,128,129,32,33,160,161,64,65,192,193,96,97,224,225,2,3,130,131,34,3..., dimensions={0} | all-to-all | bytes 2621440 | tf_op jit(solution)/shard_map/all_to_all | solution.py:539
  91.4 5.5 %collective-permute-start.7 = (bf16[5120,128]{1,0:T(8,128)(2,1)S(1)}, bf16[5120,128]{1,0:T(8,128)(2,1)S(1)}, u32[]{:S(2)}, u32[]{:S(2)}) collective-permute-start(bf16[5120,128]{1,0:T(8,128)(2,1)S(1)} %bitcast.8), channel_id=1, source_target_pairs={{0,16},{16,0},{32,48},{48,32},{64,80},{80,64},{96,112},{112,96},{1... | collective-permute-start | bytes 3932168 | tf_op jit(solution)/shard_map/ppermute | solution.py:552
  96.8 2.1 %shard_map.105 = (f32[4096,128]{1,0:T(8,128)}, f32[2304,256]{1,0:T(8,128)}, f32[1152,128]{1,0:T(8,128)}) custom-call(s32[5]{0:T(128)S(1)} %pad_add_fusion.pos_ref, bf16[5120,128]{1,0:T(8,128)(2,1)S(1)} %bitcast.9), custom_call_target="tpu_custom_call" | custom-call | bytes 4000000 | tf_op jit(solution)/shard_map/pallas_call | solution.py:520
  98.9 0.6 collective-permute-done.7.half
  99.5 2.1 %shard_map.106 = (f32[4096,128]{1,0:T(8,128)}, f32[2304,256]{1,0:T(8,128)}, f32[1152,128]{1,0:T(8,128)}) custom-call(s32[5]{0:T(128)S(1)} %pad_add_fusion.pos_ref, bf16[5120,128]{1,0:T(8,128)(2,1)S(1)} %collective-permute-done.7.half, f32[4096,128]{1,0:T(8,128)} %get-tuple-element.49.refs_0_, ...), custom_call_target="tpu_custom_call", output_to_operand_aliasing={{0}: (2, {}), {1}: (3, {}), {2}: (4, {})} | custom-call | bytes 4000000 | tf_op jit(solution)/shard_map/pallas_call | solution.py:520
  (17 shorter events, 0.6 us)
Async XLA Ops:
  2.8 12.4 %copy-start.2 = (bf16[5,16,16,256]{3,2,1,0:T(8,128)(2,1)S(1)}, bf16[5,16,16,256]{3,2,1,0:T(8,128)(2,1)}, u32[]{:S(2)}) copy-start(bf16[5,16,16,256]{3,2,1,0:T(8,128)(2,1)} %get-tuple-element.33) | copy-start | bytes 1966084
  2.8 6.8 %collective-permute-start = (bf16[7,16,256]{2,1,0:T(8,128)(2,1)}, bf16[7,16,256]{2,1,0:T(8,128)(2,1)S(1)}, u32[]{:S(2)}, u32[]{:S(2)}) collective-permute-start(bf16[7,16,256]{2,1,0:T(8,128)(2,1)} %get-tuple-element.30), channel_id=1, source_target_pairs={{16,32},{32,16},{48,64},{64,48},{80,96},{96,80},{112,128},{128,112... | collective-permute-start | bytes 172040 | tf_op jit(solution)/shard_map/ppermute | solution.py:534
  7.5 2.1 %collective-permute-start.1 = (bf16[7,16,256]{2,1,0:T(8,128)(2,1)}, bf16[7,16,256]{2,1,0:T(8,128)(2,1)S(1)}, u32[]{:S(2)}, u32[]{:S(2)}) collective-permute-start(bf16[7,16,256]{2,1,0:T(8,128)(2,1)} %get-tuple-element.31), channel_id=1, source_target_pairs={{0,16},{16,0},{32,48},{48,32},{64,80},{80,64},{96,112},{112,96},{1... | collective-permute-start | bytes 172040 | tf_op jit(solution)/shard_map/ppermute | solution.py:535
  10.3 6.4 %collective-permute-start.2 = (bf16[78,2,256]{2,1,0:T(2,128)(2,1)}, bf16[78,2,256]{2,1,0:T(2,128)(2,1)S(1)}, u32[]{:S(2)}, u32[]{:S(2)}) collective-permute-start(bf16[78,2,256]{2,1,0:T(2,128)(2,1)} %get-tuple-element.37), channel_id=1, source_target_pairs={{1,2},{2,1},{3,4},{4,3},{5,6},{6,5},{7,8},{8,7},{9,10},{10,9},{11,... | collective-permute-start | bytes 239624 | tf_op jit(solution)/shard_map/ppermute | solution.py:534
  11.0 7.4 %collective-permute-start.3 = (bf16[78,2,256]{2,1,0:T(2,128)(2,1)S(1)}, bf16[78,2,256]{2,1,0:T(2,128)(2,1)S(1)}, u32[]{:S(2)}, u32[]{:S(2)}) collective-permute-start(bf16[78,2,256]{2,1,0:T(2,128)(2,1)S(1)} %get-tuple-element.38), channel_id=1, source_target_pairs={{0,1},{1,0},{2,3},{3,2},{4,5},{5,4},{6,7},{7,6},{8,9},{9,8},{10,11... | collective-permute-start | bytes 239624 | tf_op jit(solution)/shard_map/ppermute | solution.py:535
  15.3 3.1 %copy-start = (bf16[3,3,256,256]{3,2,1,0:T(8,128)(2,1)S(1)}, bf16[3,3,256,256]{3,2,1,0:T(8,128)(2,1)}, u32[]{:S(2)}) copy-start(bf16[3,3,256,256]{3,2,1,0:T(8,128)(2,1)} %bk_ref.3) | copy-start | bytes 3538948
  16.7 10.0 %copy-start.1 = (bf16[3,3,128,128]{3,2,1,0:T(8,128)(2,1)S(1)}, bf16[3,3,128,128]{3,2,1,0:T(8,128)(2,1)}, u32[]{:S(2)}) copy-start(bf16[3,3,128,128]{3,2,1,0:T(8,128)(2,1)} %lk_ref.1) | copy-start | bytes 884740
  26.0 3.3 %collective-permute-start.4 = (bf16[5120,128]{1,0:T(8,128)(2,1)S(1)}, bf16[5120,128]{1,0:T(8,128)(2,1)S(1)}, u32[]{:S(2)}, u32[]{:S(2)}) collective-permute-start(bf16[5120,128]{1,0:T(8,128)(2,1)S(1)} %get-tuple-element.40), channel_id=1, source_target_pairs={{0,16},{16,0},{32,48},{48,32},{64,80},{80,64},{96,112},{112,96},{1... | collective-permute-start | bytes 3932168 | tf_op jit(solution)/shard_map/ppermute | solution.py:543
  58.6 5.7 %collective-permute-start.5 = (bf16[160,128]{1,0:T(8,128)(2,1)S(1)}, bf16[160,128]{1,0:T(8,128)(2,1)S(1)}, u32[]{:S(2)}, u32[]{:S(2)}) collective-permute-start(bf16[160,128]{1,0:T(8,128)(2,1)S(1)} %reduce_sum.12), channel_id=1, source_target_pairs={{0,4},{16,20},{2,6},{18,22},{4,0},{20,16},{6,2},{22,18},{8,12},{24... | collective-permute-start | bytes 122888 | tf_op jit(solution)/shard_map/ppermute | solution.py:549
  64.3 6.9 %collective-permute-start.6 = (bf16[160,128]{1,0:T(8,128)(2,1)S(1)}, bf16[160,128]{1,0:T(8,128)(2,1)S(1)}, u32[]{:S(2)}, u32[]{:S(2)}) collective-permute-start(bf16[160,128]{1,0:T(8,128)(2,1)S(1)} %add_convert_fusion.2), channel_id=1, source_target_pairs={{0,8},{16,24},{2,10},{18,26},{4,12},{20,28},{6,14},{22,30},{8,0},{... | collective-permute-start | bytes 122888 | tf_op jit(solution)/shard_map/ppermute | solution.py:549
  91.4 8.1 %collective-permute-start.7 = (bf16[5120,128]{1,0:T(8,128)(2,1)S(1)}, bf16[5120,128]{1,0:T(8,128)(2,1)S(1)}, u32[]{:S(2)}, u32[]{:S(2)}) collective-permute-start(bf16[5120,128]{1,0:T(8,128)(2,1)S(1)} %bitcast.8), channel_id=1, source_target_pairs={{0,16},{16,0},{32,48},{48,32},{64,80},{80,64},{96,112},{112,96},{1... | collective-permute-start | bytes 3932168 | tf_op jit(solution)/shard_map/ppermute | solution.py:552
